TPU v7x, 32 devices: a whole 2x2x4 slice. The times are simulated.
32 devices in a mesh: seq: 8 (over z, core), wt: 4 (over y, x).
Axes of the slice: x: 2, y: 2, z: 4, core: 2. Of those that a mesh axis runs over, the one named last changes fastest.
Arguments:
- tokens: bfloat16 [4, 1024, 1024], P('wt', 'seq'), may hold values from -6 to 6
- cotangent: bfloat16 [4, 1024, 1024], P('wt', 'seq'), may hold values from -6 to 6
- doc_bounds: int32 [4, 2], P('wt'), may hold values from 1 to 1023, as said below
- attn_master: float32 [4, 1024, 1024], P(None, 'wt'), may hold values from -0.375 to 0.375
- mlp_master: float32 [3, 1024, 2816], P(None, 'wt'), may hold values from -0.15075567 to 0.15075567
- attn_momentum: float32 [4, 1024, 1024], P(None, 'wt'), may hold values from -512 to 512
- mlp_momentum: float32 [3, 1024, 2816], P(None, 'wt'), may hold values from -179.2 to 179.2
- gains: float32 [2, 1024], P(None, 'wt'), may hold values from 0.5 to 1.5
- gain_first: float32 [2, 1024], P(None, 'wt'), may hold values from -51.2 to 51.2
- gain_second: float32 [2, 1024], P(None, 'wt'), may hold values from 819.2 to 3276.8
- qkv_bias: float32 [3, 1024], P(None, 'wt'), may hold values from -2.5 to 2.5
- bias_first: float32 [3, 1024], P(None, 'wt'), may hold values from -51.2 to 51.2
- bias_second: float32 [3, 1024], P(None, 'wt'), may hold values from 819.2 to 3276.8
Outputs:
- output: bfloat16 [4, 1024, 1024], P('wt', 'seq')
- tokens_grad: float32 [4, 1024, 1024], P('wt', 'seq')
- attn_grad: float32 [4, 1024, 1024], P(None, 'wt')
- mlp_grad: float32 [3, 1024, 2816], P(None, 'wt')
- attn_momentum_new: float32 [4, 1024, 1024], P(None, 'wt')
- mlp_momentum_new: float32 [3, 1024, 2816], P(None, 'wt')
- attn_new: float32 [4, 1024, 1024], P(None, 'wt', 'seq')
- mlp_new: float32 [3, 1024, 2816], P(None, 'wt', 'seq')
- gain_grad: float32 [2, 1024], P(None, 'wt')
- gain_second_new: float32 [2, 1024], P(None, 'wt')
- gain_new: float32 [2, 1024], P(None, 'wt')
- bias_grad: float32 [3, 1024], P(None, 'wt')
- bias_second_new: float32 [3, 1024], P(None, 'wt')
- bias_new: float32 [3, 1024], P(None, 'wt')
Inputs may be any that keep to these rules, and one draw needn't show every extreme that they name: `doc_bounds`: row g holds the first tokens of documents 1 and 2 of sequence g: 0 < first < 128 and 896 < second < 1024.
All inputs are finite; a program needn't handle non-finite values.
Results may differ from a plain program's by a relative error of at most 0.018.
The roundings to bfloat16 on the way count: a program that leaves them out, or rounds other values in their place, can miss the bound.
Values may be sent and summed in bfloat16 or wider, within the bound.
No kernel may reach another device: no remote copies, remote signals or barrier semaphores. Data moves between devices by JAX's collectives and lax.ppermute only.
A program may use at most 320 MiB of HBM per device.

v0:
```python
import math

import jax
import jax.numpy as jnp
from jax import lax
from jax.sharding import PartitionSpec as P

HEADS = 16
HEAD_DIM = 64
NS_STEPS = 5
STEP = 10


norm_eps = 1e-06
rope_base = 1000000.0
coef_a = 3.4445
coef_b = -4.775
coef_c = 2.0315
momentum_decay = 0.95
matrix_rate = 0.5
decay_rate = 0.01
first_decay = 0.9
second_decay = 0.95
vector_rate = 0.25
adam_eps = 1e-08
ortho_eps = 1e-07
block_limit = 512
masked_score = -1e30


def for_sending(value):

    def short(part):
        return part.astype(jnp.bfloat16) if part.dtype == jnp.float32 else part

    return jax.tree.map(short, value)


def from_root(value, axis, root):
    mine = lax.axis_index(axis) == root
    return lax.psum(jnp.where(mine, value, jnp.zeros_like(value)), axis)


def doc_layout(bounds, length):
    places = jnp.arange(length, dtype=jnp.int32)
    first_bound = bounds[0]
    second_bound = bounds[1]
    doc_index = (places >= first_bound).astype(jnp.int32) + (places >= second_bound).astype(
        jnp.int32
    )
    doc_start = jnp.where(
        places < first_bound, 0, jnp.where(places < second_bound, first_bound, second_bound)
    )
    return (doc_index, (places - doc_start).astype(jnp.float32))


def rope_tables(position, head_dim):
    half_dim = head_dim // 2
    frequency = rope_base ** (-2.0 * jnp.arange(half_dim, dtype=jnp.float32) / head_dim)
    angles = frequency[:, None] * position[None, :]
    cosine_table = jnp.cos(angles)
    sine_table = jnp.sin(angles)
    return (
        jnp.concatenate([cosine_table, cosine_table], 0),
        jnp.concatenate([sine_table, sine_table], 0),
    )


def rotate_half(values):
    half_dim = values.shape[-2] // 2
    return jnp.concatenate([-values[..., half_dim:, :], values[..., :half_dim, :]], axis=-2)


def apply_rope(values, cosine_table, sine_table):
    return values * cosine_table + rotate_half(values) * sine_table


def undo_rope(gradient, cosine_table, sine_table):
    return gradient * cosine_table - rotate_half(gradient * sine_table)


def block_scores(query_block, key_rot, doc_index, first_row, block_size, score_scale):
    length = key_rot.shape[-1]
    query_places = first_row + jnp.arange(block_size, dtype=jnp.int32)
    key_places = jnp.arange(length, dtype=jnp.int32)
    query_docs = lax.dynamic_slice_in_dim(doc_index, first_row, block_size)
    allowed = (query_docs[:, None] == doc_index[None, :]) & (
        key_places[None, :] <= query_places[:, None]
    )
    scores = (
        jnp.einsum("hdq,hdk->hqk", query_block, key_rot, preferred_element_type=jnp.float32)
        * score_scale
    )
    return jnp.where(allowed[None], scores, masked_score)


def attend_forward(query_rot, key_rot, value_heads, doc_index):
    head_count, head_dim, length = query_rot.shape
    block_size = min(block_limit, length)
    score_scale = head_dim ** (-0.5)

    def one_block(block_index):
        first_row = block_index * block_size
        query_block = lax.dynamic_slice_in_dim(query_rot, first_row, block_size, 2)
        scores = block_scores(query_block, key_rot, doc_index, first_row, block_size, score_scale)
        row_peak = jnp.max(scores, axis=-1, keepdims=True)
        exponent = jnp.exp(scores - row_peak)
        row_total = jnp.sum(exponent, axis=-1, keepdims=True)
        weights_low = (exponent / row_total).astype(jnp.bfloat16)
        attended = jnp.einsum(
            "hqk,hdk->hdq", weights_low, value_heads, preferred_element_type=jnp.float32
        )
        return (attended.astype(jnp.bfloat16), (row_peak + jnp.log(row_total))[..., 0])

    attended, log_total = lax.map(one_block, jnp.arange(length // block_size, dtype=jnp.int32))
    attended = jnp.moveaxis(attended, 0, 2).reshape(head_count, head_dim, length)
    log_total = jnp.moveaxis(log_total, 0, 1).reshape(head_count, length)
    return (attended, log_total)


def attend_backward(query_rot, key_rot, value_heads, doc_index, log_total, d_attended):
    head_count, head_dim, length = query_rot.shape
    block_size = min(block_limit, length)
    score_scale = head_dim ** (-0.5)

    def one_step(carry, block_index):
        d_keys, d_values = carry
        first_row = block_index * block_size
        query_block = lax.dynamic_slice_in_dim(query_rot, first_row, block_size, 2)
        grad_block = lax.dynamic_slice_in_dim(d_attended, first_row, block_size, 2)
        total_block = lax.dynamic_slice_in_dim(log_total, first_row, block_size, 1)
        scores = block_scores(query_block, key_rot, doc_index, first_row, block_size, score_scale)
        weights = jnp.exp(scores - total_block[..., None])
        d_values = d_values + jnp.einsum(
            "hqk,hdq->hdk",
            weights.astype(jnp.bfloat16),
            grad_block,
            preferred_element_type=jnp.float32,
        )
        d_weights = jnp.einsum(
            "hdq,hdk->hqk", grad_block, value_heads, preferred_element_type=jnp.float32
        )
        inner_sum = jnp.sum(weights * d_weights, axis=-1, keepdims=True)
        d_scores = (weights * (d_weights - inner_sum)).astype(jnp.bfloat16)
        d_query = (
            jnp.einsum("hqk,hdk->hdq", d_scores, key_rot, preferred_element_type=jnp.float32)
            * score_scale
        )
        d_keys = (
            d_keys
            + jnp.einsum("hqk,hdq->hdk", d_scores, query_block, preferred_element_type=jnp.float32)
            * score_scale
        )
        return ((d_keys, d_values), d_query)

    zero_state = jnp.zeros((head_count, head_dim, length), jnp.float32)
    carried, d_query = lax.scan(
        one_step, (zero_state, zero_state), jnp.arange(length // block_size, dtype=jnp.int32)
    )
    d_query = jnp.moveaxis(d_query, 0, 2).reshape(head_count, head_dim, length)
    return (d_query, carried[0], carried[1])


def norm_backward(d_normed, values, inverse, gain_row):
    scaled = d_normed * gain_row
    gain_part = jnp.sum(d_normed * values * inverse, axis=0)
    d_values = inverse * scaled - values * inverse**3 * jnp.mean(
        scaled * values, axis=-1, keepdims=True
    )
    return (d_values, gain_part)


def orthogonalize(matrix):
    frobenius = jnp.sqrt(jnp.sum(matrix * matrix))
    iterate = (matrix / (frobenius + ortho_eps)).astype(jnp.bfloat16)
    for repeat_index in range(NS_STEPS):
        gram_low = jnp.einsum(
            "ik,jk->ij", iterate, iterate, preferred_element_type=jnp.float32
        ).astype(jnp.bfloat16)
        poly_low = (
            coef_b * gram_low.astype(jnp.float32)
            + coef_c * jnp.dot(gram_low, gram_low, preferred_element_type=jnp.float32)
        ).astype(jnp.bfloat16)
        iterate = (
            coef_a * iterate.astype(jnp.float32)
            + jnp.dot(poly_low, iterate, preferred_element_type=jnp.float32)
        ).astype(jnp.bfloat16)
    return iterate


def owner_order(partial_value, wt_count, seq_count):
    lead_count = partial_value.shape[0]
    total_rows = partial_value.shape[1]
    tail_shape = partial_value.shape[2:]
    blocked = partial_value.reshape(
        (lead_count, wt_count, seq_count, total_rows // (wt_count * seq_count)) + tail_shape
    )
    return jnp.swapaxes(blocked, 1, 2).reshape(partial_value.shape)


def adam_update(parameter, gradient, first_state, second_state):
    first_new = first_decay * first_state + (1.0 - first_decay) * gradient
    second_new = second_decay * second_state + (1.0 - second_decay) * gradient * gradient
    first_hat = first_new / (1.0 - first_decay**STEP)
    second_hat = second_new / (1.0 - second_decay**STEP)
    return (parameter - vector_rate * first_hat / (jnp.sqrt(second_hat) + adam_eps), second_new)


def per_device(
    tokens,
    cotangent,
    doc_bounds,
    attn_master,
    mlp_master,
    attn_momentum,
    mlp_momentum,
    gains,
    gain_first,
    gain_second,
    qkv_bias,
    bias_first,
    bias_second,
):
    seq_count = lax.axis_size("seq")
    wt_count = lax.axis_size("wt")
    seq_index = lax.axis_index("seq")
    wt_index = lax.axis_index("wt")
    row_count = tokens.shape[1]
    model_width = tokens.shape[2]
    token_values = tokens[0].astype(jnp.float32)
    attn_w, mlp_w, gain_w, bias_w = (
        lax.all_gather(attn_master.astype(jnp.bfloat16), "wt", axis=1, tiled=True),
        lax.all_gather(mlp_master.astype(jnp.bfloat16), "wt", axis=1, tiled=True),
        lax.all_gather(gains.astype(jnp.bfloat16), "wt", axis=1, tiled=True),
        lax.all_gather(qkv_bias.astype(jnp.bfloat16), "wt", axis=1, tiled=True),
    )
    rms_attn = jnp.sqrt(jnp.mean(jnp.square(attn_w.astype(jnp.float32)), axis=(1, 2)))
    rms_mlp = jnp.sqrt(jnp.mean(jnp.square(mlp_w.astype(jnp.float32)), axis=(1, 2)))
    gain_attn = gain_w[0].astype(jnp.float32)
    gain_mlp = gain_w[1].astype(jnp.float32)
    inverse_one = lax.rsqrt(
        jnp.mean(token_values * token_values, axis=-1, keepdims=True) + norm_eps
    )
    normed_one = (token_values * inverse_one * gain_attn).astype(jnp.bfloat16)
    projected = (
        jnp.einsum("jdc,td->jct", attn_w[:3], normed_one, preferred_element_type=jnp.float32)
        + bias_w.astype(jnp.float32)[:, :, None]
    )
    projected = projected.astype(jnp.bfloat16).reshape(3, HEADS, HEAD_DIM, row_count)
    heads_qkv = lax.all_to_all(projected, "seq", split_axis=1, concat_axis=3, tiled=True)
    length = heads_qkv.shape[3]
    doc_index, position = doc_layout(doc_bounds[0], length)
    cosine_table, sine_table = rope_tables(position, HEAD_DIM)
    query_rot = apply_rope(heads_qkv[0].astype(jnp.float32), cosine_table, sine_table).astype(
        jnp.bfloat16
    )
    key_rot = apply_rope(heads_qkv[1].astype(jnp.float32), cosine_table, sine_table).astype(
        jnp.bfloat16
    )
    value_heads = heads_qkv[2]
    attended, log_total = attend_forward(query_rot, key_rot, value_heads, doc_index)
    attn_tokens = lax.all_to_all(attended, "seq", split_axis=2, concat_axis=0, tiled=True)
    attn_flat = attn_tokens.reshape(model_width, row_count)
    resid = token_values + jnp.einsum(
        "ct,cd->td", attn_flat, attn_w[3], preferred_element_type=jnp.float32
    )
    inverse_two = lax.rsqrt(jnp.mean(resid * resid, axis=-1, keepdims=True) + norm_eps)
    normed_two = (resid * inverse_two * gain_mlp).astype(jnp.bfloat16)
    gate_act = jnp.dot(normed_two, mlp_w[0], preferred_element_type=jnp.float32)
    up_act = jnp.dot(normed_two, mlp_w[1], preferred_element_type=jnp.float32)
    sigmoid_gate = jax.nn.sigmoid(gate_act)
    silu_act = gate_act * sigmoid_gate
    hidden = (silu_act * up_act).astype(jnp.bfloat16)
    layer_out = resid + jnp.einsum(
        "tf,df->td", hidden, mlp_w[2], preferred_element_type=jnp.float32
    )
    attn_back, mlp_back = (
        lax.all_gather(attn_master.astype(jnp.bfloat16), "wt", axis=1, tiled=True),
        lax.all_gather(mlp_master.astype(jnp.bfloat16), "wt", axis=1, tiled=True),
    )
    d_out_low = cotangent[0]
    d_hidden = jnp.dot(d_out_low, mlp_back[2], preferred_element_type=jnp.float32)
    grad_down = jnp.einsum("td,tf->df", d_out_low, hidden, preferred_element_type=jnp.float32)
    d_gate = (d_hidden * up_act * (sigmoid_gate * (1.0 + gate_act * (1.0 - sigmoid_gate)))).astype(
        jnp.bfloat16
    )
    d_up = (d_hidden * silu_act).astype(jnp.bfloat16)
    grad_gate = jnp.einsum("td,tf->df", normed_two, d_gate, preferred_element_type=jnp.float32)
    grad_up = jnp.einsum("td,tf->df", normed_two, d_up, preferred_element_type=jnp.float32)
    d_normed_two = jnp.einsum(
        "tf,df->td", d_gate, mlp_back[0], preferred_element_type=jnp.float32
    ) + jnp.einsum("tf,df->td", d_up, mlp_back[1], preferred_element_type=jnp.float32)
    d_resid_mlp, gain_part_two = norm_backward(d_normed_two, resid, inverse_two, gain_mlp)
    d_resid = d_out_low.astype(jnp.float32) + d_resid_mlp
    d_resid_low = d_resid.astype(jnp.bfloat16)
    grad_outproj = jnp.einsum(
        "ct,td->cd", attn_flat, d_resid_low, preferred_element_type=jnp.float32
    )
    d_attn = jnp.einsum("td,cd->ct", d_resid_low, attn_back[3], preferred_element_type=jnp.float32)
    d_attn = d_attn.astype(jnp.bfloat16).reshape(HEADS, HEAD_DIM, row_count)
    d_attended = lax.all_to_all(d_attn, "seq", split_axis=0, concat_axis=2, tiled=True)
    d_query, d_keys, d_values = attend_backward(
        query_rot, key_rot, value_heads, doc_index, log_total, d_attended
    )
    d_qkv = jnp.stack(
        [
            undo_rope(d_query, cosine_table, sine_table),
            undo_rope(d_keys, cosine_table, sine_table),
            d_values,
        ]
    ).astype(jnp.bfloat16)
    d_projected = lax.all_to_all(d_qkv, "seq", split_axis=3, concat_axis=1, tiled=True)
    d_projected = d_projected.reshape(3, model_width, row_count)
    grad_qkv = jnp.einsum(
        "td,jct->jdc", normed_one, d_projected, preferred_element_type=jnp.float32
    )
    bias_part = jnp.sum(d_projected.astype(jnp.float32), axis=2)
    d_normed_one = jnp.einsum(
        "jdc,jct->td", attn_back[:3], d_projected, preferred_element_type=jnp.float32
    )
    d_input_norm, gain_part_one = norm_backward(d_normed_one, token_values, inverse_one, gain_attn)
    tokens_grad = d_resid + d_input_norm
    attn_part = jnp.concatenate([grad_qkv, grad_outproj[None]], axis=0)
    mlp_part = jnp.stack([grad_gate, grad_up, grad_down])
    gain_part = jnp.stack([gain_part_one, gain_part_two])
    arranged = (
        owner_order(attn_part, wt_count, seq_count),
        owner_order(mlp_part, wt_count, seq_count),
        owner_order(gain_part, wt_count, seq_count),
        owner_order(bias_part, wt_count, seq_count),
    )
    shares = (
        lax.psum_scatter(arranged[0], ("seq", "wt"), scatter_dimension=1, tiled=True),
        lax.psum_scatter(arranged[1], ("seq", "wt"), scatter_dimension=1, tiled=True),
        lax.psum_scatter(arranged[2], ("seq", "wt"), scatter_dimension=1, tiled=True),
        lax.psum_scatter(arranged[3], ("seq", "wt"), scatter_dimension=1, tiled=True),
    )
    summed = (
        lax.all_gather(shares[0].astype(jnp.bfloat16), "seq", axis=1, tiled=True).astype(
            jnp.float32
        ),
        lax.all_gather(shares[1].astype(jnp.bfloat16), "seq", axis=1, tiled=True).astype(
            jnp.float32
        ),
        lax.all_gather(shares[2].astype(jnp.bfloat16), "seq", axis=1, tiled=True).astype(
            jnp.float32
        ),
        lax.all_gather(shares[3].astype(jnp.bfloat16), "seq", axis=1, tiled=True).astype(
            jnp.float32
        ),
    )
    attn_grad, mlp_grad, gain_grad, bias_grad = summed
    attn_mom = momentum_decay * attn_momentum + attn_grad
    mlp_mom = momentum_decay * mlp_momentum + mlp_grad
    attn_pick = jnp.minimum(seq_index, 3)
    mlp_pick = jnp.clip(seq_index - 4, 0, 2)
    full_attn, full_mlp = (
        lax.all_gather(
            for_sending(lax.dynamic_index_in_dim(attn_mom, attn_pick, 0, keepdims=False)),
            "wt",
            axis=0,
            tiled=True,
        ),
        lax.all_gather(
            for_sending(lax.dynamic_index_in_dim(mlp_mom, mlp_pick, 0, keepdims=False)),
            "wt",
            axis=0,
            tiled=True,
        ),
    )

    def empty_attn(matrix):
        return jnp.zeros(matrix.shape, jnp.bfloat16)

    ortho_attn = lax.cond(seq_index < 4, orthogonalize, empty_attn, full_attn)
    ortho_mlp = lax.cond((seq_index >= 4) & (seq_index < 7), orthogonalize, empty_attn, full_mlp)
    shard_rows = attn_master.shape[1]
    attn_rows = lax.dynamic_slice_in_dim(ortho_attn, wt_index * shard_rows, shard_rows, 0)
    mlp_rows = lax.dynamic_slice_in_dim(ortho_mlp, wt_index * shard_rows, shard_rows, 0)
    attn_updates = []
    for owner in range(4):
        attn_updates.append(from_root(attn_rows, "seq", owner))
    mlp_updates = []
    for owner in range(3):
        mlp_updates.append(from_root(mlp_rows, "seq", 4 + owner))
    attn_cols = attn_master.shape[2] // seq_count
    mlp_cols = mlp_master.shape[2] // seq_count
    attn_steps = lax.dynamic_slice_in_dim(
        jnp.stack(attn_updates).astype(jnp.float32), seq_index * attn_cols, attn_cols, 2
    )
    mlp_steps = lax.dynamic_slice_in_dim(
        jnp.stack(mlp_updates).astype(jnp.float32), seq_index * mlp_cols, mlp_cols, 2
    )
    attn_own = lax.dynamic_slice_in_dim(attn_master, seq_index * attn_cols, attn_cols, 2)
    mlp_own = lax.dynamic_slice_in_dim(mlp_master, seq_index * mlp_cols, mlp_cols, 2)
    attn_new = (
        attn_own * (1.0 - matrix_rate * decay_rate)
        - (matrix_rate * math.sqrt(attn_w.shape[2]) * rms_attn)[:, None, None] * attn_steps
    )
    mlp_new = (
        mlp_own * (1.0 - matrix_rate * decay_rate)
        - (matrix_rate * math.sqrt(mlp_w.shape[2]) * rms_mlp)[:, None, None] * mlp_steps
    )
    gain_new, gain_second_new = adam_update(gains, gain_grad, gain_first, gain_second)
    bias_new, bias_second_new = adam_update(qkv_bias, bias_grad, bias_first, bias_second)
    return (
        layer_out.astype(jnp.bfloat16)[None],
        tokens_grad[None],
        attn_grad,
        mlp_grad,
        attn_mom,
        mlp_mom,
        attn_new,
        mlp_new,
        gain_grad,
        gain_second_new,
        gain_new,
        bias_grad,
        bias_second_new,
        bias_new,
    )


def solution(mesh):
    return jax.shard_map(
        per_device,
        mesh=mesh,
        in_specs=(
            P("wt", "seq", None),
            P("wt", "seq", None),
            P("wt", None),
            P(None, "wt", None),
            P(None, "wt", None),
            P(None, "wt", None),
            P(None, "wt", None),
            P(None, "wt"),
            P(None, "wt"),
            P(None, "wt"),
            P(None, "wt"),
            P(None, "wt"),
            P(None, "wt"),
        ),
        out_specs=(
            P("wt", "seq", None),
            P("wt", "seq", None),
            P(None, "wt", None),
            P(None, "wt", None),
            P(None, "wt", None),
            P(None, "wt", None),
            P(None, "wt", "seq"),
            P(None, "wt", "seq"),
            P(None, "wt"),
            P(None, "wt"),
            P(None, "wt"),
            P(None, "wt"),
            P(None, "wt"),
            P(None, "wt"),
        ),
        check_vma=False,
    )
```

profile of v0, /device:TPU:1, one launch (start us, length us, event | category | flops | bytes accessed | tf_op | source)
XLA Modules:
  0.0 2065.2 jit_solution(10845539299273111625)
XLA Ops:
  7.2 3.8 convert_element_type.336
  11.1 5.9 convert_element_type.349
  17.8 6.9 all_gather.40
  24.7 7.1 all_gather.38
  32.4 68.6 %all-gather.11.cloned.1.call-done = bf16[4,1024,1024]{2,1,0:T(8,128)(2,1)} async-done(((bf16[4,256,1024]{2,1,0:T(8,128)(2,1)}), bf16[4,1024,1024]{2,1,0:T(8,128)(2,1)}) %all-gather.11.cloned.1.call-update) | async-done | bytes 8388624 | tf_op jit(solution)/shard_map/all_gather | solution.py:232
  101.0 3.8 fusion.84
  106.2 5.3 all-to-all-start
  114.0 17.6 all-to-all-done
  132.9 12.8 while.27
  147.4 12.4 all_to_all.63
  160.4 2.1 multiply_reduce_fusion.7
  162.7 102.9 %all-gather.13.cloned.1.call-done = bf16[3,1024,2816]{2,1,0:T(8,128)(2,1)} async-done(((bf16[3,256,2816]{2,1,0:T(8,128)(2,1)}), bf16[3,1024,2816]{2,1,0:T(8,128)(2,1)}) %all-gather.13.cloned.1.call-update) | async-done | bytes 17301520 | tf_op jit(solution)/shard_map/all_gather | solution.py:233
  265.6 3.7 fusion.76
  269.4 4.0 fusion.74
  273.4 5.2 multiply_convert_fusion.1
  280.6 2.6 multiply_reduce_fusion.5
  283.4 2.6 fusion.95
  286.9 5.6 all-to-all-start.2
  292.5 9.0 all-to-all-done.2
  301.5 18.7 while.28
  329.1 2.2 copy.162
  333.2 4.5 all-to-all-start.3
  338.2 2.7 convolution_bitcast_fusion
  340.9 16.9 all-to-all-done.3
  363.1 2.4 maximum_bitcast_fusion.1
  365.4 6.1 copy.168
  372.7 5.9 fusion.157
  378.6 5.9 fusion.156
  384.5 5.9 fusion.133
  390.4 12.6 maximum_bitcast_fusion
  403.1 11.5 copy.169
  414.6 312.7 %reduce-scatter.9.cloned.1.call-done = f32[4,32,1024]{2,1,0:T(8,128)} async-done(((f32[4,1024,1024]{2,1,0:T(8,128)}), f32[4,32,1024]{2,1,0:T(8,128)}) %reduce-scatter.9.cloned.1.call-update) | async-done | bytes 524304 | tf_op jit(solution)/shard_map/reduce_scatter | solution.py:333
  729.2 730.0 %reduce-scatter.11.cloned.1.call-done = f32[3,32,2816]{2,1,0:T(8,128)} async-done(((f32[3,1024,2816]{2,1,0:T(8,128)}), f32[3,32,2816]{2,1,0:T(8,128)}) %reduce-scatter.11.cloned.1.call-update) | async-done | bytes 1081360 | tf_op jit(solution)/shard_map/reduce_scatter | solution.py:334
  1459.2 2.1 convert_element_type.363
  1461.4 30.9 %all-gather.15.cloned.1.call-done = bf16[4,256,1024]{2,1,0:T(8,128)(2,1)} async-done(((bf16[4,32,1024]{2,1,0:T(8,128)(2,1)}), bf16[4,256,1024]{2,1,0:T(8,128)(2,1)}) %all-gather.15.cloned.1.call-update) | async-done | bytes 2097168 | tf_op jit(solution)/shard_map/all_gather | solution.py:339
  1492.3 6.4 multiply_add_fusion.1
  1501.8 40.5 %all-gather.17.cloned.1.call-done = bf16[3,256,2816]{2,1,0:T(8,128)(2,1)} async-done(((bf16[3,32,2816]{2,1,0:T(8,128)(2,1)}), bf16[3,256,2816]{2,1,0:T(8,128)(2,1)}) %all-gather.17.cloned.1.call-update) | async-done | bytes 4325392 | tf_op jit(solution)/shard_map/all_gather | solution.py:342
  1542.3 12.5 multiply_add_fusion
  1554.8 3.0 dynamic-slice_convert_fusion
  1561.1 5.8 multiply_reduce_fusion.4
  1569.5 6.3 fusion.113
  1579.0 80.2 %conditional.2 = (bf16[1024,1024]{1,0:T(8,128)(2,1)S(1)}) conditional(s32[]{:T(128)} %convert_element_type.366, () %tuple.30, bf16[1024,1024]{1,0:T(8,128)(2,1)} %bitcast.347), branch_computations={%region_14.15_spmd, %region_15.17_spmd} | conditional | flops 32266780672 | bytes 88080520 | solution.py:375
  1579.2 3.3 multiply_reduce_fusion
  1583.2 6.1 fusion.37
  1589.3 9.2 add_convert_fusion.8
  1598.6 6.1 fusion.148
  1604.7 9.0 add_convert_fusion.6
  1613.7 6.6 fusion.149
  1620.3 8.9 add_convert_fusion.4
  1629.2 6.1 fusion.150
  1635.3 8.9 add_convert_fusion.2
  1644.2 6.0 fusion.151
  1650.2 8.8 add_convert_fusion
  1660.8 9.1 conditional.3
  1660.8 3.3 broadcast.241.clone
  1670.0 4.0 select_bitcast_fusion.2
  1674.0 7.8 multiply_reduce_fusion.3
  1682.0 5.4 fusion.96
  1688.5 88.7 %reduce-scatter.13.cloned.1.call-done = f32[32,2]{1,0:T(8,128)} async-done(((f32[1024,2]{1,0:T(8,128)}), f32[32,2]{1,0:T(8,128)}) %reduce-scatter.13.cloned.1.call-update) | async-done | bytes 272
  1778.0 40.9 %all-gather.2 = bf16[8,32,2]{1,2,0:T(2,128)(2,1)S(1)} all-gather(bf16[1,32,2]{1,2,0:T(2,128)(2,1)S(1)} %bitcast.371), channel_id=1, replica_groups=mesh['seq'=8,'wt'=4] {'seq'}, dimensions={0}, use_global_device_ids=true | all-gather | bytes 1152 | tf_op jit(solution)/shard_map/all_gather | solution.py:345
  1819.7 90.0 %reduce-scatter.15.cloned.1.call-done = f32[32,3]{1,0:T(8,128)} async-done(((f32[1024,3]{1,0:T(8,128)}), f32[32,3]{1,0:T(8,128)}) %reduce-scatter.15.cloned.1.call-update) | async-done | bytes 400
  1910.5 13.5 all-gather.3
  1924.7 129.1 %all-reduce.3.cloned.1.call-done = (bf16[1,256,1024]{2,1,0:T(8,128)(2,1)}, bf16[1,256,1024]{2,1,0:T(8,128)(2,1)}, bf16[1,256,1024]{2,1,0:T(8,128)(2,1)}, bf16[1,...) async-done(((bf16[1,256,1024]{2,1,0:T(8,128)(2,1)}, bf16[1,256,1024]{2,1,0:T(8,128)(2,1)}, ...) | async-done | bytes 6422544 | tf_op jit(solution)/shard_map/psum | solution.py:41
  2053.8 2.4 multiply_subtract_fusion
  (275 shorter events, 80.1 us)
Async XLA Ops:
  7.2 93.8 %all-gather.11.cloned.1.call-start = ((), (), s32[]{:S(2)}) async-start(), calls=%async_computation.8 | async-start | bytes 10485760 | tf_op jit(solution)/shard_map/all_gather | solution.py:232
  11.1 254.5 %all-gather.13.cloned.1.call-start = ((), (), s32[]{:S(2)}) async-start(), calls=%async_computation.9 | async-start | bytes 21626880 | tf_op jit(solution)/shard_map/all_gather | solution.py:233
  17.1 14.7 copy-start.7
  32.4 1537.1 %copy-start.47 = (f32[128]{0:T(128)}, f32[128]{0:T(128)S(1)}, u32[]{:S(2)}) copy-start(f32[128]{0:T(128)S(1)} %get-tuple-element.257) | copy-start | bytes 1540
  32.4 1537.1 %copy-start.33 = (f32[1,1024]{1,0:T(1,128)}, f32[1,1024]{1,0:T(1,128)S(1)}, u32[]{:S(2)}) copy-start(f32[1,1024]{1,0:T(1,128)S(1)} %get-tuple-element.255) | copy-start | bytes 12292
  104.8 6.6 copy-start.44
  106.2 25.4 %all-to-all-start = ((bf16[3,16,64,128]{3,2,0,1:T(8,128)(2,1)}), bf16[3,16,64,128]{3,2,0,1:T(8,128)(2,1)S(1)}, u32[]{:S(2)}, u32[]{:S(2)}) async-start(bf16[3,16,64,128]{3,2,0,1:T(8,128)(2,1)} %copy.152), calls=%async_computation | async-start | bytes 1572864 | tf_op jit(solution)/shard_map/all_to_all | solution.py:250
  134.8 2.3 copy-start.31
  141.2 2.3 copy-start.31
  162.6 120.6 %copy-start.4 = (f32[128,1024]{1,0:T(8,128)}, f32[128,1024]{1,0:T(8,128)S(1)}, u32[]{:S(2)}) copy-start(f32[128,1024]{1,0:T(8,128)S(1)} %get-tuple-element.263) | copy-start | bytes 1572868
  162.7 110.7 %copy-start.10 = (bf16[128,1024]{1,0:T(8,128)(2,1)}, bf16[128,1024]{1,0:T(8,128)(2,1)S(1)}, u32[]{:S(2)}) copy-start(bf16[128,1024]{1,0:T(8,128)(2,1)S(1)} %multiply_convert_fusion.4) | copy-start | bytes 786436
  265.6 13.0 slice-start
  265.6 13.0 slice-start.1
  269.3 4.1 copy-start.16
  269.3 9.3 slice-start.2
  273.4 5.2 slice-start.3
  273.4 5.2 slice-start.4
  278.6 2.0 copy-start.22
  283.4 54.8 %copy-start.2 = (f32[128,1024]{1,0:T(8,128)}, f32[128,1024]{1,0:T(8,128)S(1)}, u32[]{:S(2)}) copy-start(f32[128,1024]{1,0:T(8,128)S(1)} %subtract_add_fusion) | copy-start | bytes 1572868
  286.9 14.6 all-to-all-start.2
  320.2 3.9 copy-start.15
  333.2 24.6 %all-to-all-start.3 = ((bf16[8,2,24576]{2,1,0:T(2,128)(2,1)}), bf16[8,2,24576]{2,1,0:T(2,128)(2,1)S(1)}, u32[]{:S(2)}, u32[]{:S(2)}) async-start(bf16[8,2,24576]{2,1,0:T(2,128)(2,1)} %reshape.397), calls=%async_computation.3 | async-start | bytes 1572864 | tf_op jit(solution)/shard_map/all_to_all | solution.py:312
  337.7 389.6 %reduce-scatter.9.cloned.1.call-start = ((), (), s32[]{:S(2)}) async-start(), calls=%async_computation.10 | async-start | bytes 17301504 | tf_op jit(solution)/shard_map/reduce_scatter | solution.py:333
  360.9 2.2 copy-start
  371.5 1087.7 %reduce-scatter.11.cloned.1.call-start = ((), (), s32[]{:S(2)}) async-start(), calls=%async_computation.12 | async-start | bytes 35684352 | tf_op jit(solution)/shard_map/reduce_scatter | solution.py:334
  372.7 5.9 copy-start.21
  378.6 5.9 copy-start.17
  378.6 5.9 copy-start.18
  414.6 1077.7 %all-gather.15.cloned.1.call-start = ((), (), s32[]{:S(2)}) async-start(), calls=%async_computation.11 | async-start | bytes 2359296 | tf_op jit(solution)/shard_map/all_gather | solution.py:339
  729.2 813.2 %all-gather.17.cloned.1.call-start = ((), (), s32[]{:S(2)}) async-start(), calls=%async_computation.13 | async-start | bytes 4866048 | tf_op jit(solution)/shard_map/all_gather | solution.py:342
  1461.3 117.6 %all-gather.19.cloned.1.call-start = ((), (), s32[]{:S(2)}) async-start(), calls=%async_computation.14 | async-start | bytes 2621440 | tf_op jit(solution)/shard_map/all_gather | solution.py:358
  1501.6 159.2 %all-gather.21.cloned.1.call-start = ((), (), s32[]{:S(2)}) async-start(), calls=%async_computation.15 | async-start | bytes 7208960 | tf_op jit(solution)/shard_map/all_gather | solution.py:364
  1557.8 219.4 %reduce-scatter.13.cloned.1.call-start = ((), (), s32[]{:S(2)}) async-start(), calls=%async_computation.16 | async-start | bytes 540672
  1561.1 6.4 copy-start.41
  1561.1 8.5 copy-start.8
  1577.1 332.6 %reduce-scatter.15.cloned.1.call-start = ((), (), s32[]{:S(2)}) async-start(), calls=%async_computation.17 | async-start | bytes 540672
  1578.9 474.9 %all-reduce.3.cloned.1.call-start = ((), (), s32[]{:S(2)}) async-start(), calls=%async_computation.18 | async-start | bytes 12845056 | tf_op jit(solution)/shard_map/psum | solution.py:41
  1583.2 6.1 copy-start.12
  1598.6 6.1 copy-start.52
  1613.7 6.6 copy-start.53
  1629.2 6.1 copy-start.54
  1674.0 7.8 copy-start.5
  1674.0 7.8 copy-start.19
  1681.8 5.6 copy-start.51
  1681.8 5.6 copy-start.3
  1681.8 5.6 copy-start.9
  1681.8 5.6 copy-start.26
  1681.8 5.6 copy-start.34
  1681.9 5.6 copy-start.48
  1681.9 5.6 copy-start.50
  1681.9 137.2 %copy-start.40 = (f32[2,256]{1,0:T(2,128)S(1)}, f32[2,256]{1,0:T(2,128)}, u32[]{:S(2)}) copy-start(f32[2,256]{1,0:T(2,128)} %param.28) | copy-start | bytes 6148
  1681.9 137.2 %copy-start.45 = (f32[2,256]{1,0:T(2,128)S(1)}, f32[2,256]{1,0:T(2,128)}, u32[]{:S(2)}) copy-start(f32[2,256]{1,0:T(2,128)} %param.29) | copy-start | bytes 6148
  1681.9 137.2 %copy-start.46 = (f32[2,256]{1,0:T(2,128)S(1)}, f32[2,256]{1,0:T(2,128)}, u32[]{:S(2)}) copy-start(f32[2,256]{1,0:T(2,128)} %param.30) | copy-start | bytes 6148
  1681.9 242.1 %copy-start.36 = (f32[3,256]{1,0:T(4,128)S(1)}, f32[3,256]{1,0:T(4,128)}, u32[]{:S(2)}) copy-start(f32[3,256]{1,0:T(4,128)} %param.31) | copy-start | bytes 9220
  1681.9 242.1 %copy-start.42 = (f32[3,256]{1,0:T(4,128)S(1)}, f32[3,256]{1,0:T(4,128)}, u32[]{:S(2)}) copy-start(f32[3,256]{1,0:T(4,128)} %param.32) | copy-start | bytes 9220
  1681.9 242.1 %copy-start.43 = (f32[3,256]{1,0:T(4,128)S(1)}, f32[3,256]{1,0:T(4,128)}, u32[]{:S(2)}) copy-start(f32[3,256]{1,0:T(4,128)} %param.33) | copy-start | bytes 9220
  1682.0 371.8 %copy-start.6 = (f32[3,256,352]{1,2,0:T(8,128)S(1)}, f32[3,256,352]{1,2,0:T(8,128)}, u32[]{:S(2)}) copy-start(f32[3,256,352]{1,2,0:T(8,128)} %copy.198) | copy-start | bytes 3244036
  1687.5 368.8 %copy-start.49 = (f32[4]{0:T(128)S(1)}, f32[4]{0:T(128)}, u32[]{:S(2)}) copy-start(f32[4]{0:T(128)} %sqrt_multiply_fusion.1) | copy-start | bytes 52
  1819.1 239.2 %copy-start.38 = (f32[256,2]{0,1:T(2,128)}, f32[256,2]{0,1:T(2,128)S(1)}, u32[]{:S(2)}) copy-start(f32[256,2]{0,1:T(2,128)S(1)} %reshape.385) | copy-start | bytes 6148
  1924.1 134.2 %copy-start.37 = (f32[256,3]{0,1:T(4,128)}, f32[256,3]{0,1:T(4,128)S(1)}, u32[]{:S(2)}) copy-start(f32[256,3]{0,1:T(4,128)S(1)} %reshape.386) | copy-start | bytes 9220
  2053.8 2.5 copy-start.27
  2053.8 2.5 copy-start.28
  2053.8 2.5 copy-start.29
  2053.8 2.5 copy-start.30
  (16 other events, 20.8 us)
Sparse Core Ops, SparseCore 0:
  11.2 89.7 all-gather.10
  103.4 162.1 all-gather.12
  371.7 355.6 reduce-scatter.8
  729.5 729.6 reduce-scatter.10
  1461.3 30.9 all-gather.14
  1494.3 47.9 all-gather.16
  1544.2 33.6 all-gather.18
  1579.7 65.7 all-gather.20
  1647.8 129.4 reduce-scatter.12
  1779.4 130.1 reduce-scatter.14
  1912.6 141.1 all-reduce.2
where the time goes:
time: 2070 us
  waiting for transfers between devices  1640 us (79%)
  matrix products  151 us (7%)
  other arithmetic  93.6 us (5%)
  blocking collectives  80.7 us (4%)
  local copies, waits for them, and re-layouts  60.8 us (3%)
    reduce_scatter x1, waiting for transfers between devices, per_device(): lax.psum_scatter(arranged[1], ('seq', 'wt'), scatter_dimension=1, tiled=T...  730 us
    reduce_scatter x1, waiting for transfers between devices, per_device(): lax.psum_scatter(arranged[0], ('seq', 'wt'), scatter_dimension=1, tiled=T...  313 us
    unnamed x13, waiting for transfers between devices  179 us
    psum x1, waiting for transfers between devices, from_root(): return lax.psum(jnp.where(mine, value, jnp.zeros_like(value)), axis)  129 us
    all_gather x1, waiting for transfers between devices, per_device(): lax.all_gather(mlp_master.astype(jnp.bfloat16), 'wt', axis=1, tiled=True)  103 us
    all_gather x1, waiting for transfers between devices, per_device(): lax.all_gather(attn_master.astype(jnp.bfloat16), 'wt', axis=1, tiled=True)  68.6 us
    dot_general x5, matrix products, orthogonalize(): jnp.dot(poly_low, iterate, preferred_element_type=jnp.float32)  44.9 us
  transfers between devices with their start and end apart: 14, of which 12 were waited for; matrix products, arithmetic and copies ran while one was open for 11% of the time, Pallas kernels for 0%

commit v1 on v0

v1 whole, which is shorter than its diff:
```python
import math

import jax
import jax.numpy as jnp
from jax import lax
from jax.sharding import PartitionSpec as P

HEAD_DIM = 64
NS_STEPS = 5
STEP = 10

norm_eps = 1e-06
rope_base = 1000000.0
coef_a = 3.4445
coef_b = -4.775
coef_c = 2.0315
momentum_decay = 0.95
matrix_rate = 0.5
decay_rate = 0.01
first_decay = 0.9
second_decay = 0.95
vector_rate = 0.25
adam_eps = 1e-08
ortho_eps = 1e-07
masked_score = -1e30

MLP_OWNERS = (0, 2, 4)
ATTN_OWNERS = (1, 3, 5, 6)

f32 = jnp.float32
bf16 = jnp.bfloat16


def dot32(a, b, ca, cb):
    return lax.dot_general(a, b, (((ca,), (cb,)), ((), ())), preferred_element_type=f32)


def doc_layout(bounds, length):
    places = jnp.arange(length, dtype=jnp.int32)
    first_bound = bounds[0]
    second_bound = bounds[1]
    doc_index = (places >= first_bound).astype(jnp.int32) + (places >= second_bound).astype(
        jnp.int32
    )
    doc_start = jnp.where(
        places < first_bound, 0, jnp.where(places < second_bound, first_bound, second_bound)
    )
    return (doc_index, (places - doc_start).astype(f32))


def rope_tables(position, head_dim):
    half_dim = head_dim // 2
    frequency = rope_base ** (-2.0 * jnp.arange(half_dim, dtype=f32) / head_dim)
    angles = position[:, None] * frequency[None, :]
    cosine_table = jnp.cos(angles)
    sine_table = jnp.sin(angles)
    return (
        jnp.concatenate([cosine_table, cosine_table], 1),
        jnp.concatenate([sine_table, sine_table], 1),
    )


def rotate_half(values):
    half_dim = values.shape[-1] // 2
    return jnp.concatenate([-values[..., half_dim:], values[..., :half_dim]], axis=-1)


def apply_rope(values, cosine_table, sine_table):
    return values * cosine_table + rotate_half(values) * sine_table


def undo_rope(gradient, cosine_table, sine_table):
    return gradient * cosine_table - rotate_half(gradient * sine_table)


def masked_scores(query, key, doc_index):
    length = key.shape[1]
    places = jnp.arange(length, dtype=jnp.int32)
    allowed = (doc_index[:, None] == doc_index[None, :]) & (places[None, :] <= places[:, None])
    scores = jnp.einsum("hqd,hkd->hqk", query, key, preferred_element_type=f32)
    return jnp.where(allowed[None], scores * HEAD_DIM ** (-0.5), masked_score)


def attend_forward(query, key, value, doc_index):
    scores = masked_scores(query, key, doc_index)
    row_peak = jnp.max(scores, axis=-1, keepdims=True)
    exponent = jnp.exp(scores - row_peak)
    row_total = jnp.sum(exponent, axis=-1, keepdims=True)
    weights = (exponent / row_total).astype(bf16)
    attended = jnp.einsum("hqk,hkd->hqd", weights, value, preferred_element_type=f32)
    return attended.astype(bf16), row_peak + jnp.log(row_total)


def attend_backward(query, key, value, doc_index, log_total, d_attended):
    scores = masked_scores(query, key, doc_index)
    weights = jnp.exp(scores - log_total)
    d_value = jnp.einsum(
        "hqk,hqd->hkd", weights.astype(bf16), d_attended, preferred_element_type=f32
    )
    d_weights = jnp.einsum("hqd,hkd->hqk", d_attended, value, preferred_element_type=f32)
    inner = jnp.sum(weights * d_weights, axis=-1, keepdims=True)
    d_scores = (weights * (d_weights - inner)).astype(bf16)
    scale = HEAD_DIM ** (-0.5)
    d_query = jnp.einsum("hqk,hkd->hqd", d_scores, key, preferred_element_type=f32) * scale
    d_key = jnp.einsum("hqk,hqd->hkd", d_scores, query, preferred_element_type=f32) * scale
    return d_query, d_key, d_value


def norm_backward(d_normed, values, inverse, gain_row):
    scaled = d_normed * gain_row
    gain_part = jnp.sum(d_normed * values * inverse, axis=0)
    d_values = inverse * scaled - values * inverse**3 * jnp.mean(
        scaled * values, axis=-1, keepdims=True
    )
    return (d_values, gain_part)


def orthogonalize(matrix):
    wide = matrix.astype(f32)
    frobenius = jnp.sqrt(jnp.sum(wide * wide))
    iterate = (wide / (frobenius + ortho_eps)).astype(bf16)
    for _ in range(NS_STEPS):
        gram_low = dot32(iterate, iterate, 1, 1).astype(bf16)
        poly_low = (
            coef_b * gram_low.astype(f32) + coef_c * dot32(gram_low, gram_low, 1, 0)
        ).astype(bf16)
        iterate = (coef_a * iterate.astype(f32) + dot32(poly_low, iterate, 1, 0)).astype(bf16)
    return iterate


def adam_update(parameter, gradient, first_state, second_state):
    first_new = first_decay * first_state + (1.0 - first_decay) * gradient
    second_new = second_decay * second_state + (1.0 - second_decay) * gradient * gradient
    first_hat = first_new / (1.0 - first_decay**STEP)
    second_hat = second_new / (1.0 - second_decay**STEP)
    return (parameter - vector_rate * first_hat / (jnp.sqrt(second_hat) + adam_eps), second_new)


def swap(value, axis, bits, count):
    return lax.ppermute(value, axis, [(i, i ^ bits) for i in range(count)])


def sum_all(value, axis, count):
    bits = 1
    while bits < count:
        value = value + swap(value, axis, bits, count)
        bits *= 2
    return value


def gather_wt(block, wt_index, wt_count):
    rows = block.shape[0]
    whole = jnp.zeros((rows * wt_count,) + block.shape[1:], block.dtype)
    zeros = (0,) * (block.ndim - 1)
    for bits in range(wt_count):
        part = block if bits == 0 else swap(block, "wt", bits, wt_count)
        whole = lax.dynamic_update_slice(whole, part, ((wt_index ^ bits) * rows,) + zeros)
    return whole


def scatter_sum_wt(partial, wt_index, wt_count):
    rows = partial.shape[0] // wt_count
    total = lax.dynamic_slice_in_dim(partial, wt_index * rows, rows, 0)
    for bits in range(1, wt_count):
        sent = lax.dynamic_slice_in_dim(partial, (wt_index ^ bits) * rows, rows, 0).astype(bf16)
        total = total + swap(sent, "wt", bits, wt_count).astype(f32)
    return total


def scatter_sum_seq(partial, seq_index, seq_count):
    rows = partial.shape[0] // seq_count
    blocks = partial.reshape((seq_count // 2, 2, rows) + partial.shape[1:])
    core = seq_index % 2
    chip = seq_index // 2
    mine = lax.dynamic_index_in_dim(blocks, core, 1, keepdims=False)
    other = lax.dynamic_index_in_dim(blocks, 1 - core, 1, keepdims=False).astype(bf16)
    pair = mine + swap(other, "seq", 1, seq_count).astype(f32)
    total = lax.dynamic_index_in_dim(pair, chip, 0, keepdims=False)
    for bits in range(1, seq_count // 2):
        sent = lax.dynamic_index_in_dim(pair, chip ^ bits, 0, keepdims=False).astype(bf16)
        total = total + swap(sent, "seq", 2 * bits, seq_count).astype(f32)
    return total


def gather_owned(block, owners, wt_index, wt_count):
    rows, cols = block.shape
    whole = jnp.zeros((rows * wt_count, cols), block.dtype)
    whole = lax.dynamic_update_slice(whole, block, (wt_index * rows, 0))
    for bits in range(1, wt_count):
        pairs = [
            (owner * wt_count + w, owner * wt_count + (w ^ bits))
            for owner in owners
            for w in range(wt_count)
        ]
        part = lax.ppermute(block, ("seq", "wt"), pairs)
        whole = lax.dynamic_update_slice(whole, part, ((wt_index ^ bits) * rows, 0))
    return whole


def spread_owned(rows_block, owners, seq_index, seq_count):
    cols = rows_block.shape[1] // seq_count
    got = []
    for turn in range(seq_count):
        place = (seq_index + turn) % seq_count
        block = lax.dynamic_slice_in_dim(rows_block, place * cols, cols, 1)
        if turn:
            block = lax.ppermute(
                block, "seq", [(owner, (owner + turn) % seq_count) for owner in owners]
            )
        got.append(block)
    got = jnp.stack(got)
    return jnp.stack(
        [
            lax.dynamic_index_in_dim(got, (seq_index - owner) % seq_count, 0, keepdims=False)
            for owner in owners
        ]
    )


def per_device(
    tokens,
    cotangent,
    doc_bounds,
    attn_master,
    mlp_master,
    attn_momentum,
    mlp_momentum,
    gains,
    gain_first,
    gain_second,
    qkv_bias,
    bias_first,
    bias_second,
):
    seq_count = lax.axis_size("seq")
    wt_count = lax.axis_size("wt")
    seq_index = lax.axis_index("seq")
    wt_index = lax.axis_index("wt")
    row_count = tokens.shape[1]
    width = tokens.shape[2]
    ff = mlp_master.shape[2]
    shard = attn_master.shape[1]
    length = row_count * seq_count
    head_cols = width // seq_count
    ff_cols = ff // seq_count
    heads = head_cols // HEAD_DIM

    x_low = lax.all_gather(tokens[0], "seq", axis=0, tiled=True)
    dy_low = lax.all_gather(cotangent[0], "seq", axis=0, tiled=True)

    vectors = jnp.concatenate([gains, qkv_bias, jnp.zeros((3, shard), f32)], 0).astype(bf16)
    vectors = gather_wt(vectors[None], wt_index, wt_count)
    vectors = jnp.moveaxis(vectors, 0, 1).reshape(8, width).astype(f32)
    attn_own = lax.dynamic_slice_in_dim(attn_master, seq_index * head_cols, head_cols, 2)
    mlp_own = lax.dynamic_slice_in_dim(mlp_master, seq_index * ff_cols, ff_cols, 2)
    qkv_w = gather_wt(
        jnp.concatenate([attn_own[0], attn_own[1], attn_own[2]], 1).astype(bf16),
        wt_index,
        wt_count,
    )
    out_w = gather_wt(attn_master[3].astype(bf16), wt_index, wt_count)
    mlp_w = gather_wt(
        jnp.concatenate([mlp_own[0], mlp_own[1], mlp_own[2]], 1).astype(bf16),
        wt_index,
        wt_count,
    )
    gate_up_w = mlp_w[:, : 2 * ff_cols]
    down_w = mlp_w[:, 2 * ff_cols :]

    squares = jnp.concatenate(
        [
            jnp.sum(jnp.square(attn_master.astype(bf16).astype(f32)), axis=(1, 2)),
            jnp.sum(jnp.square(mlp_master.astype(bf16).astype(f32)), axis=(1, 2)),
        ]
    )
    squares = sum_all(jnp.pad(squares, (0, 121))[None], "wt", wt_count)[0]
    rms_attn = jnp.sqrt(squares[:4] / (width * width))
    rms_mlp = jnp.sqrt(squares[4:7] / (width * ff))

    gain_attn = vectors[0]
    gain_mlp = vectors[1]
    x_all = x_low.astype(f32)
    inverse_one = lax.rsqrt(jnp.mean(x_all * x_all, axis=-1, keepdims=True) + norm_eps)
    normed_one = (x_all * inverse_one * gain_attn).astype(bf16)
    bias_own = lax.dynamic_slice_in_dim(vectors[2:5], seq_index * head_cols, head_cols, 1)
    projected = (dot32(normed_one, qkv_w, 1, 0) + bias_own.reshape(1, 3 * head_cols)).astype(bf16)
    projected = jnp.moveaxis(projected.reshape(length, 3, heads, HEAD_DIM), 0, 2)
    doc_index, position = doc_layout(doc_bounds[0], length)
    cosine_table, sine_table = rope_tables(position, HEAD_DIM)
    query = apply_rope(projected[0].astype(f32), cosine_table, sine_table).astype(bf16)
    key = apply_rope(projected[1].astype(f32), cosine_table, sine_table).astype(bf16)
    value = projected[2]
    attended, log_total = attend_forward(query, key, value, doc_index)
    attended = jnp.moveaxis(attended, 0, 1).reshape(length, head_cols)
    attn_all = lax.all_gather(attended, "seq", axis=0)
    attn_all = jnp.moveaxis(attn_all, 0, 1).reshape(length, width)
    resid = x_all + dot32(attn_all, out_w, 1, 0)
    inverse_two = lax.rsqrt(jnp.mean(resid * resid, axis=-1, keepdims=True) + norm_eps)
    normed_two = (resid * inverse_two * gain_mlp).astype(bf16)
    gate_up = dot32(normed_two, gate_up_w, 1, 0)
    gate = gate_up[:, :ff_cols]
    up = gate_up[:, ff_cols:]
    sigmoid = jax.nn.sigmoid(gate)
    silu = gate * sigmoid
    hidden = (silu * up).astype(bf16)

    d_hidden = dot32(dy_low, down_w, 1, 0)
    d_gate = (d_hidden * up * (sigmoid * (1.0 + gate * (1.0 - sigmoid)))).astype(bf16)
    d_up = (d_hidden * silu).astype(bf16)
    d_gate_up = jnp.concatenate([d_gate, d_up], 1)
    d_normed_two = scatter_sum_seq(dot32(d_gate_up, gate_up_w, 1, 1), seq_index, seq_count)
    own_rows = seq_index * row_count
    x_own = tokens[0].astype(f32)
    resid_own = lax.dynamic_slice_in_dim(resid, own_rows, row_count, 0)
    inverse_two_own = lax.dynamic_slice_in_dim(inverse_two, own_rows, row_count, 0)
    d_resid_mlp, gain_part_two = norm_backward(d_normed_two, resid_own, inverse_two_own, gain_mlp)
    d_resid = cotangent[0].astype(f32) + d_resid_mlp
    d_resid_low = d_resid.astype(bf16)
    d_attn = dot32(d_resid_low, out_w, 1, 1).astype(bf16)
    pair = jnp.stack([d_attn, d_resid_low]).reshape(2, row_count, seq_count, head_cols)
    pair = lax.all_to_all(jnp.moveaxis(pair, 2, 0), "seq", split_axis=0, concat_axis=0)
    pair = jnp.moveaxis(pair, 0, 1).reshape(2, length, head_cols)
    d_attended = jnp.moveaxis(pair[0].reshape(length, heads, HEAD_DIM), 1, 0)

    mlp_part = jnp.concatenate(
        [dot32(normed_two, d_gate_up, 0, 0), dot32(dy_low, hidden, 0, 0)], 1
    )
    mlp_share = scatter_sum_wt(mlp_part, wt_index, wt_count).astype(bf16)
    mlp_grad = lax.all_gather(mlp_share, "seq", axis=0)
    mlp_grad = jnp.moveaxis(mlp_grad.reshape(seq_count, shard, 3, ff_cols), 0, 2)
    mlp_grad = mlp_grad.reshape(shard, 3, ff).swapaxes(0, 1).astype(f32)
    mlp_mom = momentum_decay * mlp_momentum + mlp_grad

    d_query, d_key, d_value = attend_backward(
        query, key, value, doc_index, log_total, d_attended
    )
    d_qkv = jnp.stack(
        [
            undo_rope(d_query, cosine_table, sine_table),
            undo_rope(d_key, cosine_table, sine_table),
            d_value,
        ]
    ).astype(bf16)
    d_qkv = jnp.moveaxis(d_qkv, 2, 0).reshape(length, 3 * head_cols)
    attn_part = jnp.concatenate(
        [dot32(normed_one, d_qkv, 0, 0), dot32(attn_all, pair[1], 0, 0)], 1
    )
    attn_share = scatter_sum_wt(attn_part, wt_index, wt_count).astype(bf16)
    attn_grad = lax.all_gather(attn_share, "seq", axis=0)
    attn_grad = jnp.moveaxis(attn_grad.reshape(seq_count, shard, 4, head_cols), 0, 2)
    attn_grad = attn_grad.reshape(shard, 4, width).swapaxes(0, 1).astype(f32)
    attn_mom = momentum_decay * attn_momentum + attn_grad
    bias_part = jnp.sum(d_qkv.astype(f32), axis=0).reshape(3, head_cols)

    mlp_pick = jnp.minimum(seq_index // 2, 2)
    attn_pick = jnp.minimum(seq_index // 2, 3)
    full_mlp = gather_owned(
        lax.dynamic_index_in_dim(mlp_mom, mlp_pick, 0, keepdims=False).astype(bf16),
        MLP_OWNERS,
        wt_index,
        wt_count,
    )
    full_attn = gather_owned(
        lax.dynamic_index_in_dim(attn_mom, attn_pick, 0, keepdims=False).astype(bf16),
        ATTN_OWNERS,
        wt_index,
        wt_count,
    )
    own_mlp = (seq_index == 0) | (seq_index == 2) | (seq_index == 4)
    own_attn = (seq_index == 1) | (seq_index == 3) | (seq_index == 5) | (seq_index == 6)

    def own_block(matrix):
        return lax.dynamic_slice_in_dim(orthogonalize(matrix), wt_index * shard, shard, 0)

    def empty_block(matrix):
        return jnp.zeros((shard, matrix.shape[1]), bf16)

    mlp_rows = lax.cond(own_mlp, own_block, empty_block, full_mlp)
    attn_rows = lax.cond(own_attn, own_block, empty_block, full_attn)
    mlp_steps = spread_owned(mlp_rows, MLP_OWNERS, seq_index, seq_count).astype(f32)
    attn_steps = spread_owned(attn_rows, ATTN_OWNERS, seq_index, seq_count).astype(f32)
    attn_new = (
        attn_own * (1.0 - matrix_rate * decay_rate)
        - (matrix_rate * math.sqrt(width) * rms_attn)[:, None, None] * attn_steps
    )
    mlp_new = (
        mlp_own * (1.0 - matrix_rate * decay_rate)
        - (matrix_rate * math.sqrt(ff) * rms_mlp)[:, None, None] * mlp_steps
    )

    layer_part = scatter_sum_seq(dot32(hidden, down_w, 1, 1), seq_index, seq_count)
    layer_out = (resid_own + layer_part).astype(bf16)
    d_normed_one = scatter_sum_seq(dot32(d_qkv, qkv_w, 1, 1), seq_index, seq_count)
    inverse_one_own = lax.dynamic_slice_in_dim(inverse_one, own_rows, row_count, 0)
    d_input_norm, gain_part_one = norm_backward(d_normed_one, x_own, inverse_one_own, gain_attn)
    tokens_grad = d_resid + d_input_norm

    bias_wide = lax.dynamic_update_slice(
        jnp.zeros((3, width), f32), bias_part, (0, seq_index * head_cols)
    )
    small = jnp.concatenate(
        [gain_part_one[None], gain_part_two[None], bias_wide, jnp.zeros((3, width), f32)], 0
    )
    small = sum_all(sum_all(small, "seq", seq_count), "wt", wt_count)
    small = lax.dynamic_slice_in_dim(small, wt_index * shard, shard, 1)
    gain_grad = small[:2]
    bias_grad = small[2:5]
    gain_new, gain_second_new = adam_update(gains, gain_grad, gain_first, gain_second)
    bias_new, bias_second_new = adam_update(qkv_bias, bias_grad, bias_first, bias_second)
    return (
        layer_out[None],
        tokens_grad[None],
        attn_grad,
        mlp_grad,
        attn_mom,
        mlp_mom,
        attn_new,
        mlp_new,
        gain_grad,
        gain_second_new,
        gain_new,
        bias_grad,
        bias_second_new,
        bias_new,
    )


def solution(mesh):
    return jax.shard_map(
        per_device,
        mesh=mesh,
        in_specs=(
            P("wt", "seq", None),
            P("wt", "seq", None),
            P("wt", None),
            P(None, "wt", None),
            P(None, "wt", None),
            P(None, "wt", None),
            P(None, "wt", None),
            P(None, "wt"),
            P(None, "wt"),
            P(None, "wt"),
            P(None, "wt"),
            P(None, "wt"),
            P(None, "wt"),
        ),
        out_specs=(
            P("wt", "seq", None),
            P("wt", "seq", None),
            P(None, "wt", None),
            P(None, "wt", None),
            P(None, "wt", None),
            P(None, "wt", None),
            P(None, "wt", "seq"),
            P(None, "wt", "seq"),
            P(None, "wt"),
            P(None, "wt"),
            P(None, "wt"),
            P(None, "wt"),
            P(None, "wt"),
            P(None, "wt"),
        ),
        check_vma=False,
    )
```

time: 2070 us -> 801 us (0.39)
  waiting for transfers between devices: 1640 us -> 351 us
  local copies, waits for them, and re-layouts: 60.8 us -> 150 us
  blocking collectives: 80.7 us -> 0 us
  starting transfers between devices: 16.4 us -> 80.7 us
  matrix products: 151 us -> 121 us
  other arithmetic: 93.6 us -> 66 us
    reduce_scatter x2 -> x0, waiting for transfers between devices: 1040 us -> none  [the longest x1 730 us: per_device(): lax.psum_scatter(arranged[1], ('seq', 'wt'), scatter_dimension=1, tiled=T...]
    ppermute x0 -> x57, waiting for transfers between devices: none -> 322 us  [the longest x14 184 us: spread_owned(): lax.ppermute(block, 'seq', [(owner, (owner + turn) % seq_count) for owner...]
    all_gather x6 -> x5, waiting for transfers between devices: 243 us -> 15 us  [the longest x1 15 us: per_device(): x_low = lax.all_gather(tokens[0], 'seq', axis=0, tiled=True)]
    unnamed x13 -> x5, waiting for transfers between devices: 179 us -> 0.75 us
    psum x1 -> x0, waiting for transfers between devices: 129 us -> none  [from_root(): return lax.psum(jnp.where(mine, value, jnp.zeros_like(value)), axis)]
    ppermute x0 -> x57, starting transfers between devices: none -> 76.3 us  [the longest x37 40.1 us: swap(): return lax.ppermute(value, axis, [(i, i ^ bits) for i in range(count)])]
    all_gather x4 -> x0, blocking collectives: 68.4 us -> none  [the longest x1 40.9 us: per_device(): lax.all_gather(shares[2].astype(jnp.bfloat16), 'seq', axis=1, tiled=True)]
    unnamed x109 -> x119, local copies, waits for them, and re-layouts: 13.1 us -> 73.2 us
  transfers between devices with their start and end apart: 14 -> 63, of which waited for: 12 -> 23; matrix products, arithmetic and copies ran while one was open for 11% -> 33% of each run, Pallas kernels for 0% -> 0%
where the time goes in v1:
time: 801 us; the launch traced here: 789 us
  waiting for transfers between devices  351 us (44%)
  local copies, waits for them, and re-layouts  150 us (19%)
  matrix products  121 us (15%)
  starting transfers between devices  80.7 us (10%)
  other arithmetic  66 us (8%)
  between operations  15.7 us (2%)
    ppermute x14, waiting for transfers between devices, spread_owned(): lax.ppermute(block, 'seq', [(owner, (owner + turn) % seq_count) for owner...  184 us
    ppermute x37, waiting for transfers between devices, swap(): return lax.ppermute(value, axis, [(i, i ^ bits) for i in range(count)])  129 us
    dot_general x22, matrix products, dot32(): lax.dot_general(a, b, (((ca,), (cb,)), ((), ())), preferred_element_type=...  105 us
    unnamed x119, local copies, waits for them, and re-layouts  73.2 us
    ppermute x37, starting transfers between devices, swap(): return lax.ppermute(value, axis, [(i, i ^ bits) for i in range(count)])  40.1 us
    ppermute x14, starting transfers between devices, spread_owned(): lax.ppermute(block, 'seq', [(owner, (owner + turn) % seq_count) for owner...  23.1 us
    dynamic_slice x6, local copies, waits for them, and re-layouts, scatter_sum_seq(): mine = lax.dynamic_index_in_dim(blocks, core, 1, keepdims=False)  17.4 us
  transfers between devices with their start and end apart: 63, of which 23 were waited for; matrix products, arithmetic and copies ran while one was open for 33% of the time, Pallas kernels for 0%

profile of v1, /device:TPU:1, one launch (start us, length us, event | category | flops | bytes accessed | tf_op | source)
XLA Modules:
  0.0 788.6 jit_solution(10917706785322569909)
XLA Ops:
  22.9 5.6 collective-permute-done.5
  28.6 15.0 %all-gather.12.cloned.1.call-done = bf16[1,1024,1024]{1,2,0:T(8,128)(2,1)} async-done(((bf16[1,128,1024]{1,2,0:T(8,128)(2,1)}), bf16[1,1024,1024]{1,2,0:T(8,128)(2,1)}) %all-gather.12.cloned.1.call-update) | async-done | bytes 2097168 | tf_op jit(solution)/shard_map/all_gather | solution.py:248
  81.1 7.9 %collective-permute-done.8 = bf16[256,1024]{1,0:T(8,128)(2,1)} collective-permute-done((bf16[256,1024]{1,0:T(8,128)(2,1)}, bf16[256,1024]{1,0:T(8,128)(2,1)}, u32[]{:S(2)}, u32[]{:S(2)}) %collective-permute-start.8) | collective-permute-done | bytes 524320 | tf_op jit(solution)/shard_map/ppermute | solution.py:140
  90.1 9.9 %collective-permute-done.9 = bf16[256,1056]{0,1:T(8,128)(2,1)} collective-permute-done((bf16[256,1056]{0,1:T(8,128)(2,1)S(1)}, bf16[256,1056]{0,1:T(8,128)(2,1)}, u32[]{:S(2)}, u32[]{:S(2)}) %collective-permute-start.9) | collective-permute-done | bytes 540704 | tf_op jit(solution)/shard_map/ppermute | solution.py:140
  103.8 8.5 %collective-permute-done.11 = bf16[256,1056]{0,1:T(8,128)(2,1)S(1)} collective-permute-done((bf16[256,1056]{0,1:T(8,128)(2,1)S(1)}, bf16[256,1056]{0,1:T(8,128)(2,1)S(1)}, u32[]{:S(2)}, u32[]{:S(2)}) %collective-permute-start.11) | collective-permute-done | bytes 540704 | tf_op jit(solution)/shard_map/ppermute | solution.py:140
  113.1 4.2 copy.131
  117.2 5.0 multiply_reduce_fusion.3
  124.3 4.7 fusion.76
  129.0 4.9 multiply_convert_fusion.3
  133.9 3.7 fusion.74
  141.2 3.1 collective-permute-start.16
  144.3 3.2 constant_dynamic-slice_fusion.27
  158.4 5.2 collective-permute-done.19
  163.6 17.1 %collective-permute-done.18 = bf16[128,1024]{0,1:T(8,128)(2,1)} collective-permute-done((bf16[128,1024]{0,1:T(8,128)(2,1)S(1)}, bf16[128,1024]{0,1:T(8,128)(2,1)}, u32[]{:S(2)}, u32[]{:S(2)}) %collective-permute-start.18) | collective-permute-done | bytes 262176 | tf_op jit(solution)/shard_map/ppermute | solution.py:140
  187.4 3.8 all-to-all-start
  191.7 14.1 %all-to-all-done = bf16[8,2,128,128]{3,2,1,0:T(8,128)(2,1)S(1)} async-done(((bf16[8,2,128,128]{3,2,1,0:T(8,128)(2,1)}), bf16[8,2,128,128]{3,2,1,0:T(8,128)(2,1)S(1)}, u32[]{:S(2)}, u32[]{:S(2)}) %all-to-all-start) | async-done | bytes 524320 | tf_op jit(solution)/shard_map/all_to_all | solution.py:321
  206.2 4.9 fusion.83
  211.1 5.4 multiply_reduce_fusion.1
  229.4 5.3 collective-permute-done.26
  234.7 6.8 collective-permute-done.25
  245.5 2.9 fusion.97
  251.3 11.7 %collective-permute-done.29 = bf16[256,1056]{0,1:T(8,128)(2,1)S(1)} collective-permute-done((bf16[256,1056]{0,1:T(8,128)(2,1)S(1)}, bf16[256,1056]{0,1:T(8,128)(2,1)S(1)}, u32[]{:S(2)}, u32[]{:S(2)}) %collective-permute-start.29) | collective-permute-done | bytes 540704 | tf_op jit(solution)/shard_map/ppermute | solution.py:140
  263.1 12.3 %collective-permute-done.28 = bf16[256,1056]{0,1:T(8,128)(2,1)S(1)} collective-permute-done((bf16[256,1056]{0,1:T(8,128)(2,1)S(1)}, bf16[256,1056]{0,1:T(8,128)(2,1)S(1)}, u32[]{:S(2)}, u32[]{:S(2)}) %collective-permute-start.28) | collective-permute-done | bytes 540704 | tf_op jit(solution)/shard_map/ppermute | solution.py:140
  276.5 4.3 multiply_reduce_fusion
  281.2 9.4 %copy.151 = f32[3,256,2816]{1,2,0:T(8,128)} copy(f32[3,256,2816]{2,1,0:T(8,128)} %param.23) | data formatting | bytes 17301504 | tf_op args[6]
  306.4 3.3 constant_dynamic-slice_fusion.29
  311.6 3.2 constant_dynamic-slice_fusion.25
  314.8 3.0 copy.146
  327.2 3.1 collective-permute-done.23
  330.3 13.7 %collective-permute-done.22 = bf16[128,1024]{0,1:T(8,128)(2,1)} collective-permute-done((bf16[128,1024]{0,1:T(8,128)(2,1)}, bf16[128,1024]{0,1:T(8,128)(2,1)}, u32[]{:S(2)}, u32[]{:S(2)}) %collective-permute-start.22) | collective-permute-done | bytes 262176 | tf_op jit(solution)/shard_map/ppermute | solution.py:140
  351.3 15.1 %collective-permute-done.53 = f32[8,1024]{1,0:T(8,128)S(1)} collective-permute-done((f32[8,1024]{1,0:T(8,128)S(1)}, f32[8,1024]{1,0:T(8,128)S(1)}, u32[]{:S(2)}, u32[]{:S(2)}) %collective-permute-start.53) | collective-permute-done | bytes 32800 | tf_op jit(solution)/shard_map/ppermute | solution.py:140
  380.1 4.0 copy.185
  384.1 5.5 copy.149
  389.6 4.9 reshape.318
  394.6 4.5 multiply_add_fusion.1
  401.1 3.3 collective-permute-start.32
  406.6 3.3 collective-permute-start.34
  411.2 8.8 %collective-permute-done.33 = bf16[256,1024]{1,0:T(8,128)(2,1)S(1)} collective-permute-done((bf16[256,1024]{1,0:T(8,128)(2,1)S(1)}, bf16[256,1024]{1,0:T(8,128)(2,1)S(1)}, u32[]{:S(2)}, u32[]{:S(2)}) %collective-permute-start.33) | collective-permute-done | bytes 524320 | tf_op jit(solution)/shard_map/ppermute | solution.py:195
  420.0 89.1 %conditional.2 = (bf16[256,1024]{1,0:T(8,128)(2,1)S(1)}) conditional(s32[]{:T(128)} %convert_element_type.703, () %tuple.28, (bf16[256,1024]{1,0:T(8,128)(2,1)S(1)}, s32[]{:T(128)}, bf16[256,1024]{1,0:T(8,128)(2,1)S(1)}, s32[]{:T(128)}, bf16[256,1024]{1,0:T(8,128)(2,1)S(1)}, /*index=5*/s32[]{:T(128)}, bf16[256,1024]{1,0:T(8,128)(2,1)S(1)}, ...), branch_computations={%region_9.10_spmd, %region_10.12_spmd} | conditional | flops 32268877824 | bytes 92274984 | solution.py:379
  421.4 2.9 dynamic_update_slice.90
  424.4 2.9 dynamic_update_slice.91
  427.3 4.1 dynamic_update_slice.92
  436.4 3.7 fusion.29
  440.1 9.0 %add_convert_fusion.7 = bf16[1024,1024]{1,0:T(8,128)(2,1)} fusion(bf16[1024,1024]{1,0:T(8,128)(2,1)} %fusion.29, f32[]{:T(128)S(6)} %add.431, bf16[1024,1024]{1,0:T(8,128)(2,1)S(1)} %dynamic_update_slice.93), kind=kOutput, calls=%fused_computation.11 | convolution fusion | flops 4310695936 | bytes 6291460 | tf_op jit(solution)/shard_map/cond/branch_1_fun/dot_general | solution.py:35
  449.0 6.1 fusion.177
  455.1 8.9 %add_convert_fusion.5 = bf16[1024,1024]{1,0:T(8,128)(2,1)} fusion(bf16[1024,1024]{1,0:T(8,128)(2,1)S(1)} %copy-done.47, bf16[1024,1024]{1,0:T(8,128)(2,1)} %fusion.177), kind=kOutput, calls=%fused_computation.9 | convolution fusion | flops 4304404480 | bytes 6291456 | tf_op jit(solution)/shard_map/cond/branch_1_fun/dot_general | solution.py:35
  464.0 6.3 fusion.178
  470.3 8.9 %add_convert_fusion.3 = bf16[1024,1024]{1,0:T(8,128)(2,1)} fusion(bf16[1024,1024]{1,0:T(8,128)(2,1)S(1)} %copy-done.48, bf16[1024,1024]{1,0:T(8,128)(2,1)} %fusion.178), kind=kOutput, calls=%fused_computation.7 | convolution fusion | flops 4304404480 | bytes 6291456 | tf_op jit(solution)/shard_map/cond/branch_1_fun/dot_general | solution.py:35
  479.2 5.9 fusion.179
  485.1 8.8 %add_convert_fusion.1 = bf16[1024,1024]{1,0:T(8,128)(2,1)S(1)} fusion(bf16[1024,1024]{1,0:T(8,128)(2,1)} %add_convert_fusion.3, bf16[1024,1024]{1,0:T(8,128)(2,1)} %fusion.179), kind=kOutput, calls=%fused_computation.5 | convolution fusion | flops 4304404480 | bytes 6291456 | tf_op jit(solution)/shard_map/cond/branch_1_fun/dot_general | solution.py:35
  494.0 3.7 fusion.180
  497.7 9.6 %fusion.17 = f32[1024,1024]{1,0:T(8,128)} fusion(bf16[1024,1024]{1,0:T(8,128)(2,1)S(1)} %add_convert_fusion.1, bf16[1024,1024]{1,0:T(8,128)(2,1)} %fusion.180), kind=kOutput, calls=%fused_computation.20 | convolution fusion | flops 4300210176 | bytes 8388608 | tf_op jit(solution)/shard_map/cond/branch_1_fun/dot_general | solution.py:35
  511.2 3.1 collective-permute-start.36
  516.3 5.5 collective-permute-start.38
  525.0 3.3 convert_element_type.727
  528.3 4.2 copy.186
  532.6 6.1 copy.150
  538.6 10.6 %multiply_add_fusion = f32[3,256,2816]{1,2,0:T(8,128)} fusion(f32[3,256,2816]{1,2,0:T(8,128)} %copy.151, f32[8,256,3,352]{1,3,0,2:T(8,128)} %copy.150), kind=kLoop, calls=%fused_computation.59 | loop fusion | flops 4325376 | bytes 25952256 | tf_op jit(solution)/shard_map/add | solution.py:332
  565.7 9.1 %copy.167 = f32[3,256,2816]{2,1,0:T(8,128)} copy(f32[3,256,2816]{1,2,0:T(8,128)} %multiply_add_fusion) | data formatting | bytes 17301504
  574.7 9.1 %copy.166 = f32[3,256,2816]{2,1,0:T(8,128)} copy(f32[3,256,2816]{1,2,0:T(8,128)} %bitcast.338) | data formatting | bytes 17301504
  583.8 2.9 conditional.3
  594.1 170.6 %collective-permute-done.45 = bf16[256,352]{0,1:T(8,128)(2,1)} collective-permute-done((bf16[256,352]{0,1:T(8,128)(2,1)}, bf16[256,352]{0,1:T(8,128)(2,1)}, u32[]{:S(2)}, u32[]{:S(2)}) %collective-permute-start.45) | collective-permute-done | bytes 180256 | tf_op jit(solution)/shard_map/ppermute | solution.py:207
  767.7 9.1 %collective-permute-done.49 = bf16[256,352]{0,1:T(8,128)(2,1)S(1)} collective-permute-done((bf16[256,352]{0,1:T(8,128)(2,1)S(1)}, bf16[256,352]{0,1:T(8,128)(2,1)S(1)}, u32[]{:S(2)}, u32[]{:S(2)}) %collective-permute-start.49) | collective-permute-done | bytes 180256 | tf_op jit(solution)/shard_map/ppermute | solution.py:207
  776.9 3.7 collective-permute-done.51
  (367 shorter events, 199.1 us)
Async XLA Ops:
  7.2 36.4 %all-gather.12.cloned.1.call-start = ((), (), s32[]{:S(2)}) async-start(), calls=%async_computation.2 | async-start | bytes 2359296 | tf_op jit(solution)/shard_map/all_gather | solution.py:248
  9.1 104.0 %all-gather.10.cloned.1.call-start = ((), (), s32[]{:S(2)}) async-start(), calls=%async_computation.1 | async-start | bytes 2359296 | tf_op jit(solution)/shard_map/all_gather | solution.py:295
  10.6 12.0 %collective-permute-start = (bf16[1,8,256]{2,1,0:T(8,128)(2,1)S(1)}, bf16[1,8,256]{2,1,0:T(8,128)(2,1)S(1)}, u32[]{:S(2)}, u32[]{:S(2)}) collective-permute-start(bf16[1,8,256]{2,1,0:T(8,128)(2,1)S(1)} %get-tuple-element.365), channel_id=1, source_target_pairs={{0,1},{1,0},{2,3},{3,2},{4,5},{5,4},{6,7},{7,6},{8,9},{9,8},{10,11... | collective-permute-start | bytes 12296 | tf_op jit(solution)/shard_map/ppermute | solution.py:140
  12.7 10.0 %collective-permute-start.1 = (bf16[1,8,256]{2,1,0:T(8,128)(2,1)S(1)}, bf16[1,8,256]{2,1,0:T(8,128)(2,1)S(1)}, u32[]{:S(2)}, u32[]{:S(2)}) collective-permute-start(bf16[1,8,256]{2,1,0:T(8,128)(2,1)S(1)} %get-tuple-element.365), channel_id=1, source_target_pairs={{0,2},{1,3},{2,0},{3,1},{4,6},{5,7},{6,4},{7,5},{8,10},{9,11},{10,... | collective-permute-start | bytes 12296 | tf_op jit(solution)/shard_map/ppermute | solution.py:140
  13.9 8.8 %collective-permute-start.2 = (bf16[1,8,256]{2,1,0:T(8,128)(2,1)S(1)}, bf16[1,8,256]{2,1,0:T(8,128)(2,1)S(1)}, u32[]{:S(2)}, u32[]{:S(2)}) collective-permute-start(bf16[1,8,256]{2,1,0:T(8,128)(2,1)S(1)} %get-tuple-element.365), channel_id=1, source_target_pairs={{0,3},{1,2},{2,1},{3,0},{4,7},{5,6},{6,5},{7,4},{8,11},{9,10},{10,... | collective-permute-start | bytes 12296 | tf_op jit(solution)/shard_map/ppermute | solution.py:140
  15.2 7.6 collective-permute-start.3
  16.6 6.2 collective-permute-start.4
  22.7 5.8 collective-permute-start.5
  57.8 71.2 %all-gather.14.cloned.1.call-start = ((), (), s32[]{:S(2)}) async-start(), calls=%async_computation.3 | async-start | bytes 2359296 | tf_op jit(solution)/shard_map/all_gather | solution.py:249
  63.5 13.6 %collective-permute-start.6 = (bf16[256,1024]{1,0:T(8,128)(2,1)}, bf16[256,1024]{1,0:T(8,128)(2,1)}, u32[]{:S(2)}, u32[]{:S(2)}) collective-permute-start(bf16[256,1024]{1,0:T(8,128)(2,1)} %slice_bitcast_fusion), channel_id=1, source_target_pairs={{0,1},{1,0},{2,3},{3,2},{4,5},{5,4},{6,7},{7,6},{8,9},{9,8},{10,11... | collective-permute-start | bytes 1572872 | tf_op jit(solution)/shard_map/ppermute | solution.py:140
  64.5 15.6 %collective-permute-start.7 = (bf16[256,1024]{1,0:T(8,128)(2,1)}, bf16[256,1024]{1,0:T(8,128)(2,1)}, u32[]{:S(2)}, u32[]{:S(2)}) collective-permute-start(bf16[256,1024]{1,0:T(8,128)(2,1)} %slice_bitcast_fusion), channel_id=1, source_target_pairs={{0,2},{1,3},{2,0},{3,1},{4,6},{5,7},{6,4},{7,5},{8,10},{9,11},{10,... | collective-permute-start | bytes 1572872 | tf_op jit(solution)/shard_map/ppermute | solution.py:140
  65.7 23.4 %collective-permute-start.8 = (bf16[256,1024]{1,0:T(8,128)(2,1)}, bf16[256,1024]{1,0:T(8,128)(2,1)}, u32[]{:S(2)}, u32[]{:S(2)}) collective-permute-start(bf16[256,1024]{1,0:T(8,128)(2,1)} %slice_bitcast_fusion), channel_id=1, source_target_pairs={{0,3},{1,2},{2,1},{3,0},{4,7},{5,6},{6,5},{7,4},{8,11},{9,10},{10,... | collective-permute-start | bytes 1572872 | tf_op jit(solution)/shard_map/ppermute | solution.py:140
  70.9 29.1 %collective-permute-start.9 = (bf16[256,1056]{0,1:T(8,128)(2,1)S(1)}, bf16[256,1056]{0,1:T(8,128)(2,1)}, u32[]{:S(2)}, u32[]{:S(2)}) collective-permute-start(bf16[256,1056]{0,1:T(8,128)(2,1)S(1)} %get-tuple-element.322), channel_id=1, source_target_pairs={{0,1},{1,0},{2,3},{3,2},{4,5},{5,4},{6,7},{7,6},{8,9},{9,8},{10,11... | collective-permute-start | bytes 1622024 | tf_op jit(solution)/shard_map/ppermute | solution.py:140
  71.9 30.0 %collective-permute-start.10 = (bf16[256,1056]{0,1:T(8,128)(2,1)S(1)}, bf16[256,1056]{0,1:T(8,128)(2,1)}, u32[]{:S(2)}, u32[]{:S(2)}) collective-permute-start(bf16[256,1056]{0,1:T(8,128)(2,1)S(1)} %get-tuple-element.322), channel_id=1, source_target_pairs={{0,2},{1,3},{2,0},{3,1},{4,6},{5,7},{6,4},{7,5},{8,10},{9,11},{10,... | collective-permute-start | bytes 1622024 | tf_op jit(solution)/shard_map/ppermute | solution.py:140
  77.1 35.1 %collective-permute-start.11 = (bf16[256,1056]{0,1:T(8,128)(2,1)S(1)}, bf16[256,1056]{0,1:T(8,128)(2,1)S(1)}, u32[]{:S(2)}, u32[]{:S(2)}) collective-permute-start(bf16[256,1056]{0,1:T(8,128)(2,1)S(1)} %get-tuple-element.322), channel_id=1, source_target_pairs={{0,3},{1,2},{2,1},{3,0},{4,7},{5,6},{6,5},{7,4},{8,11},{9,10},{10,... | collective-permute-start | bytes 1622024 | tf_op jit(solution)/shard_map/ppermute | solution.py:140
  141.2 9.2 %collective-permute-start.16 = (bf16[4,128,1024]{1,2,0:T(8,128)(2,1)}, bf16[4,128,1024]{1,2,0:T(8,128)(2,1)S(1)}, u32[]{:S(2)}, u32[]{:S(2)}) collective-permute-start(bf16[4,128,1024]{1,2,0:T(8,128)(2,1)} %bitcast.358), channel_id=1, source_target_pairs={{0,4},{4,0},{8,12},{12,8},{16,20},{20,16},{24,28},{28,24},{1,5},{5... | collective-permute-start | bytes 3145736 | tf_op jit(solution)/shard_map/ppermute | solution.py:140
  153.6 10.0 %collective-permute-start.19 = (bf16[128,1024]{0,1:T(8,128)(2,1)S(1)}, bf16[128,1024]{0,1:T(8,128)(2,1)}, u32[]{:S(2)}, u32[]{:S(2)}) collective-permute-start(bf16[128,1024]{0,1:T(8,128)(2,1)S(1)} %get-tuple-element.302), channel_id=1, source_target_pairs={{0,24},{4,28},{8,16},{12,20},{16,8},{20,12},{24,0},{28,4},{1,25},{... | collective-permute-start | bytes 786440 | tf_op jit(solution)/shard_map/ppermute | solution.py:140
  154.8 25.9 %collective-permute-start.18 = (bf16[128,1024]{0,1:T(8,128)(2,1)S(1)}, bf16[128,1024]{0,1:T(8,128)(2,1)}, u32[]{:S(2)}, u32[]{:S(2)}) collective-permute-start(bf16[128,1024]{0,1:T(8,128)(2,1)S(1)} %get-tuple-element.303), channel_id=1, source_target_pairs={{0,16},{4,20},{8,24},{12,28},{16,0},{20,4},{24,8},{28,12},{1,17},{... | collective-permute-start | bytes 786440 | tf_op jit(solution)/shard_map/ppermute | solution.py:140
  157.0 23.7 %collective-permute-start.17 = (bf16[128,1024]{0,1:T(8,128)(2,1)S(1)}, bf16[128,1024]{0,1:T(8,128)(2,1)}, u32[]{:S(2)}, u32[]{:S(2)}) collective-permute-start(bf16[128,1024]{0,1:T(8,128)(2,1)S(1)} %get-tuple-element.301), channel_id=1, source_target_pairs={{0,8},{4,12},{8,0},{12,4},{16,24},{20,28},{24,16},{28,20},{1,9},{5... | collective-permute-start | bytes 786440 | tf_op jit(solution)/shard_map/ppermute | solution.py:140
  187.4 18.3 %all-to-all-start = ((bf16[8,2,128,128]{3,2,1,0:T(8,128)(2,1)}), bf16[8,2,128,128]{3,2,1,0:T(8,128)(2,1)S(1)}, u32[]{:S(2)}, u32[]{:S(2)}) async-start(bf16[8,2,128,128]{3,2,1,0:T(8,128)(2,1)} %maximum_bitcast_fusion), calls=%async_computation | async-start | bytes 1048576 | tf_op jit(solution)/shard_map/all_to_all | solution.py:321
  191.2 186.8 %all-gather.16.cloned.1.call-start = ((), (), s32[]{:S(2)}) async-start(), calls=%async_computation.4 | async-start | bytes 2359296 | tf_op jit(solution)/shard_map/all_gather | solution.py:349
  226.7 8.0 %collective-permute-start.26 = (bf16[256,512]{0,1:T(8,128)(2,1)S(1)}, bf16[256,512]{0,1:T(8,128)(2,1)S(1)}, u32[]{:S(2)}, u32[]{:S(2)}) collective-permute-start(bf16[256,512]{0,1:T(8,128)(2,1)S(1)} %get-tuple-element.297), channel_id=1, source_target_pairs={{0,3},{1,2},{2,1},{3,0},{4,7},{5,6},{6,5},{7,4},{8,11},{9,10},{10,... | collective-permute-start | bytes 786440 | tf_op jit(solution)/shard_map/ppermute | solution.py:140
  228.0 13.6 %collective-permute-start.25 = (bf16[256,512]{0,1:T(8,128)(2,1)S(1)}, bf16[256,512]{0,1:T(8,128)(2,1)S(1)}, u32[]{:S(2)}, u32[]{:S(2)}) collective-permute-start(bf16[256,512]{0,1:T(8,128)(2,1)S(1)} %get-tuple-element.296), channel_id=1, source_target_pairs={{0,2},{1,3},{2,0},{3,1},{4,6},{5,7},{6,4},{7,5},{8,10},{9,11},{10,... | collective-permute-start | bytes 786440 | tf_op jit(solution)/shard_map/ppermute | solution.py:140
  228.0 13.6 %collective-permute-start.24 = (bf16[256,512]{0,1:T(8,128)(2,1)S(1)}, bf16[256,512]{0,1:T(8,128)(2,1)S(1)}, u32[]{:S(2)}, u32[]{:S(2)}) collective-permute-start(bf16[256,512]{0,1:T(8,128)(2,1)S(1)} %get-tuple-element.295), channel_id=1, source_target_pairs={{0,1},{1,0},{2,3},{3,2},{4,5},{5,4},{6,7},{7,6},{8,9},{9,8},{10,11... | collective-permute-start | bytes 786440 | tf_op jit(solution)/shard_map/ppermute | solution.py:140
  242.4 282.6 %all-gather.18.cloned.1.call-start = ((), (), s32[]{:S(2)}) async-start(), calls=%async_computation.5 | async-start | bytes 4866048 | tf_op jit(solution)/shard_map/all_gather | solution.py:329
  248.6 14.5 %collective-permute-start.29 = (bf16[256,1056]{0,1:T(8,128)(2,1)S(1)}, bf16[256,1056]{0,1:T(8,128)(2,1)S(1)}, u32[]{:S(2)}, u32[]{:S(2)}) collective-permute-start(bf16[256,1056]{0,1:T(8,128)(2,1)S(1)} %get-tuple-element.289), channel_id=1, source_target_pairs={{0,3},{1,2},{2,1},{3,0},{4,7},{5,6},{6,5},{7,4},{8,11},{9,10},{10,... | collective-permute-start | bytes 1622024 | tf_op jit(solution)/shard_map/ppermute | solution.py:140
  249.9 25.5 %collective-permute-start.28 = (bf16[256,1056]{0,1:T(8,128)(2,1)S(1)}, bf16[256,1056]{0,1:T(8,128)(2,1)S(1)}, u32[]{:S(2)}, u32[]{:S(2)}) collective-permute-start(bf16[256,1056]{0,1:T(8,128)(2,1)S(1)} %get-tuple-element.288), channel_id=1, source_target_pairs={{0,2},{1,3},{2,0},{3,1},{4,6},{5,7},{6,4},{7,5},{8,10},{9,11},{10,... | collective-permute-start | bytes 1622024 | tf_op jit(solution)/shard_map/ppermute | solution.py:140
  249.9 25.5 %collective-permute-start.27 = (bf16[256,1056]{0,1:T(8,128)(2,1)S(1)}, bf16[256,1056]{0,1:T(8,128)(2,1)S(1)}, u32[]{:S(2)}, u32[]{:S(2)}) collective-permute-start(bf16[256,1056]{0,1:T(8,128)(2,1)S(1)} %get-tuple-element.287), channel_id=1, source_target_pairs={{0,1},{1,0},{2,3},{3,2},{4,5},{5,4},{6,7},{7,6},{8,9},{9,8},{10,11... | collective-permute-start | bytes 1622024 | tf_op jit(solution)/shard_map/ppermute | solution.py:140
  280.9 9.7 %collective-permute-start.30 = (f32[1,128]{1,0:T(1,128)S(1)}, f32[1,128]{1,0:T(1,128)S(1)}, u32[]{:S(2)}, u32[]{:S(2)}) collective-permute-start(f32[1,128]{1,0:T(1,128)S(1)} %fusion.164), channel_id=1, source_target_pairs={{0,1},{1,0},{2,3},{3,2},{4,5},{5,4},{6,7},{7,6},{8,9},{9,8},{10,11... | collective-permute-start | bytes 1544 | tf_op jit(solution)/shard_map/ppermute | solution.py:140
  290.7 2.8 collective-permute-start.31
  298.9 18.8 %collective-permute-start.20 = (bf16[4,128,1024]{1,2,0:T(8,128)(2,1)}, bf16[4,128,1024]{1,2,0:T(8,128)(2,1)}, u32[]{:S(2)}, u32[]{:S(2)}) collective-permute-start(bf16[4,128,1024]{1,2,0:T(8,128)(2,1)} %bitcast.359), channel_id=1, source_target_pairs={{0,4},{4,0},{8,12},{12,8},{16,20},{20,16},{24,28},{28,24},{1,5},{5... | collective-permute-start | bytes 3145736 | tf_op jit(solution)/shard_map/ppermute | solution.py:140
  306.3 18.1 %collective-permute-start.12 = (bf16[4,128,1024]{1,2,0:T(8,128)(2,1)}, bf16[4,128,1024]{1,2,0:T(8,128)(2,1)}, u32[]{:S(2)}, u32[]{:S(2)}) collective-permute-start(bf16[4,128,1024]{1,2,0:T(8,128)(2,1)} %bitcast.263), channel_id=1, source_target_pairs={{0,4},{4,0},{8,12},{12,8},{16,20},{20,16},{24,28},{28,24},{1,5},{5... | collective-permute-start | bytes 3145736 | tf_op jit(solution)/shard_map/ppermute | solution.py:140
  320.8 9.5 %collective-permute-start.23 = (bf16[128,1024]{0,1:T(8,128)(2,1)}, bf16[128,1024]{0,1:T(8,128)(2,1)S(1)}, u32[]{:S(2)}, u32[]{:S(2)}) collective-permute-start(bf16[128,1024]{0,1:T(8,128)(2,1)} %get-tuple-element.299), channel_id=1, source_target_pairs={{0,24},{4,28},{8,16},{12,20},{16,8},{20,12},{24,0},{28,4},{1,25},{... | collective-permute-start | bytes 786440 | tf_op jit(solution)/shard_map/ppermute | solution.py:140
  322.1 21.8 %collective-permute-start.22 = (bf16[128,1024]{0,1:T(8,128)(2,1)}, bf16[128,1024]{0,1:T(8,128)(2,1)}, u32[]{:S(2)}, u32[]{:S(2)}) collective-permute-start(bf16[128,1024]{0,1:T(8,128)(2,1)} %get-tuple-element.300), channel_id=1, source_target_pairs={{0,16},{4,20},{8,24},{12,28},{16,0},{20,4},{24,8},{28,12},{1,17},{... | collective-permute-start | bytes 786440 | tf_op jit(solution)/shard_map/ppermute | solution.py:140
  322.2 21.8 %collective-permute-start.21 = (bf16[128,1024]{0,1:T(8,128)(2,1)}, bf16[128,1024]{0,1:T(8,128)(2,1)}, u32[]{:S(2)}, u32[]{:S(2)}) collective-permute-start(bf16[128,1024]{0,1:T(8,128)(2,1)} %get-tuple-element.298), channel_id=1, source_target_pairs={{0,8},{4,12},{8,0},{12,4},{16,24},{20,28},{24,16},{28,20},{1,9},{5... | collective-permute-start | bytes 786440 | tf_op jit(solution)/shard_map/ppermute | solution.py:140
  345.6 5.0 collective-permute-start.52
  347.0 25.4 %collective-permute-start.15 = (bf16[128,1024]{0,1:T(8,128)(2,1)S(1)}, bf16[128,1024]{0,1:T(8,128)(2,1)S(1)}, u32[]{:S(2)}, u32[]{:S(2)}) collective-permute-start(bf16[128,1024]{0,1:T(8,128)(2,1)S(1)} %get-tuple-element.305), channel_id=1, source_target_pairs={{0,24},{4,28},{8,16},{12,20},{16,8},{20,12},{24,0},{28,4},{1,25},{... | collective-permute-start | bytes 786440 | tf_op jit(solution)/shard_map/ppermute | solution.py:140
  348.8 23.6 %collective-permute-start.14 = (bf16[128,1024]{0,1:T(8,128)(2,1)S(1)}, bf16[128,1024]{0,1:T(8,128)(2,1)S(1)}, u32[]{:S(2)}, u32[]{:S(2)}) collective-permute-start(bf16[128,1024]{0,1:T(8,128)(2,1)S(1)} %get-tuple-element.306), channel_id=1, source_target_pairs={{0,16},{4,20},{8,24},{12,28},{16,0},{20,4},{24,8},{28,12},{1,17},{... | collective-permute-start | bytes 786440 | tf_op jit(solution)/shard_map/ppermute | solution.py:140
  348.8 23.6 %collective-permute-start.13 = (bf16[128,1024]{0,1:T(8,128)(2,1)S(1)}, bf16[128,1024]{0,1:T(8,128)(2,1)S(1)}, u32[]{:S(2)}, u32[]{:S(2)}) collective-permute-start(bf16[128,1024]{0,1:T(8,128)(2,1)S(1)} %get-tuple-element.304), channel_id=1, source_target_pairs={{0,8},{4,12},{8,0},{12,4},{16,24},{20,28},{24,16},{28,20},{1,9},{5... | collective-permute-start | bytes 786440 | tf_op jit(solution)/shard_map/ppermute | solution.py:140
  350.6 15.9 %collective-permute-start.53 = (f32[8,1024]{1,0:T(8,128)S(1)}, f32[8,1024]{1,0:T(8,128)S(1)}, u32[]{:S(2)}, u32[]{:S(2)}) collective-permute-start(f32[8,1024]{1,0:T(8,128)S(1)} %fusion.167), channel_id=1, source_target_pairs={{0,8},{4,12},{8,0},{12,4},{16,24},{20,28},{24,16},{28,20},{1,9},{5... | collective-permute-start | bytes 98312 | tf_op jit(solution)/shard_map/ppermute | solution.py:140
  366.5 4.6 collective-permute-start.54
  371.1 6.4 collective-permute-start.55
  377.5 32.4 %collective-permute-start.56 = (f32[8,1024]{1,0:T(8,128)S(1)}, f32[8,1024]{1,0:T(8,128)S(1)}, u32[]{:S(2)}, u32[]{:S(2)}) collective-permute-start(f32[8,1024]{1,0:T(8,128)S(1)} %add.673), channel_id=1, source_target_pairs={{0,2},{1,3},{2,0},{3,1},{4,6},{5,7},{6,4},{7,5},{8,10},{9,11},{10,... | collective-permute-start | bytes 98312 | tf_op jit(solution)/shard_map/ppermute | solution.py:140
  401.1 10.1 %collective-permute-start.32 = (bf16[256,1024]{1,0:T(8,128)(2,1)S(1)}, bf16[256,1024]{1,0:T(8,128)(2,1)S(1)}, u32[]{:S(2)}, u32[]{:S(2)}) collective-permute-start(bf16[256,1024]{1,0:T(8,128)(2,1)S(1)} %fusion.114), channel_id=1, source_target_pairs={{4,5},{5,4},{6,7},{7,6},{12,13},{13,12},{14,15},{15,14},{20,21},{2... | collective-permute-start | bytes 1572872 | tf_op jit(solution)/shard_map/ppermute | solution.py:195
  404.5 15.5 %collective-permute-start.33 = (bf16[256,1024]{1,0:T(8,128)(2,1)S(1)}, bf16[256,1024]{1,0:T(8,128)(2,1)S(1)}, u32[]{:S(2)}, u32[]{:S(2)}) collective-permute-start(bf16[256,1024]{1,0:T(8,128)(2,1)S(1)} %fusion.114), channel_id=1, source_target_pairs={{4,6},{5,7},{6,4},{7,5},{12,14},{13,15},{14,12},{15,13},{20,22},{2... | collective-permute-start | bytes 1572872 | tf_op jit(solution)/shard_map/ppermute | solution.py:195
  406.6 13.4 %collective-permute-start.34 = (bf16[256,1024]{1,0:T(8,128)(2,1)S(1)}, bf16[256,1024]{1,0:T(8,128)(2,1)S(1)}, u32[]{:S(2)}, u32[]{:S(2)}) collective-permute-start(bf16[256,1024]{1,0:T(8,128)(2,1)S(1)} %fusion.114), channel_id=1, source_target_pairs={{4,7},{5,6},{6,5},{7,4},{12,15},{13,14},{14,13},{15,12},{20,23},{2... | collective-permute-start | bytes 1572872 | tf_op jit(solution)/shard_map/ppermute | solution.py:195
  509.9 13.8 %collective-permute-start.35 = (bf16[256,128]{1,0:T(8,128)(2,1)S(1)}, bf16[256,128]{1,0:T(8,128)(2,1)S(1)}, u32[]{:S(2)}, u32[]{:S(2)}) collective-permute-start(bf16[256,128]{1,0:T(8,128)(2,1)S(1)} %get-tuple-element.337), channel_id=1, source_target_pairs={{4,8},{12,16},{20,24},{24,28},{5,9},{13,17},{21,25},{25,29},{6,10}... | collective-permute-start | bytes 196616 | tf_op jit(solution)/shard_map/ppermute | solution.py:207
  511.2 13.2 %collective-permute-start.36 = (bf16[256,128]{1,0:T(8,128)(2,1)S(1)}, bf16[256,128]{1,0:T(8,128)(2,1)S(1)}, u32[]{:S(2)}, u32[]{:S(2)}) collective-permute-start(bf16[256,128]{1,0:T(8,128)(2,1)S(1)} %get-tuple-element.336), channel_id=1, source_target_pairs={{4,12},{12,20},{20,28},{24,0},{5,13},{13,21},{21,29},{25,1},{6,14}... | collective-permute-start | bytes 196616 | tf_op jit(solution)/shard_map/ppermute | solution.py:207
  514.3 39.3 %collective-permute-start.37 = (bf16[256,128]{1,0:T(8,128)(2,1)}, bf16[256,128]{1,0:T(8,128)(2,1)S(1)}, u32[]{:S(2)}, u32[]{:S(2)}) collective-permute-start(bf16[256,128]{1,0:T(8,128)(2,1)} %get-tuple-element.335), channel_id=1, source_target_pairs={{4,16},{12,24},{20,0},{24,4},{5,17},{13,25},{21,1},{25,5},{6,18},{... | collective-permute-start | bytes 196616 | tf_op jit(solution)/shard_map/ppermute | solution.py:207
  516.3 39.8 %collective-permute-start.38 = (bf16[256,128]{1,0:T(8,128)(2,1)}, bf16[256,128]{1,0:T(8,128)(2,1)S(1)}, u32[]{:S(2)}, u32[]{:S(2)}) collective-permute-start(bf16[256,128]{1,0:T(8,128)(2,1)} %get-tuple-element.334), channel_id=1, source_target_pairs={{4,20},{12,28},{20,4},{24,8},{5,21},{13,29},{21,5},{25,9},{6,22},{... | collective-permute-start | bytes 196616 | tf_op jit(solution)/shard_map/ppermute | solution.py:207
  521.8 36.9 %collective-permute-start.39 = (bf16[256,128]{1,0:T(8,128)(2,1)S(1)}, bf16[256,128]{1,0:T(8,128)(2,1)S(1)}, u32[]{:S(2)}, u32[]{:S(2)}) collective-permute-start(bf16[256,128]{1,0:T(8,128)(2,1)S(1)} %get-tuple-element.333), channel_id=1, source_target_pairs={{4,24},{12,0},{20,8},{24,12},{5,25},{13,1},{21,9},{25,13},{6,26},{... | collective-permute-start | bytes 196616 | tf_op jit(solution)/shard_map/ppermute | solution.py:207
  551.1 32.7 %collective-permute-start.42 = (bf16[256,2816]{0,1:T(8,128)(2,1)S(1)}, bf16[256,2816]{0,1:T(8,128)(2,1)S(1)}, u32[]{:S(2)}, u32[]{:S(2)}) collective-permute-start(bf16[256,2816]{0,1:T(8,128)(2,1)S(1)} %fusion.72), channel_id=1, source_target_pairs={{0,1},{1,0},{2,3},{3,2},{8,9},{9,8},{10,11},{11,10},{16,17},{17,16... | collective-permute-start | bytes 4325384 | tf_op jit(solution)/shard_map/ppermute | solution.py:195
  551.9 31.9 %collective-permute-start.43 = (bf16[256,2816]{0,1:T(8,128)(2,1)S(1)}, bf16[256,2816]{0,1:T(8,128)(2,1)}, u32[]{:S(2)}, u32[]{:S(2)}) collective-permute-start(bf16[256,2816]{0,1:T(8,128)(2,1)S(1)} %fusion.72), channel_id=1, source_target_pairs={{0,2},{1,3},{2,0},{3,1},{8,10},{9,11},{10,8},{11,9},{16,18},{17,19... | collective-permute-start | bytes 4325384 | tf_op jit(solution)/shard_map/ppermute | solution.py:195
  553.7 30.2 %collective-permute-start.44 = (bf16[256,2816]{0,1:T(8,128)(2,1)S(1)}, bf16[256,2816]{0,1:T(8,128)(2,1)}, u32[]{:S(2)}, u32[]{:S(2)}) collective-permute-start(bf16[256,2816]{0,1:T(8,128)(2,1)S(1)} %fusion.72), channel_id=1, source_target_pairs={{0,3},{1,2},{2,1},{3,0},{8,11},{9,10},{10,9},{11,8},{16,19},{17,18... | collective-permute-start | bytes 4325384 | tf_op jit(solution)/shard_map/ppermute | solution.py:195
  556.1 5.4 collective-permute-start.40
  558.6 3.5 collective-permute-start.41
  588.6 176.2 %collective-permute-start.45 = (bf16[256,352]{0,1:T(8,128)(2,1)}, bf16[256,352]{0,1:T(8,128)(2,1)}, u32[]{:S(2)}, u32[]{:S(2)}) collective-permute-start(bf16[256,352]{0,1:T(8,128)(2,1)} %copy.177), channel_id=1, source_target_pairs={{0,4},{8,12},{16,20},{1,5},{9,13},{17,21},{2,6},{10,14},{18,22},{3... | collective-permute-start | bytes 540680 | tf_op jit(solution)/shard_map/ppermute | solution.py:207
  590.0 176.3 %collective-permute-start.46 = (bf16[256,352]{0,1:T(8,128)(2,1)S(1)}, bf16[256,352]{0,1:T(8,128)(2,1)S(1)}, u32[]{:S(2)}, u32[]{:S(2)}) collective-permute-start(bf16[256,352]{0,1:T(8,128)(2,1)S(1)} %copy.178), channel_id=1, source_target_pairs={{0,8},{8,16},{16,24},{1,9},{9,17},{17,25},{2,10},{10,18},{18,26},{... | collective-permute-start | bytes 540680 | tf_op jit(solution)/shard_map/ppermute | solution.py:207
  590.8 176.8 %collective-permute-start.47 = (bf16[256,352]{0,1:T(8,128)(2,1)S(1)}, bf16[256,352]{0,1:T(8,128)(2,1)S(1)}, u32[]{:S(2)}, u32[]{:S(2)}) collective-permute-start(bf16[256,352]{0,1:T(8,128)(2,1)S(1)} %copy.179), channel_id=1, source_target_pairs={{0,12},{8,20},{16,28},{1,13},{9,21},{17,29},{2,14},{10,22},{18,30}... | collective-permute-start | bytes 540680 | tf_op jit(solution)/shard_map/ppermute | solution.py:207
  591.6 176.1 %collective-permute-start.48 = (bf16[256,352]{0,1:T(8,128)(2,1)S(1)}, bf16[256,352]{0,1:T(8,128)(2,1)S(1)}, u32[]{:S(2)}, u32[]{:S(2)}) collective-permute-start(bf16[256,352]{0,1:T(8,128)(2,1)S(1)} %copy.180), channel_id=1, source_target_pairs={{0,16},{8,24},{16,0},{1,17},{9,25},{17,1},{2,18},{10,26},{18,2},{3... | collective-permute-start | bytes 540680 | tf_op jit(solution)/shard_map/ppermute | solution.py:207
  592.5 184.4 %collective-permute-start.49 = (bf16[256,352]{0,1:T(8,128)(2,1)S(1)}, bf16[256,352]{0,1:T(8,128)(2,1)S(1)}, u32[]{:S(2)}, u32[]{:S(2)}) collective-permute-start(bf16[256,352]{0,1:T(8,128)(2,1)S(1)} %copy.181), channel_id=1, source_target_pairs={{0,20},{8,28},{16,4},{1,21},{9,29},{17,5},{2,22},{10,30},{18,6},{3... | collective-permute-start | bytes 540680 | tf_op jit(solution)/shard_map/ppermute | solution.py:207
  593.9 186.8 %copy-start.4 = (f32[3,256,352]{1,2,0:T(8,128)S(1)}, f32[3,256,352]{1,2,0:T(8,128)}, u32[]{:S(2)}) copy-start(f32[3,256,352]{1,2,0:T(8,128)} %copy-done.3) | copy-start | bytes 3244036
  764.7 12.1 %collective-permute-start.50 = (bf16[256,352]{0,1:T(8,128)(2,1)S(1)}, bf16[256,352]{0,1:T(8,128)(2,1)S(1)}, u32[]{:S(2)}, u32[]{:S(2)}) collective-permute-start(bf16[256,352]{0,1:T(8,128)(2,1)S(1)} %copy.182), channel_id=1, source_target_pairs={{0,24},{8,0},{16,8},{1,25},{9,1},{17,9},{2,26},{10,2},{18,10},{3,2... | collective-permute-start | bytes 540680 | tf_op jit(solution)/shard_map/ppermute | solution.py:207
  766.3 14.3 %collective-permute-start.51 = (bf16[256,352]{0,1:T(8,128)(2,1)S(1)}, bf16[256,352]{0,1:T(8,128)(2,1)S(1)}, u32[]{:S(2)}, u32[]{:S(2)}) collective-permute-start(bf16[256,352]{0,1:T(8,128)(2,1)S(1)} %copy.183), channel_id=1, source_target_pairs={{0,28},{8,4},{16,12},{1,29},{9,5},{17,13},{2,30},{10,6},{18,14},{3... | collective-permute-start | bytes 540680 | tf_op jit(solution)/shard_map/ppermute | solution.py:207
  (48 other events, 549.9 us)
Sparse Core Ops, SparseCore 0:
  10.2 33.3 all-gather.11
  57.9 28.1 all-gather.9
  87.7 28.5 all-gather.13
  242.5 29.3 all-gather.15
  276.7 47.6 all-gather.17

commit v2 on v1

v2 whole, which is shorter than its diff:
```python
import functools
import math

import jax
import jax.numpy as jnp
from jax import lax
from jax.experimental import pallas as pl
from jax.experimental.pallas import tpu as pltpu
from jax.sharding import PartitionSpec as P

HEAD_DIM = 64
NS_STEPS = 5
STEP = 10

norm_eps = 1e-06
rope_base = 1000000.0
coef_a = 3.4445
coef_b = -4.775
coef_c = 2.0315
momentum_decay = 0.95
matrix_rate = 0.5
decay_rate = 0.01
first_decay = 0.9
second_decay = 0.95
vector_rate = 0.25
adam_eps = 1e-08
ortho_eps = 1e-07
masked_score = -1e30
tile = 256

MLP_OWNERS = (0, 2, 4)
ATTN_OWNERS = (1, 3, 5, 6)

f32 = jnp.float32
bf16 = jnp.bfloat16


def dot32(a, b, ca, cb):
    return lax.dot_general(a, b, (((ca,), (cb,)), ((), ())), preferred_element_type=f32)


def doc_layout(bounds, length):
    places = jnp.arange(length, dtype=jnp.int32)
    first_bound = bounds[0]
    second_bound = bounds[1]
    doc_index = (places >= first_bound).astype(jnp.int32) + (places >= second_bound).astype(
        jnp.int32
    )
    doc_start = jnp.where(
        places < first_bound, 0, jnp.where(places < second_bound, first_bound, second_bound)
    )
    return (doc_index, (places - doc_start).astype(f32))


def rope_tables(position, cols):
    half_dim = HEAD_DIM // 2
    lane = jnp.arange(cols, dtype=jnp.int32) % HEAD_DIM
    frequency = rope_base ** (-2.0 * jnp.arange(half_dim, dtype=f32) / HEAD_DIM)
    angles = position[:, None] * frequency[None, :]
    repeat = cols // half_dim
    cosine = jnp.concatenate([jnp.cos(angles)] * repeat, 1)
    sine = jnp.concatenate([jnp.sin(angles)] * repeat, 1)
    return cosine, jnp.where(lane < half_dim, -1.0, 1.0)[None, :] * sine


def swap_halves(values):
    half_dim = HEAD_DIM // 2
    parts = []
    for first in range(0, values.shape[1], HEAD_DIM):
        parts.append(values[:, first + half_dim : first + HEAD_DIM])
        parts.append(values[:, first : first + half_dim])
    return jnp.concatenate(parts, axis=1)


def visible(bounds_ref, first, rows, length):
    query = first + lax.broadcasted_iota(jnp.int32, (rows, length), 0)
    key = lax.broadcasted_iota(jnp.int32, (rows, length), 1)
    one, two = bounds_ref[0, 0], bounds_ref[0, 1]
    start = jnp.where(query < one, 0, jnp.where(query < two, one, two))
    return (key <= query) & (key >= start)


def front_kernel(
    bounds_ref,
    place_ref,
    same_ref,
    other_ref,
    weight_ref,
    gain_ref,
    bias_ref,
    cosine_ref,
    sine_ref,
    x_ref,
    normed_ref,
    query_ref,
    key_ref,
    value_ref,
    attended_ref,
    log_ref,
):
    length = x_ref.shape[0]
    cols = query_ref.shape[1]
    chips, rows, _ = same_ref.shape
    for chip in range(chips):
        at = pl.ds(chip * 2 * rows, 2 * rows)
        slot = place_ref[0] ^ chip
        low = pl.ds(chip * 2 * rows + place_ref[1] * rows, rows)
        high = pl.ds(chip * 2 * rows + (1 - place_ref[1]) * rows, rows)
        x_ref[low, :] = same_ref[slot]
        x_ref[high, :] = other_ref[slot]
        x = x_ref[at, :].astype(f32)
        inverse = lax.rsqrt(jnp.mean(x * x, axis=-1, keepdims=True) + norm_eps)
        normed = (x * inverse * gain_ref[...]).astype(bf16)
        normed_ref[at, :] = normed
        projected = (dot32(normed, weight_ref[...], 1, 0) + bias_ref[...]).astype(bf16).astype(f32)
        cosine, sine = cosine_ref[at, :], sine_ref[at, :]
        query = projected[:, :cols]
        key = projected[:, cols : 2 * cols]
        query_ref[at, :] = (query * cosine + swap_halves(query) * sine).astype(bf16)
        key_ref[at, :] = (key * cosine + swap_halves(key) * sine).astype(bf16)
        value_ref[at, :] = projected[:, 2 * cols :].astype(bf16)
    for first in range(0, length, tile):
        at, keys = pl.ds(first, tile), pl.ds(0, first + tile)
        allowed = visible(bounds_ref, first, tile, first + tile)
        attended = []
        for head in range(cols // HEAD_DIM):
            lanes = pl.ds(head * HEAD_DIM, HEAD_DIM)
            scores = dot32(query_ref[at, lanes], key_ref[keys, lanes], 1, 1)
            scores = jnp.where(allowed, scores * HEAD_DIM ** (-0.5), masked_score)
            peak = jnp.max(scores, axis=-1, keepdims=True)
            exponent = jnp.exp(scores - peak)
            total = jnp.sum(exponent, axis=-1, keepdims=True)
            weights = (exponent * (1.0 / total)).astype(bf16)
            attended.append(dot32(weights, value_ref[keys, lanes], 1, 0))
            log_ref[at, pl.ds(head, 1)] = peak + jnp.log(total)
        attended_ref[at, :] = jnp.concatenate(attended, axis=1).astype(bf16)


def vmem_specs(count):
    return [pl.BlockSpec(memory_space=pltpu.VMEM)] * count


def whole_spec(shape):
    return pl.BlockSpec(shape, lambda i: (0,) * len(shape))


def whole_specs(arrays):
    return [whole_spec(value.shape) for value in arrays]


def any_specs(count):
    return [pl.BlockSpec(memory_space=pl.ANY)] * count


def smem_spec():
    return pl.BlockSpec(memory_space=pltpu.SMEM)


def front(bounds, place, same, other, weight, gain, bias, cosine, sine):
    chips, rows, width = same.shape
    length, cols = cosine.shape
    part = jax.ShapeDtypeStruct((length, cols), bf16)
    shapes = [
        jax.ShapeDtypeStruct((length, width), bf16),
        jax.ShapeDtypeStruct((length, width), bf16),
        part,
        part,
        part,
        part,
        jax.ShapeDtypeStruct((length, cols // HEAD_DIM), f32),
    ]
    args = (same, other, weight, gain, bias, cosine, sine)
    return pl.pallas_call(
        front_kernel,
        grid=(1,),
        in_specs=[smem_spec()] * 2 + whole_specs(args),
        out_specs=whole_specs(shapes),
        out_shape=shapes,
        compiler_params=pltpu.CompilerParams(vmem_limit_bytes=56 * 2**20),
        cost_estimate=pl.CostEstimate(
            flops=8 * 10**9, bytes_accessed=8 * 10**6, transcendentals=2 * 10**6
        ),
        name="front",
    )(bounds, place, *args)


def store_split(place_ref, mine_ref, other_ref, index, value):
    chips, _, rows, _ = mine_ref.shape
    core = place_ref[1]
    for at in range(chips):
        slot = at ^ (place_ref[0] & (chips - 1))
        top = value[2 * at * rows : (2 * at + 1) * rows]
        low = value[(2 * at + 1) * rows : (2 * at + 2) * rows]
        mine_ref[slot, index] = jnp.where(core == 0, top, low)
        other_ref[slot, index] = jnp.where(core == 0, low, top).astype(bf16)


def split_out(chips, step, sums, rows, width):
    spec = pl.BlockSpec(
        (step, sums, rows, width), lambda i, place: (i ^ (place[0] // step), 0, 0, 0)
    )
    shape = (chips, sums, rows, width)
    return [spec, spec], [jax.ShapeDtypeStruct(shape, f32), jax.ShapeDtypeStruct(shape, bf16)]


def middle_kernel(
    place_ref,
    attended_ref,
    x_ref,
    dy_ref,
    weight_ref,
    gain_ref,
    normed_ref,
    d_gate_ref,
    d_up_ref,
    hidden_ref,
    d_mine_ref,
    d_other_ref,
    resid_ref,
):
    width = x_ref.shape[1]
    cols = d_gate_ref.shape[1]
    count = attended_ref.shape[0]
    chips, _, rows, _ = d_mine_ref.shape
    gate_w = weight_ref.at[:, pl.ds(width, cols)]
    up_w = weight_ref.at[:, pl.ds(width + cols, cols)]
    down_w = weight_ref.at[:, pl.ds(width + 2 * cols, cols)]
    attended = jnp.concatenate([attended_ref[part] for part in range(count)], axis=1)
    resid = x_ref[...].astype(f32) + dot32(attended, weight_ref[:, pl.ds(0, width)], 1, 0)
    for at in range(2 * chips):

        @pl.when(pl.program_id(0) * 2 * chips + at == place_ref[0] * 2 + place_ref[1])
        def _():
            resid_ref[...] = resid[at * rows : (at + 1) * rows]

    inverse = lax.rsqrt(jnp.mean(resid * resid, axis=-1, keepdims=True) + norm_eps)
    normed = (resid * inverse * gain_ref[...]).astype(bf16)
    normed_ref[...] = normed
    gate = dot32(normed, gate_w[...], 1, 0)
    up = dot32(normed, up_w[...], 1, 0)
    d_hidden = dot32(dy_ref[...], down_w[...], 1, 0)
    sigmoid = jax.nn.sigmoid(gate)
    silu = gate * sigmoid
    hidden = (silu * up).astype(bf16)
    hidden_ref[...] = hidden
    d_gate = (d_hidden * up * (sigmoid * (1.0 + gate * (1.0 - sigmoid)))).astype(bf16)
    d_up = (d_hidden * silu).astype(bf16)
    d_gate_ref[...] = d_gate
    d_up_ref[...] = d_up
    d_normed = dot32(d_gate, gate_w[...], 1, 1) + dot32(d_up, up_w[...], 1, 1)
    store_split(place_ref, d_mine_ref, d_other_ref, 0, d_normed)


def middle(place, attended, x, dy, weight, gain):
    count, length, head_cols = attended.shape
    width = x.shape[1]
    cols = (weight.shape[1] - width) // 3
    chips = count // 2
    half = length // count
    step = 1
    rows = step * 2 * half

    def block(size):
        return pl.BlockSpec((rows, size), lambda i, place: (i, 0))

    def whole(shape):
        return pl.BlockSpec(shape, lambda i, place: (0,) * len(shape))

    split_specs, split_shapes = split_out(chips, step, 1, half, width)
    wide = jax.ShapeDtypeStruct((length, cols), bf16)
    return pl.pallas_call(
        middle_kernel,
        grid_spec=pltpu.PrefetchScalarGridSpec(
            num_scalar_prefetch=1,
            grid=(chips // step,),
            in_specs=[
                pl.BlockSpec((count, rows, head_cols), lambda i, place: (0, i, 0)),
                block(width),
                block(width),
                whole(weight.shape),
                whole(gain.shape),
            ],
            out_specs=[
                block(width),
                block(cols),
                block(cols),
                block(cols),
                *split_specs,
                whole((half, width)),
            ],
        ),
        out_shape=[
            jax.ShapeDtypeStruct((length, width), bf16),
            wide,
            wide,
            wide,
            *split_shapes,
            jax.ShapeDtypeStruct((half, width), f32),
        ],
        compiler_params=pltpu.CompilerParams(vmem_limit_bytes=56 * 2**20),
        cost_estimate=pl.CostEstimate(
            flops=10 * 10**9, bytes_accessed=20 * 10**6, transcendentals=10**6
        ),
        name="middle",
    )(place, attended, x, dy, weight, gain)


def pair_kernel(mine_ref, got_ref, *outs):
    outs[0][...] = mine_ref[0] + got_ref[0].astype(f32)
    for slot in range(1, len(outs)):
        outs[slot][...] = (mine_ref[slot] + got_ref[slot].astype(f32)).astype(bf16)


def pair_sums(mine, got):
    chips = mine.shape[0]
    shapes = [jax.ShapeDtypeStruct(mine.shape[1:], f32)]
    shapes += [jax.ShapeDtypeStruct(mine.shape[1:], bf16)] * (chips - 1)
    return pl.pallas_call(
        pair_kernel,
        grid=(1,),
        in_specs=whole_specs((mine, got)),
        out_specs=whole_specs(shapes),
        out_shape=shapes,
        compiler_params=pltpu.CompilerParams(vmem_limit_bytes=48 * 2**20),
        name="pair_sums",
    )(mine, got)


def post_kernel(
    own_ref, resid_ref, dy_ref, gain_ref, weight_ref, *refs
):
    arrived, (pair_ref, d_resid_ref, gain_part_ref) = refs[:-3], refs[-3:]
    d_normed = own_ref[0]
    for ref in arrived:
        d_normed = d_normed + ref[0].astype(f32)
    resid = resid_ref[...]
    inverse = lax.rsqrt(jnp.mean(resid * resid, axis=-1, keepdims=True) + norm_eps)
    scaled = d_normed * gain_ref[...]
    gain_part_ref[...] = jnp.sum(d_normed * resid * inverse, axis=0, keepdims=True)
    d_resid = (
        dy_ref[...].astype(f32)
        + inverse * scaled
        - resid * (inverse * inverse * inverse) * jnp.mean(scaled * resid, axis=-1, keepdims=True)
    )
    d_resid_ref[...] = d_resid
    low = d_resid.astype(bf16)
    d_attn = dot32(low, weight_ref[...], 1, 1).astype(bf16)
    cols = pair_ref.shape[3]
    for part in range(pair_ref.shape[0]):
        pair_ref[part, 0] = d_attn[:, part * cols : (part + 1) * cols]
        pair_ref[part, 1] = low[:, part * cols : (part + 1) * cols]


def post(own, arrived, resid, dy, gain, weight, count):
    rows, width = resid.shape
    cols = width // count

    def whole(shape):
        return pl.BlockSpec(shape, lambda i: (0,) * len(shape))

    return pl.pallas_call(
        post_kernel,
        grid=(1,),
        in_specs=[whole(own.shape), whole(resid.shape), whole(dy.shape), whole(gain.shape)]
        + [whole((width, width))]
        + [whole(value.shape) for value in arrived],
        out_specs=[whole((count, 2, rows, cols)), whole((rows, width)), whole((1, width))],
        out_shape=[
            jax.ShapeDtypeStruct((count, 2, rows, cols), bf16),
            jax.ShapeDtypeStruct((rows, width), f32),
            jax.ShapeDtypeStruct((1, width), f32),
        ],
        compiler_params=pltpu.CompilerParams(vmem_limit_bytes=40 * 2**20),
        name="post",
    )(own, resid, dy, gain, weight, *arrived)


def mlp_grads_kernel(parts, control_ref, normed_ref, dy_ref, d_gate_ref, d_up_ref, hidden_ref, *outs):
    shard = outs[0].shape[1]
    for part in range(parts):
        at = pl.ds(pl.multiple_of((control_ref[2] ^ part) * shard, 128), shard)
        normed = normed_ref[:, at]
        outs[part][0] = dot32(normed, d_gate_ref[...], 0, 0).astype(bf16)
        outs[part][1] = dot32(normed, d_up_ref[...], 0, 0).astype(bf16)
        outs[part][2] = dot32(dy_ref[:, at], hidden_ref[...], 0, 0).astype(bf16)


def mlp_grads(control, normed, dy, d_gate, d_up, hidden, parts):
    length, width = normed.shape
    cols = hidden.shape[1]
    args = (normed, dy, d_gate, d_up, hidden)
    shapes = [jax.ShapeDtypeStruct((3, width // parts, cols), bf16)] * parts
    return pl.pallas_call(
        functools.partial(mlp_grads_kernel, parts),
        grid=(1,),
        in_specs=[smem_spec()] + whole_specs(args),
        out_specs=whole_specs(shapes),
        out_shape=shapes,
        compiler_params=pltpu.CompilerParams(vmem_limit_bytes=56 * 2**20),
        cost_estimate=pl.CostEstimate(
            flops=3 * 10**9, bytes_accessed=9 * 10**6, transcendentals=0
        ),
        name="mlp_grads",
    )(control, *args)


def back_kernel(
    parts,
    bounds_ref,
    control_ref,
    query_ref,
    key_ref,
    value_ref,
    log_ref,
    arrived_ref,
    normed_ref,
    attended_ref,
    cosine_ref,
    sine_ref,
    d_qkv_ref,
    bias_ref,
    *refs,
):
    grads_refs, (d_key_ref, d_value_ref, d_attn_ref, d_resid_ref) = refs[:parts], refs[parts:]
    length, cols = query_ref.shape
    count, _, rows, _ = arrived_ref.shape
    scale = HEAD_DIM ** (-0.5)
    for part in range(count):
        d_attn_ref[pl.ds(part * rows, rows), :] = arrived_ref[part, 0]
        d_resid_ref[pl.ds(part * rows, rows), :] = arrived_ref[part, 1]
    d_key_ref[...] = jnp.zeros_like(d_key_ref)
    d_value_ref[...] = jnp.zeros_like(d_value_ref)

    def undo(values, at):
        return values * cosine_ref[at, :] - swap_halves(values) * sine_ref[at, :]

    for first in range(0, length, tile):
        at, keys = pl.ds(first, tile), pl.ds(0, first + tile)
        allowed = visible(bounds_ref, first, tile, first + tile)
        d_query, d_key, d_value = [], [], []
        for head in range(cols // HEAD_DIM):
            lanes = pl.ds(head * HEAD_DIM, HEAD_DIM)
            query, d_out = query_ref[at, lanes], d_attn_ref[at, lanes]
            key, value = key_ref[keys, lanes], value_ref[keys, lanes]
            scores = jnp.where(allowed, dot32(query, key, 1, 1) * scale, masked_score)
            weights = jnp.exp(scores - log_ref[at, pl.ds(head, 1)])
            d_value.append(dot32(weights.astype(bf16), d_out, 0, 0))
            d_weights = dot32(d_out, value, 1, 1)
            inner = jnp.sum(weights * d_weights, axis=-1, keepdims=True)
            d_scores = (weights * (d_weights - inner)).astype(bf16)
            d_query.append(dot32(d_scores, key, 1, 0) * scale)
            d_key.append(dot32(d_scores, query, 0, 0) * scale)
        d_key_ref[keys, :] += jnp.concatenate(d_key, axis=1)
        d_value_ref[keys, :] += jnp.concatenate(d_value, axis=1)
        d_qkv_ref[at, pl.ds(0, cols)] = undo(jnp.concatenate(d_query, axis=1), at).astype(bf16)
    for first in range(0, length, tile):
        at = pl.ds(first, tile)
        d_qkv_ref[at, pl.ds(cols, cols)] = undo(d_key_ref[at, :], at).astype(bf16)
        d_qkv_ref[at, pl.ds(2 * cols, cols)] = d_value_ref[at, :].astype(bf16)
    bias_ref[...] = jnp.sum(d_qkv_ref[...].astype(f32), axis=0, keepdims=True)
    shard, pad = grads_refs[0].shape[1:]
    for part in range(parts):
        block = control_ref[2] ^ part
        grads_ref = grads_refs[part]
        at = pl.ds(pl.multiple_of(block * shard, 128), shard)
        grads = dot32(normed_ref[:, at], d_qkv_ref[...], 0, 0).astype(bf16)
        for index in range(3):
            grads_ref[index, :, pl.ds(0, cols)] = grads[:, index * cols : (index + 1) * cols]
        for piece in range(shard // cols):
            grads_ref[3, pl.ds(piece * cols, cols), pl.ds(0, cols)] = dot32(
                attended_ref[block * (shard // cols) + piece], d_resid_ref[...], 0, 0
            ).astype(bf16)
        if pad > cols:
            grads_ref[:, :, pl.ds(cols, pad - cols)] = jnp.zeros((4, shard, pad - cols), bf16)


def back(bounds, control, query, key, value, log_total, arrived, normed, attended, cosine, sine, parts):
    length, cols = query.shape
    width = normed.shape[1]
    pad = -(-cols // 128) * 128
    args = (query, key, value, log_total, arrived, normed, attended, cosine, sine)
    shapes = [
        jax.ShapeDtypeStruct((length, 3 * cols), bf16),
        jax.ShapeDtypeStruct((1, 3 * cols), f32),
    ]
    shapes += [jax.ShapeDtypeStruct((4, width // parts, pad), bf16)] * parts
    results = pl.pallas_call(
        functools.partial(back_kernel, parts),
        grid=(1,),
        in_specs=[smem_spec()] * 2 + whole_specs(args),
        out_specs=whole_specs(shapes),
        out_shape=shapes,
        scratch_shapes=[
            pltpu.VMEM((length, cols), f32),
            pltpu.VMEM((length, cols), f32),
            pltpu.VMEM((length, cols), bf16),
            pltpu.VMEM((length, cols), bf16),
        ],
        compiler_params=pltpu.CompilerParams(vmem_limit_bytes=48 * 2**20),
        cost_estimate=pl.CostEstimate(
            flops=10 * 10**9, bytes_accessed=8 * 10**6, transcendentals=2 * 10**6
        ),
        name="back",
    )(bounds, control, *args)
    return results[0], results[1], results[2:]


def late_kernel(place_ref, hidden_ref, down_ref, d_qkv_ref, weight_ref, mine_ref, other_ref):
    store_split(place_ref, mine_ref, other_ref, 0, dot32(hidden_ref[...], down_ref[...], 1, 1))
    store_split(place_ref, mine_ref, other_ref, 1, dot32(d_qkv_ref[...], weight_ref[...], 1, 1))


def late_sums(place, hidden, wide_w, d_qkv, weight, count):
    length, cols = d_qkv.shape
    width = weight.shape[0]
    pad = hidden.shape[1]
    down = wide_w[:, wide_w.shape[1] - pad :]
    chips = count // 2
    half = length // count
    step = 2
    rows = step * 2 * half
    split_specs, split_shapes = split_out(chips, step, 2, half, width)
    return pl.pallas_call(
        late_kernel,
        grid_spec=pltpu.PrefetchScalarGridSpec(
            num_scalar_prefetch=1,
            grid=(chips // step,),
            in_specs=[
                pl.BlockSpec((rows, pad), lambda i, place: (i, 0)),
                pl.BlockSpec(down.shape, lambda i, place: (0, 0)),
                pl.BlockSpec((rows, cols), lambda i, place: (i, 0)),
                pl.BlockSpec(weight.shape, lambda i, place: (0, 0)),
            ],
            out_specs=split_specs,
        ),
        out_shape=split_shapes,
        compiler_params=pltpu.CompilerParams(vmem_limit_bytes=48 * 2**20),
        cost_estimate=pl.CostEstimate(
            flops=2 * 10**9, bytes_accessed=16 * 10**6, transcendentals=0
        ),
        name="late_sums",
    )(place, hidden, down, d_qkv, weight)


def picked_kernel(pick_ref, momentum_ref, out_ref):
    count, rows, pad = out_ref.shape
    cols = momentum_ref.shape[2] // count
    for turn in range(count):
        value = momentum_ref[0, :, pl.ds(turn * cols, cols)] * momentum_decay
        out_ref[turn, :, pl.ds(0, cols)] = value
        if pad > cols:
            out_ref[turn, :, pl.ds(cols, pad - cols)] = jnp.zeros((rows, pad - cols), f32)


def picked(momentum, pick, count):
    rows, width = momentum.shape[1:]
    pad = -(-(width // count) // 128) * 128
    step = min(64, rows)
    return pl.pallas_call(
        picked_kernel,
        grid_spec=pltpu.PrefetchScalarGridSpec(
            num_scalar_prefetch=1,
            grid=(rows // step,),
            in_specs=[pl.BlockSpec((1, step, width), lambda i, pick: (pick[0], i, 0))],
            out_specs=pl.BlockSpec((count, step, pad), lambda i, pick: (0, i, 0)),
        ),
        out_shape=jax.ShapeDtypeStruct((count, rows, pad), f32),
        compiler_params=pltpu.CompilerParams(vmem_limit_bytes=40 * 2**20),
        cost_estimate=pl.CostEstimate(
            flops=rows * width, bytes_accessed=8 * rows * width, transcendentals=0
        ),
        name="picked",
    )(pick, momentum)


def squares_kernel(order_ref, attn_ref, mlp_ref, out_ref):
    @pl.when(pl.program_id(0) == 0)
    def _():
        out_ref[...] = jnp.zeros_like(out_ref)

    at = 0
    for ref in (attn_ref, mlp_ref):
        for index in range(ref.shape[0]):
            value = ref[index].astype(bf16).astype(f32)
            total = jnp.sum(jnp.sum(value * value, axis=0, keepdims=True), axis=1, keepdims=True)
            out_ref[pl.ds(at, 1), :] += jnp.broadcast_to(total, (1, out_ref.shape[1]))
            at += 1


def sums_of_squares(order, attn, mlp):
    rows = attn.shape[1]
    step = min(64, rows)
    return pl.pallas_call(
        squares_kernel,
        grid=(rows // step,),
        in_specs=[
            smem_spec(),
            pl.BlockSpec((attn.shape[0], step, attn.shape[2]), lambda i: (0, i, 0)),
            pl.BlockSpec((mlp.shape[0], step, mlp.shape[2]), lambda i: (0, i, 0)),
        ],
        out_specs=pl.BlockSpec((8, 128), lambda i: (0, 0)),
        out_shape=jax.ShapeDtypeStruct((8, 128), f32),
        compiler_params=pltpu.CompilerParams(vmem_limit_bytes=40 * 2**20),
        cost_estimate=pl.CostEstimate(
            flops=2 * (attn.size + mlp.size),
            bytes_accessed=4 * (attn.size + mlp.size),
            transcendentals=0,
        ),
        name="sums_of_squares",
    )(order, attn, mlp)


def assemble_kernel(places, wt_ref, *refs):
    pieces, out_ref, arrived = refs[: len(places)], refs[-2], refs[-1]
    copies = []
    for at, (bits, first, rows) in enumerate(places):
        start = pl.multiple_of((wt_ref[0] ^ bits) * rows + first, 16)
        target = out_ref.at[pl.ds(start, pieces[at].shape[0]), :]
        copies.append(pltpu.make_async_copy(pieces[at], target, arrived.at[at]))
    for copy in copies:
        copy.start()
    for copy in copies:
        copy.wait()


def assemble(wt_index, pieces, places, rows):
    size = rows * pieces[0].shape[1]
    return pl.pallas_call(
        functools.partial(assemble_kernel, places),
        in_specs=[smem_spec()] + any_specs(len(pieces)),
        out_specs=vmem_specs(1)[0],
        out_shape=jax.ShapeDtypeStruct((rows, pieces[0].shape[1]), pieces[0].dtype),
        scratch_shapes=[pltpu.SemaphoreType.DMA((len(pieces),))],
        compiler_params=pltpu.CompilerParams(vmem_limit_bytes=24 * 2**20),
        cost_estimate=pl.CostEstimate(flops=0, bytes_accessed=4 * size, transcendentals=0),
        name="assemble",
    )(wt_index.reshape(1), *pieces)


def norm_backward(d_normed, values, inverse, gain_row):
    scaled = d_normed * gain_row
    gain_part = jnp.sum(d_normed * values * inverse, axis=0)
    d_values = inverse * scaled - values * inverse**3 * jnp.mean(
        scaled * values, axis=-1, keepdims=True
    )
    return (d_values, gain_part)


def ortho_kernel(parts, count, extra, control_ref, *refs):
    blocks = refs[:parts]
    refs = refs[extra:]
    outs = refs[parts : parts + count]
    whole, gram, prod, gram_low, prod_low, poly_low, rows, arrived = refs[parts + count :]
    shard, pad = outs[0].shape
    width = gram.shape[0]
    tiles = width // tile

    def upper(j):
        return pl.ds(0, (j + 1) * tile), pl.ds(j * tile, tile)

    def mirror(low):
        for j in range(1, tiles):
            for i in range(j):
                here, there = pl.ds(i * tile, tile), pl.ds(j * tile, tile)
                low[there, here] = low[here, there].T

    @pl.when(control_ref[0] == 1)
    def _():
        copies = [
            [
                pltpu.make_async_copy(
                    blocks[part].at[turn],
                    whole.at[pl.ds(part * shard, shard), pl.ds(turn * pad, pad)],
                    arrived.at[part, turn],
                )
                for turn in range(count)
            ]
            for part in range(parts)
        ]
        for part in range(parts):
            for copy in copies[part]:
                copy.start()
        diagonal = lax.broadcasted_iota(jnp.int32, (tile, tile), 0) == lax.broadcasted_iota(
            jnp.int32, (tile, tile), 1
        )
        squares = jnp.zeros((1, 1), f32)
        for j in range(tiles):
            for part in range(j * tile // shard, (j + 1) * tile // shard):
                for copy in copies[part]:
                    copy.wait()
            up, at = upper(j)
            gram[up, at] = dot32(whole[up, :], whole[at, :], 1, 1)
            entries = jnp.where(diagonal, gram[at, at], 0.0)
            squares = squares + jnp.sum(
                jnp.sum(entries, axis=1, keepdims=True), axis=0, keepdims=True
            )
        inverse = 1.0 / (jnp.sqrt(squares) + ortho_eps)
        for j in range(tiles):
            up, at = upper(j)
            scaled = gram[up, at] * (inverse * inverse)
            gram[up, at] = scaled
            gram_low[up, at] = scaled.astype(bf16)
        mirror(gram_low)

        def step(index, carry):
            poly = poly_low.at[index]
            for j in range(tiles):
                up, at = upper(j)
                poly[up, at] = (
                    coef_b * gram[up, at] + coef_c * dot32(gram_low[up, :], gram_low[:, at], 1, 0)
                ).astype(bf16)
            mirror(poly)
            for j in range(tiles):
                up, at = upper(j)
                value = coef_a * gram[up, at] + dot32(poly[up, :], gram_low[:, at], 1, 0)
                prod[up, at] = value
                prod_low[up, at] = value.astype(bf16)
            mirror(prod_low)
            for j in range(tiles):
                up, at = upper(j)
                value = coef_a * prod[up, at] + dot32(prod_low[up, :], poly[:, at], 1, 0)
                gram[up, at] = value
                gram_low[up, at] = value.astype(bf16)
            mirror(gram_low)
            return carry

        lax.fori_loop(0, NS_STEPS - 1, step, 0)
        unit = lax.broadcasted_iota(jnp.int32, (shard, width), 0) == lax.broadcasted_iota(
            jnp.int32, (shard, width), 1
        )
        rows[...] = (
            coef_a * unit.astype(f32)
            + coef_b * gram[pl.ds(0, shard), :]
            + coef_c * dot32(gram_low[pl.ds(0, shard), :], gram_low[...], 1, 0)
        )

        def apply(index, carry):
            value = rows[...]
            rows[...] = coef_a * value + dot32(
                value.astype(bf16), poly_low[NS_STEPS - 2 - index], 1, 0
            )
            return carry

        lax.fori_loop(0, NS_STEPS - 1, apply, 0)
        scaled = (rows[...] * inverse).astype(bf16)
        for turn in range(count):
            place = lax.rem(control_ref[1] + turn, count)
            lanes = pl.ds(pl.multiple_of(place * pad, 128), pad)
            outs[turn][...] = dot32(scaled, whole[:, lanes], 1, 0).astype(bf16)


def orthogonalize(control, blocks, after):
    count, shard, pad = blocks[0].shape
    parts = len(blocks)
    width = shard * parts
    return pl.pallas_call(
        functools.partial(ortho_kernel, parts, count, len(after)),
        out_shape=[jax.ShapeDtypeStruct((shard, pad), bf16)] * count,
        in_specs=[smem_spec()] + any_specs(parts + len(after)),
        out_specs=vmem_specs(count),
        scratch_shapes=[
            pltpu.VMEM((width, count * pad), bf16),
            pltpu.VMEM((width, width), f32),
            pltpu.VMEM((width, width), f32),
            pltpu.VMEM((width, width), bf16),
            pltpu.VMEM((width, width), bf16),
            pltpu.VMEM((NS_STEPS - 1, width, width), bf16),
            pltpu.VMEM((shard, width), f32),
            pltpu.SemaphoreType.DMA((parts, count)),
        ],
        compiler_params=pltpu.CompilerParams(vmem_limit_bytes=56 * 2**20),
        cost_estimate=pl.CostEstimate(
            flops=30 * 10**9, bytes_accessed=4 * count * shard * pad, transcendentals=0
        ),
        name="orthogonalize",
    )(control, *blocks, *after)


def update_kernel(owners, control_ref, rate_ref, own_ref, *refs):
    arrived, out_ref = refs[:-1], refs[-1]
    count, cols = len(arrived), own_ref.shape[2]
    for index, owner in enumerate(owners):
        turn = lax.rem(control_ref[1] - owner + count, count)
        for at in range(count):

            @pl.when(turn == at)
            def _():
                out_ref[index] = (
                    own_ref[index] * (1.0 - matrix_rate * decay_rate)
                    - rate_ref[index] * arrived[at][:, pl.ds(0, cols)].astype(f32)
                )


def update(control, rate, own, arrived, owners):
    return pl.pallas_call(
        functools.partial(update_kernel, owners),
        grid=(1,),
        in_specs=[smem_spec()] * 2 + whole_specs((own, *arrived)),
        out_specs=whole_spec(own.shape),
        out_shape=jax.ShapeDtypeStruct(own.shape, f32),
        compiler_params=pltpu.CompilerParams(vmem_limit_bytes=40 * 2**20),
        name="update",
    )(control, rate, own, *arrived)


def finish_kernel(share_ref, momentum_ref, grad_ref, new_ref):
    count, matrices = share_ref.shape[:2]
    cols = grad_ref.shape[2] // count
    for index in range(matrices):
        for turn in range(count):
            at = pl.ds(turn * cols, cols)
            grad = share_ref[turn, index].astype(f32)[:, :cols]
            grad_ref[index, :, at] = grad
            new_ref[index, :, at] = momentum_decay * momentum_ref[index, :, at] + grad


def finish(share, momentum):
    count, matrices, shard, pad = share.shape
    width = momentum.shape[2]
    step = min(64, shard)
    whole = pl.BlockSpec((matrices, step, width), lambda i: (0, i, 0))
    size = matrices * shard * width
    return pl.pallas_call(
        finish_kernel,
        grid=(shard // step,),
        in_specs=[pl.BlockSpec((count, matrices, step, pad), lambda i: (0, 0, i, 0)), whole],
        out_specs=[whole, whole],
        out_shape=[jax.ShapeDtypeStruct(momentum.shape, f32)] * 2,
        compiler_params=pltpu.CompilerParams(vmem_limit_bytes=40 * 2**20),
        cost_estimate=pl.CostEstimate(
            flops=2 * size, bytes_accessed=14 * size, transcendentals=0
        ),
        name="finish",
    )(share, momentum)


def adam_update(parameter, gradient, first_state, second_state):
    first_new = first_decay * first_state + (1.0 - first_decay) * gradient
    second_new = second_decay * second_state + (1.0 - second_decay) * gradient * gradient
    first_hat = first_new / (1.0 - first_decay**STEP)
    second_hat = second_new / (1.0 - second_decay**STEP)
    return (parameter - vector_rate * first_hat / (jnp.sqrt(second_hat) + adam_eps), second_new)


def swap(value, axis, bits, count):
    return lax.ppermute(value, axis, [(i, i ^ bits) for i in range(count)])


def sum_all(value, axis, count):
    bits = 1
    while bits < count:
        value = value + swap(value, axis, bits, count)
        bits *= 2
    return value


def near_wt(block, wt_count):
    return [swap(block, "wt", bits, wt_count) for bits in range(1, min(wt_count, 3))]


def gather_wt(block, near, wt_index, wt_count):
    rows = block.shape[0]
    pieces = [block] + near
    places = [(bits, 0, rows) for bits in range(len(pieces))]
    if wt_count == 4:
        half = rows // 2
        pieces.append(swap(near[0][:half], "wt", 2, wt_count))
        pieces.append(swap(near[1][half:], "wt", 1, wt_count))
        places += [(3, 0, rows), (3, half, rows)]
    else:
        for bits in range(3, wt_count):
            pieces.append(swap(block, "wt", bits, wt_count))
            places.append((bits, 0, rows))
    return assemble(wt_index, pieces, places, rows * wt_count)


def sum_wt(parts, wt_count):
    total = parts[0].astype(f32)
    for bits in range(1, wt_count):
        total = total + swap(parts[bits], "wt", bits, wt_count).astype(f32)
    return total.astype(bf16)


def send_chips(sums, seq_count):
    return [swap(value, "seq", 2 * bits, seq_count) for bits, value in enumerate(sums) if bits]


def gather_owned(block, owners, wt_count):
    blocks = [block]
    for bits in range(1, wt_count):
        pairs = [
            (owner * wt_count + w, owner * wt_count + (w ^ bits))
            for owner in owners
            for w in range(wt_count)
        ]
        blocks.append(lax.ppermute(block, ("seq", "wt"), pairs))
    return blocks


def spread_owned(blocks, owners, seq_count):
    return [blocks[0]] + [
        lax.ppermute(
            blocks[turn], "seq", [(owner, (owner + turn) % seq_count) for owner in owners]
        )
        for turn in range(1, seq_count)
    ]


def per_device(
    tokens,
    cotangent,
    doc_bounds,
    attn_master,
    mlp_master,
    attn_momentum,
    mlp_momentum,
    gains,
    gain_first,
    gain_second,
    qkv_bias,
    bias_first,
    bias_second,
):
    seq_count = lax.axis_size("seq")
    wt_count = lax.axis_size("wt")
    seq_index = lax.axis_index("seq")
    wt_index = lax.axis_index("wt")
    row_count = tokens.shape[1]
    width = tokens.shape[2]
    ff = mlp_master.shape[2]
    shard = attn_master.shape[1]
    length = row_count * seq_count
    head_cols = width // seq_count
    ff_cols = ff // seq_count

    place = jnp.stack([seq_index // 2, seq_index % 2])

    x_same = jnp.stack(
        [tokens[0]]
        + [swap(tokens[0], "seq", 2 * bits, seq_count) for bits in range(1, seq_count // 2)]
    )
    x_other = swap(x_same, "seq", 1, seq_count)
    dy_low = lax.all_gather(cotangent[0], "seq", axis=0, tiled=True)

    attn_own = lax.dynamic_slice_in_dim(attn_master, seq_index * head_cols, head_cols, 2)
    mlp_own = lax.dynamic_slice_in_dim(mlp_master, seq_index * ff_cols, ff_cols, 2)
    vectors = jnp.pad(jnp.concatenate([gains, qkv_bias], 0), ((0, 11), (0, 3 * head_cols - shard)))
    qkv_w = jnp.concatenate([attn_own[0], attn_own[1], attn_own[2]], 1)
    qkv_w = jnp.concatenate([qkv_w, vectors], 0).astype(bf16)
    qkv_w = lax.all_gather(qkv_w, "wt", axis=0)
    vectors = jnp.moveaxis(qkv_w[:, shard : shard + 5, :shard], 0, 1).reshape(5, width).astype(f32)
    qkv_w = qkv_w[:, :shard].reshape(width, 3 * head_cols)
    ff_pad = -(-ff_cols // 128) * 128
    wide_w = jnp.pad(mlp_own, ((0, 0), (0, 0), (0, ff_pad - ff_cols)))
    wide_w = jnp.concatenate([attn_master[3], wide_w[0], wide_w[1], wide_w[2]], 1).astype(bf16)
    wide_near = near_wt(wide_w, wt_count)
    x_other, wide_near = lax.optimization_barrier((x_other, wide_near))
    wide_w = gather_wt(wide_w, wide_near, wt_index, wt_count)

    bias_own = lax.dynamic_slice_in_dim(vectors[2:5], seq_index * head_cols, head_cols, 1)
    _, position = doc_layout(doc_bounds[0], length)
    cosine, sine = rope_tables(position, head_cols)
    x_low, normed_one, query, key, value, attended, log_total = front(
        doc_bounds,
        place,
        x_same,
        x_other,
        qkv_w,
        vectors[0:1],
        bias_own.reshape(1, 3 * head_cols),
        cosine,
        sine,
    )
    attended, dy_low = lax.optimization_barrier((attended, dy_low))
    attn_all = lax.all_gather(attended, "seq", axis=0)

    mlp_pick = jnp.minimum(seq_index // 2, 2).reshape(1)
    attn_pick = jnp.minimum(seq_index // 2, 3).reshape(1)
    mlp_pick, attn_pick, wide_w, attended = lax.optimization_barrier(
        (mlp_pick, attn_pick, wide_w, attended)
    )
    squares = sums_of_squares(mlp_pick, attn_master, mlp_master)
    mlp_old = picked(mlp_momentum, mlp_pick, seq_count)
    attn_old = picked(attn_momentum, attn_pick, seq_count)
    attn_all, squares, mlp_old, attn_old = lax.optimization_barrier(
        (attn_all, squares, mlp_old, attn_old)
    )

    normed_two, d_gate, d_up, hidden, d_mine, d_other, resid_own = middle(
        place, attn_all, x_low, dy_low, wide_w, vectors[1:2]
    )

    control = jnp.stack([jnp.zeros_like(seq_index), seq_index, wt_index])
    sums = pair_sums(d_mine, swap(d_other, "seq", 1, seq_count))
    sums, normed_two = lax.optimization_barrier((sums, normed_two))
    arrived = send_chips(sums, seq_count)
    mlp_share = sum_wt(
        mlp_grads(control, normed_two, dy_low, d_gate, d_up, hidden, wt_count), wt_count
    )
    pair, d_resid, gain_part_two = post(
        sums[0], arrived, resid_own, cotangent[0], vectors[1:2], wide_w, seq_count
    )
    pair, mlp_share = lax.optimization_barrier((pair, mlp_share))
    pair = lax.all_to_all(pair, "seq", split_axis=0, concat_axis=0)
    pair, mlp_share = lax.optimization_barrier((pair, mlp_share))
    mlp_share = lax.all_gather(mlp_share, "seq", axis=0)

    d_qkv, bias_part, attn_part = back(
        doc_bounds,
        control,
        query,
        key,
        value,
        log_total,
        pair,
        normed_one,
        attn_all,
        cosine,
        sine,
        wt_count,
    )

    def new_block(share, old, pick):
        grad = lax.dynamic_index_in_dim(share, pick[0], 1, keepdims=False).astype(f32)
        return (old + grad).astype(bf16)

    def control_of(owners):
        active = functools.reduce(jnp.logical_or, [seq_index == owner for owner in owners])
        return jnp.stack([active.astype(jnp.int32), seq_index, wt_index])

    attn_share = sum_wt(attn_part, wt_count)
    attn_share, hidden = lax.optimization_barrier((attn_share, hidden))
    attn_share = lax.all_gather(attn_share, "seq", axis=0)
    mlp_block = new_block(mlp_share, mlp_old, mlp_pick)
    mlp_gathered = gather_owned(mlp_block, MLP_OWNERS, wt_count)

    mine, other = late_sums(place, hidden, wide_w, d_qkv, qkv_w, seq_count)
    sums = pair_sums(mine, swap(other, "seq", 1, seq_count))

    mlp_grad, mlp_mom = finish(mlp_share, mlp_momentum)
    mlp_blocks = orthogonalize(control_of(MLP_OWNERS), mlp_gathered, [mlp_grad, sums[0]])

    attn_block = new_block(attn_share, attn_old, attn_pick)
    attn_block, mlp_blocks, sums = lax.optimization_barrier((attn_block, mlp_blocks, sums))
    attn_gathered = gather_owned(attn_block, ATTN_OWNERS, wt_count)
    arrived = send_chips(sums, seq_count)
    attn_grad, attn_mom = finish(attn_share, attn_momentum)
    attn_blocks = orthogonalize(control_of(ATTN_OWNERS), attn_gathered, [attn_grad])
    mlp_blocks, attn_blocks = lax.optimization_barrier((mlp_blocks, attn_blocks))

    squares = sum_all(squares, "wt", wt_count)[:, 0]
    attn_rate = matrix_rate * math.sqrt(width) * jnp.sqrt(squares[:4] / (width * width))
    mlp_rate = matrix_rate * math.sqrt(ff) * jnp.sqrt(squares[4:7] / (width * ff))
    mlp_new = update(
        control, mlp_rate, mlp_own, spread_owned(mlp_blocks, MLP_OWNERS, seq_count), MLP_OWNERS
    )
    attn_new = update(
        control,
        attn_rate,
        attn_own,
        spread_owned(attn_blocks, ATTN_OWNERS, seq_count),
        ATTN_OWNERS,
    )

    total = sums[0]
    for value in arrived:
        total = total + value.astype(f32)
    layer_out = (resid_own + total[0]).astype(bf16)
    x_own = tokens[0].astype(f32)
    inverse_own = lax.rsqrt(jnp.mean(x_own * x_own, axis=-1, keepdims=True) + norm_eps)
    d_input_norm, gain_part_one = norm_backward(total[1], x_own, inverse_own, vectors[0])
    tokens_grad = d_resid + d_input_norm

    bias_wide = lax.dynamic_update_slice(
        jnp.zeros((3, width), f32), bias_part.reshape(3, head_cols), (0, seq_index * head_cols)
    )
    small = jnp.concatenate(
        [gain_part_one[None], gain_part_two, bias_wide, jnp.zeros((3, width), f32)], 0
    )
    small = sum_all(sum_all(small, "seq", seq_count), "wt", wt_count)
    small = lax.dynamic_slice_in_dim(small, wt_index * shard, shard, 1)
    gain_grad = small[:2]
    bias_grad = small[2:5]
    gain_new, gain_second_new = adam_update(gains, gain_grad, gain_first, gain_second)
    bias_new, bias_second_new = adam_update(qkv_bias, bias_grad, bias_first, bias_second)
    return (
        layer_out[None],
        tokens_grad[None],
        attn_grad,
        mlp_grad,
        attn_mom,
        mlp_mom,
        attn_new,
        mlp_new,
        gain_grad,
        gain_second_new,
        gain_new,
        bias_grad,
        bias_second_new,
        bias_new,
    )


def solution(mesh):
    return jax.shard_map(
        per_device,
        mesh=mesh,
        in_specs=(
            P("wt", "seq", None),
            P("wt", "seq", None),
            P("wt", None),
            P(None, "wt", None),
            P(None, "wt", None),
            P(None, "wt", None),
            P(None, "wt", None),
            P(None, "wt"),
            P(None, "wt"),
            P(None, "wt"),
            P(None, "wt"),
            P(None, "wt"),
            P(None, "wt"),
        ),
        out_specs=(
            P("wt", "seq", None),
            P("wt", "seq", None),
            P(None, "wt", None),
            P(None, "wt", None),
            P(None, "wt", None),
            P(None, "wt", None),
            P(None, "wt", "seq"),
            P(None, "wt", "seq"),
            P(None, "wt"),
            P(None, "wt"),
            P(None, "wt"),
            P(None, "wt"),
            P(None, "wt"),
            P(None, "wt"),
        ),
        check_vma=False,
    )
```

time: 801 us -> 470 us (0.59)
  waiting for transfers between devices: 351 us -> 89.2 us
  matrix products: 121 us -> 0 us
  Pallas kernels: 0 us -> 116 us
  local copies, waits for them, and re-layouts: 150 us -> 52.5 us
  blocking collectives: 0 us -> 48.2 us
  other arithmetic: 66 us -> 25.4 us
  starting transfers between devices: 80.7 us -> 114 us
    ppermute x20, waiting for transfers between devices: 193 us -> 12.8 us  [the longest x14 12.8 us: spread_owned(): lax.ppermute(blocks[turn], 'seq', [(owner, (owner + turn) % seq_count) fo...]
    dot_general x28 -> x0, matrix products: 121 us -> none  [the longest x22 105 us: dot32(): lax.dot_general(a, b, (((ca,), (cb,)), ((), ())), preferred_element_type=...]
    pallas_call x0 -> x18, Pallas kernels: none -> 116 us  [the longest x2 43.1 us: orthogonalize(): pl.pallas_call(functools.partial(ortho_kernel, parts, count, len(after)),...]
    ppermute x37 -> x29, waiting for transfers between devices: 129 us -> 55 us  [swap(): return lax.ppermute(value, axis, [(i, i ^ bits) for i in range(count)])]
    ppermute x37 -> x29, starting transfers between devices: 40.1 us -> 74.1 us  [swap(): return lax.ppermute(value, axis, [(i, i ^ bits) for i in range(count)])]
    unnamed x119 -> x141, local copies, waits for them, and re-layouts: 73.2 us -> 43 us
    all_gather x0 -> x1, blocking collectives: none -> 25.6 us  [per_device(): qkv_w = lax.all_gather(qkv_w, 'wt', axis=0)]
    all_to_all x0 -> x1, blocking collectives: none -> 22.5 us  [per_device(): pair = lax.all_to_all(pair, 'seq', split_axis=0, concat_axis=0)]
  transfers between devices with their start and end apart: 63 -> 53, of which waited for: 23 -> 16; matrix products, arithmetic and copies ran while one was open for 33% -> 7% of each run, Pallas kernels for 0% -> 20%
where the time goes in v2:
time: 470 us; the launch traced here: 461 us
  Pallas kernels  116 us (25%)
  starting transfers between devices  114 us (24%)
  waiting for transfers between devices  89.2 us (19%)
  local copies, waits for them, and re-layouts  52.5 us (11%)
  blocking collectives  48.2 us (10%)
  other arithmetic  25.4 us (5%)
  between operations  15.2 us (3%)
    ppermute x29, starting transfers between devices, swap(): return lax.ppermute(value, axis, [(i, i ^ bits) for i in range(count)])  74.1 us
    ppermute x29, waiting for transfers between devices, swap(): return lax.ppermute(value, axis, [(i, i ^ bits) for i in range(count)])  55 us
    pallas_call x2, Pallas kernels, orthogonalize(): pl.pallas_call(functools.partial(ortho_kernel, parts, count, len(after)),...  43.1 us
    unnamed x141, local copies, waits for them, and re-layouts  43 us
    all_gather x1, blocking collectives, per_device(): qkv_w = lax.all_gather(qkv_w, 'wt', axis=0)  25.6 us
    ppermute x14, starting transfers between devices, spread_owned(): lax.ppermute(blocks[turn], 'seq', [(owner, (owner + turn) % seq_count) fo...  24.3 us
    all_to_all x1, blocking collectives, per_device(): pair = lax.all_to_all(pair, 'seq', split_axis=0, concat_axis=0)  22.5 us
    ppermute x6, starting transfers between devices, gather_owned(): blocks.append(lax.ppermute(block, ('seq', 'wt'), pairs))  15 us
  transfers between devices with their start and end apart: 53, of which 16 were waited for; matrix products, arithmetic and copies ran while one was open for 7% of the time, Pallas kernels for 20%

profile of v2, /device:TPU:1, one launch (start us, length us, event | category | flops | bytes accessed | tf_op | source)
XLA Modules:
  0.0 460.7 jit_solution(11721036447446105485)
XLA Ops:
  8.0 1.8 constant_dynamic-slice_fusion.1.own_ref
  12.3 2.1 collective-permute-start.4
  17.0 2.2 collective-permute-start.1
  19.3 1.9 fusion.27
  21.3 25.6 %all_gather.25 = bf16[4,272,384]{2,1,0:T(8,128)(2,1)S(1)} all-gather(bf16[1,272,384]{2,1,0:T(8,128)(2,1)S(1)} %pad_maximum_fusion.3), channel_id=1, replica_groups=mesh['seq'=8,'wt'=4] {'wt'}, dimensions={0}, use_global_device_ids=true | all-gather | bytes 1044480 | tf_op jit(solution)/shard_map/all_gather | solution.py:950
  47.9 2.2 slice.127
  52.0 2.5 collective-permute-start.3
  57.6 1.9 multiply_sine_fusion
  59.5 1.8 pad_maximum_fusion.2
  62.3 9.1 %front.1 = (bf16[1024,1024]{1,0:T(8,128)(2,1)}, bf16[1024,1024]{1,0:T(8,128)(2,1)}, bf16[1024,128]{1,0:T(8,128)(2,1)}, bf16[1024,128]{1,0:T(8,128)(2,1)}, bf16[1...) custom-call(s32[1,2]{1,0:T(1,128)} %bounds_ref.3, s32[2]{0:T(128)} %pad_add_fusion.place_ref, ...), custom_call_target="tpu_custom_call" | custom-call | flops 8000000000 | bytes 8000000 | tf_op jit(solution)/shard_map/front/pallas_call | solution.py:173
  74.8 12.1 %collective-permute-done.6.refs_3_ = bf16[128,2176]{1,0:T(8,128)(2,1)} collective-permute-done((bf16[128,2176]{1,0:T(8,128)(2,1)}, bf16[128,2176]{1,0:T(8,128)(2,1)}, u32[]{:S(2)}, u32[]{:S(2)}) %collective-permute-start.6) | collective-permute-done | bytes 557088 | tf_op jit(solution)/shard_map/ppermute | solution.py:846
  87.7 2.0 assemble.1.weight_ref
  89.8 2.1 copy-done.2
  93.1 3.5 copy-done
  98.8 3.5 copy-done.5
  102.3 3.3 sums_of_squares.1
  105.6 14.7 %middle.1 = (bf16[1024,1024]{1,0:T(8,128)(2,1)}, bf16[1024,384]{1,0:T(8,128)(2,1)}, bf16[1024,384]{1,0:T(8,128)(2,1)}, bf16[1024,384]{1,0:T(8,128)(2,1)}, f32[4,...) custom-call(s32[2]{0:T(128)} %pad_add_fusion.place_ref, ...), custom_call_target="tpu_custom_call" | custom-call | flops 10000000000 | bytes 20000000 | tf_op jit(solution)/shard_map/middle/pallas_call | solution.py:271
  122.2 1.9 collective-permute-done.8.got_ref
  124.1 1.6 copy-done.13
  128.1 7.4 %mlp_grads.1 = (bf16[3,256,384]{2,1,0:T(8,128)(2,1)}, bf16[3,256,384]{2,1,0:T(8,128)(2,1)}, bf16[3,256,384]{2,1,0:T(8,128)(2,1)}, bf16[3,256,384]{2,1,0:T(8,128)(2,1)}) custom-call(s32[3]{0:T(128)} %add_add_fusion.control_ref, bf16[1024,1024]{1,0:T(8,128)(2,1)} %get-tuple-element.152.normed_ref, bf16[1024,1024]{1,0:T(8,128)(2,1)} %bitcast.110, ...), custom_call_target="tpu_custom_call" | custom-call | flops 3000000000 | bytes 9000000 | tf_op jit(solution)/shard_map/mlp_grads/pallas_call | solution.py:393
  138.2 8.7 %collective-permute-start.10 = (bf16[1,128,1024]{2,1,0:T(8,128)(2,1)}, bf16[1,128,1024]{2,1,0:T(8,128)(2,1)S(1)}, u32[]{:S(2)}, u32[]{:S(2)}) collective-permute-start(bf16[1,128,1024]{2,1,0:T(8,128)(2,1)} %copy-done.36), channel_id=1, source_target_pairs={{0,16},{4,20},{8,24},{12,28},{16,0},{20,4},{24,8},{28,12},{1,17},{... | collective-permute-start | bytes 786440 | tf_op jit(solution)/shard_map/ppermute | solution.py:846
  148.0 15.9 %collective-permute-done.10.refs_1_ = bf16[1,128,1024]{2,1,0:T(8,128)(2,1)S(1)} collective-permute-done((bf16[1,128,1024]{2,1,0:T(8,128)(2,1)}, bf16[1,128,1024]{2,1,0:T(8,128)(2,1)S(1)}, u32[]{:S(2)}, u32[]{:S(2)}) %collective-permute-start.10) | collective-permute-done | bytes 262176 | tf_op jit(solution)/shard_map/ppermute | solution.py:846
  163.9 5.2 %collective-permute-done.9.refs_0_ = bf16[1,128,1024]{2,1,0:T(8,128)(2,1)S(1)} collective-permute-done((bf16[1,128,1024]{2,1,0:T(8,128)(2,1)S(1)}, bf16[1,128,1024]{2,1,0:T(8,128)(2,1)S(1)}, u32[]{:S(2)}, u32[]{:S(2)}) %collective-permute-start.9) | collective-permute-done | bytes 262176 | tf_op jit(solution)/shard_map/ppermute | solution.py:846
  175.1 22.5 %all_to_all.5.arrived_ref = bf16[8,2,128,128]{3,2,1,0:T(8,128)(2,1)} all-to-all(bf16[8,2,128,128]{3,2,1,0:T(8,128)(2,1)} %copy-done.25), channel_id=1, replica_groups=mesh['seq'=8,'wt'=4] {'seq'}, dimensions={0} | all-to-all | bytes 1048576 | tf_op jit(solution)/shard_map/all_to_all | solution.py:1004
  204.2 11.2 %back.1 = (bf16[1024,384]{1,0:T(8,128)(2,1)S(1)}, f32[1,384]{1,0:T(1,128)S(1)}, bf16[4,256,128]{2,1,0:T(8,128)(2,1)S(1)}, bf16[4,256,128]{2,1,0:T(8,128)(2,1)S(1...) custom-call(s32[1,2]{1,0:T(1,128)S(1)} %copy-done.34, s32[3]{0:T(128)S(1)} %copy-done.32, ...), custom_call_target="tpu_custom_call" | custom-call | flops 10000000000 | bytes 8000000 | tf_op jit(solution)/shard_map/back/pallas_call | solution.py:487
  218.9 4.6 collective-permute-done.15
  223.5 6.5 %collective-permute-done.17 = bf16[4,256,128]{2,1,0:T(8,128)(2,1)S(1)} collective-permute-done((bf16[4,256,128]{2,1,0:T(8,128)(2,1)S(1)}, bf16[4,256,128]{2,1,0:T(8,128)(2,1)S(1)}, u32[]{:S(2)}, u32[]{:S(2)}) %collective-permute-start.17) | collective-permute-done | bytes 262176 | tf_op jit(solution)/shard_map/ppermute | solution.py:846
  235.5 4.9 %late_sums.1 = (f32[4,2,128,1024]{3,2,1,0:T(8,128)}, bf16[4,2,128,1024]{3,2,1,0:T(8,128)(2,1)}) custom-call(s32[2]{0:T(128)S(1)} %copy-done.37, bf16[1024,384]{1,0:T(8,128)(2,1)S(1)} %copy-done.38, bf16[1024,384]{1,0:T(8,128)(2,1)S(1)} %slice.113.down_ref, bf16[1024,384]{1,0:T(8,128)(2,1)S(1)} %copy-done.40, bf16[1024,384]{1,0:T(8,128)(2,1)S(1)} %bitcast.99), custom_call_target="tpu_custom_call" | custom-call | flops 2000000000 | bytes 16000000 | tf_op jit(solution)/shard_map/late_sums/pallas_call | solution.py:523
  240.5 1.6 collective-permute-start.21
  242.1 6.1 %all-gather.15.cloned.1.call-done = bf16[24,256,384]{2,1,0:T(8,128)(2,1)} async-done(((bf16[3,256,384]{2,1,0:T(8,128)(2,1)}), bf16[24,256,384]{2,1,0:T(8,128)(2,1)}) %all-gather.15.cloned.1.call-update) | async-done | bytes 4718608 | tf_op jit(solution)/shard_map/all_gather | solution.py:1006
  248.2 2.9 fusion.refs_0_
  251.9 1.8 collective-permute-start.19
  253.7 1.8 collective-permute-start.20
  258.4 4.2 pair_sums.3
  263.6 14.4 %all-gather.13.cloned.1.call-done = bf16[32,256,128]{2,1,0:T(8,128)(2,1)} async-done(((bf16[4,256,128]{2,1,0:T(8,128)(2,1)}), bf16[32,256,128]{2,1,0:T(8,128)(2,1)}) %all-gather.13.cloned.1.call-update) | async-done | bytes 2097168 | tf_op jit(solution)/shard_map/all_gather | solution.py:1033
  278.1 2.0 fusion.1.refs_0_
  280.0 3.5 copy-done.1
  283.5 2.3 copy-done.8
  285.8 7.0 %finish.2 = (f32[3,256,2816]{2,1,0:T(8,128)}, f32[3,256,2816]{2,1,0:T(8,128)}) custom-call(bf16[8,3,256,384]{3,2,1,0:T(8,128)(2,1)S(1)} %bitcast.94, f32[3,256,2816]{2,1,0:T(8,128)S(1)} %copy-done.1), custom_call_target="tpu_custom_call" | custom-call | flops 4325376 | bytes 30277632 | tf_op jit(solution)/shard_map/finish/pallas_call | solution.py:823
  294.0 11.0 %orthogonalize.2 = (bf16[256,384]{1,0:T(8,128)(2,1)}, bf16[256,384]{1,0:T(8,128)(2,1)}, bf16[256,384]{1,0:T(8,128)(2,1)}, bf16[256,384]{1,0:T(8,128)(2,1)}, bf16...) custom-call(s32[3]{0:T(128)} %add_add_fusion.1.control_ref, ...), custom_call_target="tpu_custom_call" | custom-call | flops 30000001024 | bytes 3145728 | tf_op jit(solution)/shard_map/orthogonalize/pallas_call | solution.py:756
  305.0 1.4 collective-permute-start.22
  307.1 1.5 collective-permute-start.24
  308.7 1.4 collective-permute-start.26
  311.2 3.5 collective-permute-start.27
  314.7 3.1 collective-permute-start.28
  318.4 4.0 collective-permute-start.29
  322.5 4.5 collective-permute-done.23
  326.9 1.7 convert_add_fusion.2
  329.8 29.9 %collective-permute-start.44 = (f32[8,1024]{1,0:T(8,128)S(1)}, f32[8,1024]{1,0:T(8,128)S(1)}, u32[]{:S(2)}, u32[]{:S(2)}) collective-permute-start(f32[8,1024]{1,0:T(8,128)S(1)} %pad_maximum_fusion.4), channel_id=1, source_target_pairs={{0,4},{4,0},{8,12},{12,8},{16,20},{20,16},{24,28},{28,24},{1,5},{5... | collective-permute-start | bytes 98312 | tf_op jit(solution)/shard_map/ppermute | solution.py:846
  360.6 6.0 %collective-permute-start.45 = (f32[8,1024]{1,0:T(8,128)S(1)}, f32[8,1024]{1,0:T(8,128)S(1)}, u32[]{:S(2)}, u32[]{:S(2)}) collective-permute-start(f32[8,1024]{1,0:T(8,128)S(1)} %fusion.24), channel_id=1, source_target_pairs={{0,8},{4,12},{8,0},{12,4},{16,24},{20,28},{24,16},{28,20},{1,9},{5... | collective-permute-start | bytes 98312 | tf_op jit(solution)/shard_map/ppermute | solution.py:846
  366.7 4.0 finish.3
  372.4 32.1 %orthogonalize.3 = (bf16[256,128]{1,0:T(8,128)(2,1)}, bf16[256,128]{1,0:T(8,128)(2,1)}, bf16[256,128]{1,0:T(8,128)(2,1)}, bf16[256,128]{1,0:T(8,128)(2,1)}, bf16...) custom-call(s32[3]{0:T(128)} %add_add_fusion.2.control_ref, ...), custom_call_target="tpu_custom_call" | custom-call | flops 30000001024 | bytes 1048576 | tf_op jit(solution)/shard_map/orthogonalize/pallas_call | solution.py:756
  404.6 1.4 collective-permute-start.30
  406.0 3.3 collective-permute-start.31
  409.4 1.9 collective-permute-start.32
  411.3 2.9 collective-permute-start.33
  415.5 1.6 collective-permute-done.47
  417.1 5.0 %collective-permute-start.34 = (bf16[256,128]{1,0:T(8,128)(2,1)}, bf16[256,128]{1,0:T(8,128)(2,1)S(1)}, u32[]{:S(2)}, u32[]{:S(2)}) collective-permute-start(bf16[256,128]{1,0:T(8,128)(2,1)} %get-tuple-element.219), channel_id=1, source_target_pairs={{4,24},{12,0},{20,8},{24,12},{5,25},{13,1},{21,9},{25,13},{6,26},{... | collective-permute-start | bytes 196616 | tf_op jit(solution)/shard_map/ppermute | solution.py:902
  422.1 1.9 collective-permute-start.35
  426.6 2.3 fusion.6
  432.3 1.9 update.2
  438.8 8.6 %collective-permute-done.41.refs_5_ = bf16[256,384]{1,0:T(8,128)(2,1)S(1)} collective-permute-done((bf16[256,384]{1,0:T(8,128)(2,1)S(1)}, bf16[256,384]{1,0:T(8,128)(2,1)S(1)}, u32[]{:S(2)}, u32[]{:S(2)}) %collective-permute-start.41) | collective-permute-done | bytes 196640 | tf_op jit(solution)/shard_map/ppermute | solution.py:902
  447.3 4.2 collective-permute-done.43.refs_7_
  452.4 1.3 copy.35
  (264 shorter events, 74.8 us)
Async XLA Ops:
  7.2 64.2 %all-gather.9.cloned.1.call-start = ((), (), s32[]{:S(2)}) async-start(), calls=%async_computation.1 | async-start | bytes 2359296 | tf_op jit(solution)/shard_map/all_gather | solution.py:943
  7.9 97.7 %all-gather.11.cloned.1.call-start = ((), (), s32[]{:S(2)}) async-start(), calls=%async_computation.2 | async-start | bytes 2359296 | tf_op jit(solution)/shard_map/all_gather | solution.py:975
  12.3 49.0 %collective-permute-start.4 = (bf16[256,2176]{1,0:T(8,128)(2,1)S(1)}, bf16[256,2176]{1,0:T(8,128)(2,1)S(1)}, u32[]{:S(2)}, u32[]{:S(2)}) collective-permute-start(bf16[256,2176]{1,0:T(8,128)(2,1)S(1)} %pad_maximum_fusion.refs_0_), channel_id=1, source_target_pairs={{0,1},{1,0},{2,3},{3,2},{4,5},{5,4},{6,7},{7,6},{8,9},{9,8},{10,11... | collective-permute-start | bytes 3342344 | tf_op jit(solution)/shard_map/ppermute | solution.py:846
  14.4 46.9 %collective-permute-start.5 = (bf16[256,2176]{1,0:T(8,128)(2,1)S(1)}, bf16[256,2176]{1,0:T(8,128)(2,1)S(1)}, u32[]{:S(2)}, u32[]{:S(2)}) collective-permute-start(bf16[256,2176]{1,0:T(8,128)(2,1)S(1)} %pad_maximum_fusion.refs_0_), channel_id=1, source_target_pairs={{0,2},{1,3},{2,0},{3,1},{4,6},{5,7},{6,4},{7,5},{8,10},{9,11},{10,... | collective-permute-start | bytes 3342344 | tf_op jit(solution)/shard_map/ppermute | solution.py:846
  15.7 34.9 %collective-permute-start = (bf16[128,1024]{1,0:T(8,128)(2,1)}, bf16[128,1024]{1,0:T(8,128)(2,1)}, u32[]{:S(2)}, u32[]{:S(2)}) collective-permute-start(bf16[128,1024]{1,0:T(8,128)(2,1)} %bitcast.2), channel_id=1, source_target_pairs={{0,8},{4,12},{8,0},{12,4},{16,24},{20,28},{24,16},{28,20},{1,9},{5... | collective-permute-start | bytes 786440 | tf_op jit(solution)/shard_map/ppermute | solution.py:846
  17.0 33.6 %collective-permute-start.1 = (bf16[128,1024]{1,0:T(8,128)(2,1)}, bf16[128,1024]{1,0:T(8,128)(2,1)}, u32[]{:S(2)}, u32[]{:S(2)}) collective-permute-start(bf16[128,1024]{1,0:T(8,128)(2,1)} %bitcast.2), channel_id=1, source_target_pairs={{0,16},{4,20},{8,24},{12,28},{16,0},{20,4},{24,8},{28,12},{1,17},{... | collective-permute-start | bytes 786440 | tf_op jit(solution)/shard_map/ppermute | solution.py:846
  19.1 31.5 %collective-permute-start.2 = (bf16[128,1024]{1,0:T(8,128)(2,1)}, bf16[128,1024]{1,0:T(8,128)(2,1)}, u32[]{:S(2)}, u32[]{:S(2)}) collective-permute-start(bf16[128,1024]{1,0:T(8,128)(2,1)} %bitcast.2), channel_id=1, source_target_pairs={{0,24},{4,28},{8,16},{12,20},{16,8},{20,12},{24,0},{28,4},{1,25},{... | collective-permute-start | bytes 786440 | tf_op jit(solution)/shard_map/ppermute | solution.py:846
  52.0 9.4 %collective-permute-start.3 = (bf16[4,128,1024]{2,1,0:T(8,128)(2,1)S(1)}, bf16[4,128,1024]{2,1,0:T(8,128)(2,1)S(1)}, u32[]{:S(2)}, u32[]{:S(2)}) collective-permute-start(bf16[4,128,1024]{2,1,0:T(8,128)(2,1)S(1)} %pad_maximum_fusion.1.same_ref), channel_id=1, source_target_pairs={{0,4},{4,0},{8,12},{12,8},{16,20},{20,16},{24,28},{28,24},{1,5},{5... | collective-permute-start | bytes 3145736 | tf_op jit(solution)/shard_map/ppermute | solution.py:846
  71.4 176.8 %all-gather.15.cloned.1.call-start = ((), (), s32[]{:S(2)}) async-start(), calls=%async_computation.4 | async-start | bytes 5308416 | tf_op jit(solution)/shard_map/all_gather | solution.py:1006
  72.5 14.4 %collective-permute-start.6 = (bf16[128,2176]{1,0:T(8,128)(2,1)}, bf16[128,2176]{1,0:T(8,128)(2,1)}, u32[]{:S(2)}, u32[]{:S(2)}) collective-permute-start(bf16[128,2176]{1,0:T(8,128)(2,1)} %slice.109), channel_id=1, source_target_pairs={{0,2},{1,3},{2,0},{3,1},{4,6},{5,7},{6,4},{7,5},{8,10},{9,11},{10,... | collective-permute-start | bytes 1671176 | tf_op jit(solution)/shard_map/ppermute | solution.py:846
  73.7 14.1 %collective-permute-start.7 = (bf16[128,2176]{1,0:T(8,128)(2,1)}, bf16[128,2176]{1,0:T(8,128)(2,1)}, u32[]{:S(2)}, u32[]{:S(2)}) collective-permute-start(bf16[128,2176]{1,0:T(8,128)(2,1)} %slice.110), channel_id=1, source_target_pairs={{0,1},{1,0},{2,3},{3,2},{4,5},{5,4},{6,7},{7,6},{8,9},{9,8},{10,11... | collective-permute-start | bytes 1671176 | tf_op jit(solution)/shard_map/ppermute | solution.py:846
  120.3 3.8 collective-permute-start.8
  128.1 41.0 %slice-start = ((s8[4456448]{0:T(1024)(128)(4,1)}), s8[4194304]{0:T(1024)(128)(4,1)S(1)}, s32[]{:S(2)}) async-start(s8[4456448]{0:T(1024)(128)(4,1)} %bitcast.91), calls=%async_computation.5 | async-start | bytes 8388608
  128.1 41.0 %slice-start.1 = ((s8[4456448]{0:T(1024)(128)(4,1)}), s8[262144]{0:T(1024)(128)(4,1)S(1)}, s32[]{:S(2)}) async-start(s8[4456448]{0:T(1024)(128)(4,1)} %bitcast.91), calls=%async_computation.6 | async-start | bytes 524288
  128.1 41.0 %copy-start.19 = (bf16[1,128,1024]{2,1,0:T(8,128)(2,1)S(1)}, bf16[1,128,1024]{2,1,0:T(8,128)(2,1)}, u32[]{:S(2)}) copy-start(bf16[1,128,1024]{2,1,0:T(8,128)(2,1)} %param.14) | copy-start | bytes 786436
  128.1 41.0 %copy-start.31 = (f32[1,4,256]{2,0,1:T(1,128)S(1)}, f32[1,4,256]{2,0,1:T(1,128)}, u32[]{:S(2)}) copy-start(f32[1,4,256]{2,0,1:T(1,128)} %get-tuple-element.292) | copy-start | bytes 12292
  135.5 38.4 %collective-permute-start.12 = (bf16[3,256,384]{2,1,0:T(8,128)(2,1)}, bf16[3,256,384]{2,1,0:T(8,128)(2,1)S(1)}, u32[]{:S(2)}, u32[]{:S(2)}) collective-permute-start(bf16[3,256,384]{2,1,0:T(8,128)(2,1)} %get-tuple-element.157), channel_id=1, source_target_pairs={{0,1},{1,0},{2,3},{3,2},{4,5},{5,4},{6,7},{7,6},{8,9},{9,8},{10,11... | collective-permute-start | bytes 1769480 | tf_op jit(solution)/shard_map/ppermute | solution.py:846
  136.7 37.2 %collective-permute-start.13 = (bf16[3,256,384]{2,1,0:T(8,128)(2,1)}, bf16[3,256,384]{2,1,0:T(8,128)(2,1)S(1)}, u32[]{:S(2)}, u32[]{:S(2)}) collective-permute-start(bf16[3,256,384]{2,1,0:T(8,128)(2,1)} %get-tuple-element.158), channel_id=1, source_target_pairs={{0,2},{1,3},{2,0},{3,1},{4,6},{5,7},{6,4},{7,5},{8,10},{9,11},{10,... | collective-permute-start | bytes 1769480 | tf_op jit(solution)/shard_map/ppermute | solution.py:846
  137.0 36.9 %collective-permute-start.14 = (bf16[3,256,384]{2,1,0:T(8,128)(2,1)}, bf16[3,256,384]{2,1,0:T(8,128)(2,1)S(1)}, u32[]{:S(2)}, u32[]{:S(2)}) collective-permute-start(bf16[3,256,384]{2,1,0:T(8,128)(2,1)} %get-tuple-element.159), channel_id=1, source_target_pairs={{0,3},{1,2},{2,1},{3,0},{4,7},{5,6},{6,5},{7,4},{8,11},{9,10},{10,... | collective-permute-start | bytes 1769480 | tf_op jit(solution)/shard_map/ppermute | solution.py:846
  138.2 25.7 %collective-permute-start.10 = (bf16[1,128,1024]{2,1,0:T(8,128)(2,1)}, bf16[1,128,1024]{2,1,0:T(8,128)(2,1)S(1)}, u32[]{:S(2)}, u32[]{:S(2)}) collective-permute-start(bf16[1,128,1024]{2,1,0:T(8,128)(2,1)} %copy-done.36), channel_id=1, source_target_pairs={{0,16},{4,20},{8,24},{12,28},{16,0},{20,4},{24,8},{28,12},{1,17},{... | collective-permute-start | bytes 786440 | tf_op jit(solution)/shard_map/ppermute | solution.py:846
  146.9 17.0 %collective-permute-start.11 = (bf16[1,128,1024]{2,1,0:T(8,128)(2,1)}, bf16[1,128,1024]{2,1,0:T(8,128)(2,1)S(1)}, u32[]{:S(2)}, u32[]{:S(2)}) collective-permute-start(bf16[1,128,1024]{2,1,0:T(8,128)(2,1)} %copy-done.35), channel_id=1, source_target_pairs={{0,24},{4,28},{8,16},{12,20},{16,8},{20,12},{24,0},{28,4},{1,25},{... | collective-permute-start | bytes 786440 | tf_op jit(solution)/shard_map/ppermute | solution.py:846
  163.9 5.2 %collective-permute-start.9 = (bf16[1,128,1024]{2,1,0:T(8,128)(2,1)S(1)}, bf16[1,128,1024]{2,1,0:T(8,128)(2,1)S(1)}, u32[]{:S(2)}, u32[]{:S(2)}) collective-permute-start(bf16[1,128,1024]{2,1,0:T(8,128)(2,1)S(1)} %get-tuple-element.148), channel_id=1, source_target_pairs={{0,8},{4,12},{8,0},{12,4},{16,24},{20,28},{24,16},{28,20},{1,9},{5... | collective-permute-start | bytes 786440 | tf_op jit(solution)/shard_map/ppermute | solution.py:846
  197.6 80.5 %all-gather.13.cloned.1.call-start = ((), (), s32[]{:S(2)}) async-start(), calls=%async_computation.3 | async-start | bytes 2359296 | tf_op jit(solution)/shard_map/all_gather | solution.py:1033
  216.3 7.2 %collective-permute-start.15 = (bf16[4,256,128]{2,1,0:T(8,128)(2,1)S(1)}, bf16[4,256,128]{2,1,0:T(8,128)(2,1)S(1)}, u32[]{:S(2)}, u32[]{:S(2)}) collective-permute-start(bf16[4,256,128]{2,1,0:T(8,128)(2,1)S(1)} %get-tuple-element.165), channel_id=1, source_target_pairs={{0,1},{1,0},{2,3},{3,2},{4,5},{5,4},{6,7},{7,6},{8,9},{9,8},{10,11... | collective-permute-start | bytes 786440 | tf_op jit(solution)/shard_map/ppermute | solution.py:846
  216.4 7.1 %collective-permute-start.16 = (bf16[4,256,128]{2,1,0:T(8,128)(2,1)S(1)}, bf16[4,256,128]{2,1,0:T(8,128)(2,1)S(1)}, u32[]{:S(2)}, u32[]{:S(2)}) collective-permute-start(bf16[4,256,128]{2,1,0:T(8,128)(2,1)S(1)} %get-tuple-element.166), channel_id=1, source_target_pairs={{0,2},{1,3},{2,0},{3,1},{4,6},{5,7},{6,4},{7,5},{8,10},{9,11},{10,... | collective-permute-start | bytes 786440 | tf_op jit(solution)/shard_map/ppermute | solution.py:846
  217.6 12.4 %collective-permute-start.17 = (bf16[4,256,128]{2,1,0:T(8,128)(2,1)S(1)}, bf16[4,256,128]{2,1,0:T(8,128)(2,1)S(1)}, u32[]{:S(2)}, u32[]{:S(2)}) collective-permute-start(bf16[4,256,128]{2,1,0:T(8,128)(2,1)S(1)} %get-tuple-element.167), channel_id=1, source_target_pairs={{0,3},{1,2},{2,1},{3,0},{4,7},{5,6},{6,5},{7,4},{8,11},{9,10},{10,... | collective-permute-start | bytes 786440 | tf_op jit(solution)/shard_map/ppermute | solution.py:846
  240.5 18.0 %collective-permute-start.21 = (bf16[4,2,128,1024]{3,2,1,0:T(8,128)(2,1)}, bf16[4,2,128,1024]{3,2,1,0:T(8,128)(2,1)}, u32[]{:S(2)}, u32[]{:S(2)}) collective-permute-start(bf16[4,2,128,1024]{3,2,1,0:T(8,128)(2,1)} %get-tuple-element.175), channel_id=1, source_target_pairs={{0,4},{4,0},{8,12},{12,8},{16,20},{20,16},{24,28},{28,24},{1,5},{5... | collective-permute-start | bytes 6291464 | tf_op jit(solution)/shard_map/ppermute | solution.py:846
  251.1 41.8 %collective-permute-start.18 = (bf16[8,256,384]{2,1,0:T(8,128)(2,1)}, bf16[8,256,384]{2,1,0:T(8,128)(2,1)S(1)}, u32[]{:S(2)}, u32[]{:S(2)}) collective-permute-start(bf16[8,256,384]{2,1,0:T(8,128)(2,1)} %fusion.refs_0_), channel_id=1, source_target_pairs={{0,1},{1,0},{2,3},{3,2},{8,9},{9,8},{10,11},{11,10},{16,17},{17,16... | collective-permute-start | bytes 4718600 | tf_op jit(solution)/shard_map/ppermute | solution.py:896
  251.9 41.0 %collective-permute-start.19 = (bf16[8,256,384]{2,1,0:T(8,128)(2,1)}, bf16[8,256,384]{2,1,0:T(8,128)(2,1)}, u32[]{:S(2)}, u32[]{:S(2)}) collective-permute-start(bf16[8,256,384]{2,1,0:T(8,128)(2,1)} %fusion.refs_0_), channel_id=1, source_target_pairs={{0,2},{1,3},{2,0},{3,1},{8,10},{9,11},{10,8},{11,9},{16,18},{17,19... | collective-permute-start | bytes 4718600 | tf_op jit(solution)/shard_map/ppermute | solution.py:896
  253.7 39.2 %collective-permute-start.20 = (bf16[8,256,384]{2,1,0:T(8,128)(2,1)}, bf16[8,256,384]{2,1,0:T(8,128)(2,1)}, u32[]{:S(2)}, u32[]{:S(2)}) collective-permute-start(bf16[8,256,384]{2,1,0:T(8,128)(2,1)} %fusion.refs_0_), channel_id=1, source_target_pairs={{0,3},{1,2},{2,1},{3,0},{8,11},{9,10},{10,9},{11,8},{16,19},{17,18... | collective-permute-start | bytes 4718600 | tf_op jit(solution)/shard_map/ppermute | solution.py:896
  257.2 51.5 %collective-permute-start.25 = (f32[8,128]{1,0:T(8,128)S(1)}, f32[8,128]{1,0:T(8,128)S(1)}, u32[]{:S(2)}, u32[]{:S(2)}) collective-permute-start(f32[8,128]{1,0:T(8,128)S(1)} %sums_of_squares.1), channel_id=1, source_target_pairs={{0,1},{1,0},{2,3},{3,2},{4,5},{5,4},{6,7},{7,6},{8,9},{9,8},{10,11... | collective-permute-start | bytes 12296 | tf_op jit(solution)/shard_map/ppermute | solution.py:846
  294.0 32.9 %copy-start.18 = (f32[2,128,1024]{2,1,0:T(8,128)S(1)}, f32[2,128,1024]{2,1,0:T(8,128)}, u32[]{:S(2)}) copy-start(f32[2,128,1024]{2,1,0:T(8,128)} %copy-done.17) | copy-start | bytes 3145732
  294.0 72.7 %copy-start.12 = (bf16[32,256,128]{2,1,0:T(8,128)(2,1)S(1)}, bf16[32,256,128]{2,1,0:T(8,128)(2,1)}, u32[]{:S(2)}) copy-start(bf16[32,256,128]{2,1,0:T(8,128)(2,1)} %all-gather.13.cloned.1.call-done) | copy-start | bytes 6291460
  305.0 13.4 %collective-permute-start.22 = (bf16[2,128,1024]{2,1,0:T(8,128)(2,1)}, bf16[2,128,1024]{2,1,0:T(8,128)(2,1)}, u32[]{:S(2)}, u32[]{:S(2)}) collective-permute-start(bf16[2,128,1024]{2,1,0:T(8,128)(2,1)} %get-tuple-element.189), channel_id=1, source_target_pairs={{0,8},{4,12},{8,0},{12,4},{16,24},{20,28},{24,16},{28,20},{1,9},{5... | collective-permute-start | bytes 1572872 | tf_op jit(solution)/shard_map/ppermute | solution.py:846
  306.4 20.5 %collective-permute-start.23 = (bf16[2,128,1024]{2,1,0:T(8,128)(2,1)}, bf16[2,128,1024]{2,1,0:T(8,128)(2,1)}, u32[]{:S(2)}, u32[]{:S(2)}) collective-permute-start(bf16[2,128,1024]{2,1,0:T(8,128)(2,1)} %get-tuple-element.190), channel_id=1, source_target_pairs={{0,16},{4,20},{8,24},{12,28},{16,0},{20,4},{24,8},{28,12},{1,17},{... | collective-permute-start | bytes 1572872 | tf_op jit(solution)/shard_map/ppermute | solution.py:846
  307.1 19.8 %collective-permute-start.24 = (bf16[2,128,1024]{2,1,0:T(8,128)(2,1)}, bf16[2,128,1024]{2,1,0:T(8,128)(2,1)}, u32[]{:S(2)}, u32[]{:S(2)}) collective-permute-start(bf16[2,128,1024]{2,1,0:T(8,128)(2,1)} %get-tuple-element.191), channel_id=1, source_target_pairs={{0,24},{4,28},{8,16},{12,20},{16,8},{20,12},{24,0},{28,4},{1,25},{... | collective-permute-start | bytes 1572872 | tf_op jit(solution)/shard_map/ppermute | solution.py:846
  308.7 2.5 collective-permute-start.26
  311.2 55.4 %copy-start.4 = (f32[4,256,1024]{2,1,0:T(8,128)S(1)}, f32[4,256,1024]{2,1,0:T(8,128)}, u32[]{:S(2)}) copy-start(f32[4,256,1024]{2,1,0:T(8,128)} %momentum_ref.7) | copy-start | bytes 12582916
  311.2 60.0 %collective-permute-start.27 = (bf16[8,256,128]{2,1,0:T(8,128)(2,1)}, bf16[8,256,128]{2,1,0:T(8,128)(2,1)S(1)}, u32[]{:S(2)}, u32[]{:S(2)}) collective-permute-start(bf16[8,256,128]{2,1,0:T(8,128)(2,1)} %fusion.1.refs_0_), channel_id=1, source_target_pairs={{4,5},{5,4},{6,7},{7,6},{12,13},{13,12},{14,15},{15,14},{20,21},{2... | collective-permute-start | bytes 1572872 | tf_op jit(solution)/shard_map/ppermute | solution.py:896
  314.7 56.5 %collective-permute-start.28 = (bf16[8,256,128]{2,1,0:T(8,128)(2,1)}, bf16[8,256,128]{2,1,0:T(8,128)(2,1)S(1)}, u32[]{:S(2)}, u32[]{:S(2)}) collective-permute-start(bf16[8,256,128]{2,1,0:T(8,128)(2,1)} %fusion.1.refs_0_), channel_id=1, source_target_pairs={{4,6},{5,7},{6,4},{7,5},{12,14},{13,15},{14,12},{15,13},{20,22},{2... | collective-permute-start | bytes 1572872 | tf_op jit(solution)/shard_map/ppermute | solution.py:896
  318.4 52.9 %collective-permute-start.29 = (bf16[8,256,128]{2,1,0:T(8,128)(2,1)}, bf16[8,256,128]{2,1,0:T(8,128)(2,1)S(1)}, u32[]{:S(2)}, u32[]{:S(2)}) collective-permute-start(bf16[8,256,128]{2,1,0:T(8,128)(2,1)} %fusion.1.refs_0_), channel_id=1, source_target_pairs={{4,7},{5,6},{6,5},{7,4},{12,15},{13,14},{14,13},{15,12},{20,23},{2... | collective-permute-start | bytes 1572872 | tf_op jit(solution)/shard_map/ppermute | solution.py:896
  329.8 30.8 %collective-permute-start.44 = (f32[8,1024]{1,0:T(8,128)S(1)}, f32[8,1024]{1,0:T(8,128)S(1)}, u32[]{:S(2)}, u32[]{:S(2)}) collective-permute-start(f32[8,1024]{1,0:T(8,128)S(1)} %pad_maximum_fusion.4), channel_id=1, source_target_pairs={{0,4},{4,0},{8,12},{12,8},{16,20},{20,16},{24,28},{28,24},{1,5},{5... | collective-permute-start | bytes 98312 | tf_op jit(solution)/shard_map/ppermute | solution.py:846
  360.6 10.1 %collective-permute-start.45 = (f32[8,1024]{1,0:T(8,128)S(1)}, f32[8,1024]{1,0:T(8,128)S(1)}, u32[]{:S(2)}, u32[]{:S(2)}) collective-permute-start(f32[8,1024]{1,0:T(8,128)S(1)} %fusion.24), channel_id=1, source_target_pairs={{0,8},{4,12},{8,0},{12,4},{16,24},{20,28},{24,16},{28,20},{1,9},{5... | collective-permute-start | bytes 98312 | tf_op jit(solution)/shard_map/ppermute | solution.py:846
  370.7 43.5 %collective-permute-start.46 = (f32[8,1024]{1,0:T(8,128)S(1)}, f32[8,1024]{1,0:T(8,128)S(1)}, u32[]{:S(2)}, u32[]{:S(2)}) collective-permute-start(f32[8,1024]{1,0:T(8,128)S(1)} %add.160), channel_id=1, source_target_pairs={{0,16},{4,20},{8,24},{12,28},{16,0},{20,4},{24,8},{28,12},{1,17},{... | collective-permute-start | bytes 98312 | tf_op jit(solution)/shard_map/ppermute | solution.py:846
  372.4 54.1 %copy-start.16 = (f32[128,1024]{1,0:T(8,128)S(1)}, f32[128,1024]{1,0:T(8,128)}, u32[]{:S(2)}) copy-start(f32[128,1024]{1,0:T(8,128)} %get-tuple-element.134.resid_ref) | copy-start | bytes 1572868
  372.4 54.1 %copy-start.22 = (f32[128,1024]{1,0:T(8,128)S(1)}, f32[128,1024]{1,0:T(8,128)}, u32[]{:S(2)}) copy-start(f32[128,1024]{1,0:T(8,128)} %copy-done.21) | copy-start | bytes 1572868
  404.6 27.7 %copy-start.14 = (f32[4,256,128]{2,1,0:T(8,128)S(1)}, f32[4,256,128]{2,1,0:T(8,128)}, u32[]{:S(2)}) copy-start(f32[4,256,128]{2,1,0:T(8,128)} %get-tuple-element.283.own_ref) | copy-start | bytes 1572868
  404.6 27.7 %copy-start.30 = (bf16[256,128]{1,0:T(8,128)(2,1)S(1)}, bf16[256,128]{1,0:T(8,128)(2,1)}, u32[]{:S(2)}) copy-start(bf16[256,128]{1,0:T(8,128)(2,1)} %get-tuple-element.214.refs_0_) | copy-start | bytes 196612
  404.6 17.5 %collective-permute-start.30 = (bf16[256,128]{1,0:T(8,128)(2,1)}, bf16[256,128]{1,0:T(8,128)(2,1)S(1)}, u32[]{:S(2)}, u32[]{:S(2)}) collective-permute-start(bf16[256,128]{1,0:T(8,128)(2,1)} %get-tuple-element.215), channel_id=1, source_target_pairs={{4,8},{12,16},{20,24},{24,28},{5,9},{13,17},{21,25},{25,29},{6,10}... | collective-permute-start | bytes 196616 | tf_op jit(solution)/shard_map/ppermute | solution.py:902
  406.0 18.0 %collective-permute-start.31 = (bf16[256,128]{1,0:T(8,128)(2,1)}, bf16[256,128]{1,0:T(8,128)(2,1)S(1)}, u32[]{:S(2)}, u32[]{:S(2)}) collective-permute-start(bf16[256,128]{1,0:T(8,128)(2,1)} %get-tuple-element.216), channel_id=1, source_target_pairs={{4,12},{12,20},{20,28},{24,0},{5,13},{13,21},{21,29},{25,1},{6,14}... | collective-permute-start | bytes 196616 | tf_op jit(solution)/shard_map/ppermute | solution.py:902
  409.4 15.9 %collective-permute-start.32 = (bf16[256,128]{1,0:T(8,128)(2,1)}, bf16[256,128]{1,0:T(8,128)(2,1)S(1)}, u32[]{:S(2)}, u32[]{:S(2)}) collective-permute-start(bf16[256,128]{1,0:T(8,128)(2,1)} %get-tuple-element.217), channel_id=1, source_target_pairs={{4,16},{12,24},{20,0},{24,4},{5,17},{13,25},{21,1},{25,5},{6,18},{... | collective-permute-start | bytes 196616 | tf_op jit(solution)/shard_map/ppermute | solution.py:902
  411.3 17.6 %collective-permute-start.33 = (bf16[256,128]{1,0:T(8,128)(2,1)}, bf16[256,128]{1,0:T(8,128)(2,1)S(1)}, u32[]{:S(2)}, u32[]{:S(2)}) collective-permute-start(bf16[256,128]{1,0:T(8,128)(2,1)} %get-tuple-element.218), channel_id=1, source_target_pairs={{4,20},{12,28},{20,4},{24,8},{5,21},{13,29},{21,5},{25,9},{6,22},{... | collective-permute-start | bytes 196616 | tf_op jit(solution)/shard_map/ppermute | solution.py:902
  414.2 2.8 collective-permute-start.47
  417.1 13.2 %collective-permute-start.34 = (bf16[256,128]{1,0:T(8,128)(2,1)}, bf16[256,128]{1,0:T(8,128)(2,1)S(1)}, u32[]{:S(2)}, u32[]{:S(2)}) collective-permute-start(bf16[256,128]{1,0:T(8,128)(2,1)} %get-tuple-element.219), channel_id=1, source_target_pairs={{4,24},{12,0},{20,8},{24,12},{5,25},{13,1},{21,9},{25,13},{6,26},{... | collective-permute-start | bytes 196616 | tf_op jit(solution)/shard_map/ppermute | solution.py:902
  422.1 8.8 %collective-permute-start.35 = (bf16[256,128]{1,0:T(8,128)(2,1)}, bf16[256,128]{1,0:T(8,128)(2,1)S(1)}, u32[]{:S(2)}, u32[]{:S(2)}) collective-permute-start(bf16[256,128]{1,0:T(8,128)(2,1)} %get-tuple-element.220), channel_id=1, source_target_pairs={{4,28},{12,4},{20,12},{24,16},{5,29},{13,5},{21,13},{25,17},{6,30}... | collective-permute-start | bytes 196616 | tf_op jit(solution)/shard_map/ppermute | solution.py:902
  424.0 7.6 %collective-permute-start.36 = (bf16[256,128]{1,0:T(8,128)(2,1)}, bf16[256,128]{1,0:T(8,128)(2,1)S(1)}, u32[]{:S(2)}, u32[]{:S(2)}) collective-permute-start(bf16[256,128]{1,0:T(8,128)(2,1)} %get-tuple-element.221), channel_id=1, source_target_pairs={{4,0},{12,8},{20,16},{24,20},{5,1},{13,9},{21,17},{25,21},{6,2},{1... | collective-permute-start | bytes 196616 | tf_op jit(solution)/shard_map/ppermute | solution.py:902
  425.3 8.8 %collective-permute-start.48 = (f32[8,1024]{1,0:T(8,128)S(1)}, f32[8,1024]{1,0:T(8,128)S(1)}, u32[]{:S(2)}, u32[]{:S(2)}) collective-permute-start(f32[8,1024]{1,0:T(8,128)S(1)} %add.162), channel_id=1, source_target_pairs={{0,2},{1,3},{2,0},{3,1},{4,6},{5,7},{6,4},{7,5},{8,10},{9,11},{10,... | collective-permute-start | bytes 98312 | tf_op jit(solution)/shard_map/ppermute | solution.py:846
  428.9 7.2 %collective-permute-start.37 = (bf16[256,384]{1,0:T(8,128)(2,1)S(1)}, bf16[256,384]{1,0:T(8,128)(2,1)S(1)}, u32[]{:S(2)}, u32[]{:S(2)}) collective-permute-start(bf16[256,384]{1,0:T(8,128)(2,1)S(1)} %copy-done.66), channel_id=1, source_target_pairs={{0,4},{8,12},{16,20},{1,5},{9,13},{17,21},{2,6},{10,14},{18,22},{3... | collective-permute-start | bytes 589832 | tf_op jit(solution)/shard_map/ppermute | solution.py:902
  430.2 6.6 %collective-permute-start.38 = (bf16[256,384]{1,0:T(8,128)(2,1)S(1)}, bf16[256,384]{1,0:T(8,128)(2,1)S(1)}, u32[]{:S(2)}, u32[]{:S(2)}) collective-permute-start(bf16[256,384]{1,0:T(8,128)(2,1)S(1)} %copy-done.65), channel_id=1, source_target_pairs={{0,8},{8,16},{16,24},{1,9},{9,17},{17,25},{2,10},{10,18},{18,26},{... | collective-permute-start | bytes 589832 | tf_op jit(solution)/shard_map/ppermute | solution.py:902
  430.9 7.8 %collective-permute-start.39 = (bf16[256,384]{1,0:T(8,128)(2,1)S(1)}, bf16[256,384]{1,0:T(8,128)(2,1)S(1)}, u32[]{:S(2)}, u32[]{:S(2)}) collective-permute-start(bf16[256,384]{1,0:T(8,128)(2,1)S(1)} %copy-done.64), channel_id=1, source_target_pairs={{0,12},{8,20},{16,28},{1,13},{9,21},{17,29},{2,14},{10,22},{18,30}... | collective-permute-start | bytes 589832 | tf_op jit(solution)/shard_map/ppermute | solution.py:902
  431.6 7.1 %collective-permute-start.40 = (bf16[256,384]{1,0:T(8,128)(2,1)S(1)}, bf16[256,384]{1,0:T(8,128)(2,1)S(1)}, u32[]{:S(2)}, u32[]{:S(2)}) collective-permute-start(bf16[256,384]{1,0:T(8,128)(2,1)S(1)} %copy-done.63), channel_id=1, source_target_pairs={{0,16},{8,24},{16,0},{1,17},{9,25},{17,1},{2,18},{10,26},{18,2},{3... | collective-permute-start | bytes 589832 | tf_op jit(solution)/shard_map/ppermute | solution.py:902
  434.2 13.2 %collective-permute-start.41 = (bf16[256,384]{1,0:T(8,128)(2,1)S(1)}, bf16[256,384]{1,0:T(8,128)(2,1)S(1)}, u32[]{:S(2)}, u32[]{:S(2)}) collective-permute-start(bf16[256,384]{1,0:T(8,128)(2,1)S(1)} %copy-done.62), channel_id=1, source_target_pairs={{0,20},{8,28},{16,4},{1,21},{9,29},{17,5},{2,22},{10,30},{18,6},{3... | collective-permute-start | bytes 589832 | tf_op jit(solution)/shard_map/ppermute | solution.py:902
  436.1 11.2 %collective-permute-start.42 = (bf16[256,384]{1,0:T(8,128)(2,1)S(1)}, bf16[256,384]{1,0:T(8,128)(2,1)S(1)}, u32[]{:S(2)}, u32[]{:S(2)}) collective-permute-start(bf16[256,384]{1,0:T(8,128)(2,1)S(1)} %copy-done.61), channel_id=1, source_target_pairs={{0,24},{8,0},{16,8},{1,25},{9,1},{17,9},{2,26},{10,2},{18,10},{3,2... | collective-permute-start | bytes 589832 | tf_op jit(solution)/shard_map/ppermute | solution.py:902
  436.8 14.7 %collective-permute-start.43 = (bf16[256,384]{1,0:T(8,128)(2,1)S(1)}, bf16[256,384]{1,0:T(8,128)(2,1)S(1)}, u32[]{:S(2)}, u32[]{:S(2)}) collective-permute-start(bf16[256,384]{1,0:T(8,128)(2,1)S(1)} %copy-done.60), channel_id=1, source_target_pairs={{0,28},{8,4},{16,12},{1,29},{9,5},{17,13},{2,30},{10,6},{18,14},{3... | collective-permute-start | bytes 589832 | tf_op jit(solution)/shard_map/ppermute | solution.py:902
  (58 other events, 437.2 us)
Sparse Core Ops, SparseCore 0:
  9.6 50.9 all-gather.8
  71.5 33.9 all-gather.10
  197.7 50.4 all-gather.14
  250.2 27.7 all-gather.12
